TPU v7x, 128 devices: a whole 4x4x4 slice. The times are simulated.
128 devices in a mesh: seq: 32 (over z, x, core), ch: 4 (over y).
Axes of the slice: x: 4, y: 4, z: 4, core: 2. Of those that a mesh axis runs over, the one named last changes fastest.
Arguments:
- tokens: bfloat16 [16384, 2048], P('seq', 'ch'), may hold values from -6 to 6
- w_in: bfloat16 [2048, 3, 2048], P(None, None, 'ch'), may hold values from -0.125 to 0.125
- short_filter: float32 [3, 3, 2048], P(None, None, 'ch'), may hold values from -3 to 3
- decay: float32 [16, 2048], P(None, 'ch'), may hold values from 6.1035156e-05 to 0.05
- residue: float32 [16, 2048], P(None, 'ch'), may hold values from -1.5 to 1.5
- skip: float32 [2048], P('ch'), may hold values from 0.5 to 1.5
- w_out: bfloat16 [2048, 2048], P(None, 'ch'), may hold values from -0.125 to 0.125
Outputs:
- mixed: bfloat16 [16384, 2048], P('seq', 'ch')
All inputs are finite; a program needn't handle non-finite values.
Results may differ from a plain program's by a relative error of at most 0.009.
Values may be sent and summed in bfloat16 or wider, within the bound.
No kernel may reach another device: no remote copies, remote signals or barrier semaphores. Data moves between devices by JAX's collectives and lax.ppermute only.
A program may use at most 192 MiB of HBM per device.

v0:
```python
from functools import partial

import jax
import jax.numpy as jnp
from jax import lax
from jax.experimental import pallas as pl
from jax.experimental.pallas import tpu as pltpu
from jax.sharding import PartitionSpec as P

LANES = 128
SUB = 8
F32 = jnp.float32
BF16 = jnp.bfloat16
MIB = 1 << 20


def vmem():
    return pl.BlockSpec(memory_space=pltpu.VMEM)


def smem():
    return pl.BlockSpec(memory_space=pltpu.SMEM)


def near(x):
    return pltpu.with_memory_space_constraint(x, pltpu.VMEM)


def params(mib=24):
    return pltpu.CompilerParams(vmem_limit_bytes=mib * MIB)


def cost(flops, nbytes, exps=0):
    return pl.CostEstimate(flops=flops, bytes_accessed=nbytes, transcendentals=exps)


def turn(block, distance):
    count = lax.axis_size("ch")
    return lax.ppermute(block, "ch", [(i, (i + distance) % count) for i in range(count)])


def ring(low, high):
    low_left, low_right = turn(low, 1), turn(low, -1)
    high_left, high_right = turn(high, 1), turn(high, -1)
    low_far = turn(low_left, 1)
    high_far = turn(high_right, -1)
    return (low, low_left, low_right, low_far), (high, high_left, high_right, high_far)


def project_kernel(me_ref, own, left, right, far, w_ref, out_ref):
    me = me_ref[0]
    depth = own.shape[1]
    for stream in range(w_ref.shape[0]):
        total = jnp.zeros((own.shape[0], w_ref.shape[2]), F32)
        for block, step in ((own, 0), (left, 3), (right, 1), (far, 2)):
            start = pl.multiple_of(lax.rem(me + step, 4) * depth, depth)
            total += jnp.dot(
                block[...], w_ref[stream, pl.ds(start, depth), :], preferred_element_type=F32
            )
        out_ref[stream] = total.astype(BF16)


def project(me, blocks, weights):
    rows = blocks[0].shape[0]
    streams, depth, cols = weights.shape
    return pl.pallas_call(
        project_kernel,
        out_shape=pltpu.VMEM((streams, rows, cols), BF16),
        in_specs=[smem()] + [vmem()] * 5,
        out_specs=vmem(),
        compiler_params=params(),
        cost_estimate=cost(2 * rows * depth * streams * cols, 4 * MIB),
        name="project",
    )(me, *[near(b) for b in blocks], near(weights))


def widen(ext, low, high, halo, stream, slot):
    half = low.shape[1]
    ext[slot, 0:SUB, :] = halo[stream, 8:16, :].astype(F32)

    @pl.loop(0, half // 16)
    def _(i):
        at = pl.multiple_of(i * 16, 16)
        ext[slot, pl.ds(at + SUB, 16), :] = low[stream, pl.ds(at, 16), :].astype(F32)
        ext[slot, pl.ds(at + SUB + half, 16), :] = high[stream, pl.ds(at, 16), :].astype(F32)


def filtered(ext, slot, taps, stream, at, size, lanes):
    total = taps[stream, 0:1, lanes] * ext[slot, pl.ds(at + SUB, size), lanes]
    for lag in range(1, 3):
        total += taps[stream, lag : lag + 1, lanes] * ext[slot, pl.ds(at + SUB - lag, size), lanes]
    return total


def state_kernel(low, high, halo, taps, decay, sig_ref, sub_ref, end_ref, ext):
    tiles, rows, _ = sig_ref.shape
    modes = decay.shape[0]
    steps = rows // SUB
    widen(ext, low, high, halo, 1, 0)
    widen(ext, low, high, halo, 2, 1)
    for tile in range(tiles):
        lanes = slice(tile * LANES, (tile + 1) * LANES)

        for at in range(0, rows, 64):
            sig_ref[tile, pl.ds(at, 64), :] = filtered(
                ext, 0, taps, 1, at, 64, lanes
            ) * filtered(ext, 1, taps, 2, at, 64, lanes)

        rates = [jnp.broadcast_to(decay[m : m + 1, lanes], (SUB, LANES)) for m in range(modes)]
        fade = [jnp.exp(-r) for r in rates]

        def step(i, held):
            now = sig_ref[tile, pl.ds(i, SUB, stride=steps), :]
            return tuple(f * h + now for f, h in zip(fade, held))

        zero = tuple(jnp.zeros((SUB, LANES), F32) for _ in range(modes))
        held = lax.fori_loop(0, steps, step, zero, unroll=8)
        later = (SUB - 1 - lax.broadcasted_iota(jnp.int32, (SUB, LANES), 0)).astype(F32) * steps
        for m in range(modes):
            sub_ref[m, :, lanes] = held[m]
            end_ref[m : m + 1, lanes] = jnp.sum(
                held[m] * jnp.exp(-rates[m] * later), axis=0, keepdims=True
            )


def local_kernel(low, high, halo, taps, decay, residue, skip, sig, sub, query_ref, part_ref, ext):
    tiles, rows, _ = sig.shape
    modes = decay.shape[0]
    steps = rows // SUB
    widen(ext, low, high, halo, 0, 0)
    place = lax.broadcasted_iota(jnp.int32, (SUB, LANES), 0)
    for tile in range(tiles):
        lanes = slice(tile * LANES, (tile + 1) * LANES)

        for at in range(0, rows, 64):
            query_ref[tile, pl.ds(at, 64), :] = filtered(ext, 0, taps, 0, at, 64, lanes)

        rates = [jnp.broadcast_to(decay[m : m + 1, lanes], (SUB, LANES)) for m in range(modes)]
        fade = [jnp.exp(-r) for r in rates]
        gain = [residue[m : m + 1, lanes] * jnp.sqrt(r) for m, r in enumerate(rates)]
        direct = jnp.broadcast_to(skip[0:1, lanes], (SUB, LANES))
        start = []
        for m in range(modes):
            run = jnp.where(place >= 1, pltpu.roll(sub[m, :, lanes], 1, 0), 0.0)
            for shift in (1, 2, 4):
                before = jnp.where(place >= shift, pltpu.roll(run, shift, 0), 0.0)
                run = run + jnp.exp(-rates[m] * float(steps * shift)) * before
            start.append(run)

        def step(i, held):
            now = sig[tile, pl.ds(i, SUB, stride=steps), :]
            held = tuple(f * h + now for f, h in zip(fade, held))
            terms = [g * h for g, h in zip(gain, held)] + [direct * now]
            while len(terms) > 1:
                terms = [sum(terms[j : j + 2]) for j in range(0, len(terms), 2)]
            part_ref[tile, pl.ds(i, SUB, stride=steps), :] = terms[0]
            return held

        lax.fori_loop(0, steps, step, tuple(start), unroll=4)


def gate_kernel(query, part, state, decay, residue, low_ref, high_ref):
    tiles, rows, _ = query.shape
    modes = decay.shape[0]
    half = rows // 2
    ahead = 1.0 + lax.broadcasted_iota(jnp.int32, (SUB, LANES), 0).astype(F32)
    for tile in range(tiles):
        lanes = slice(tile * LANES, (tile + 1) * LANES)
        rates = [jnp.broadcast_to(decay[m : m + 1, lanes], (SUB, LANES)) for m in range(modes)]
        fade = [jnp.exp(-float(SUB) * r) for r in rates]
        first = tuple(
            residue[m : m + 1, lanes] * state[m : m + 1, lanes] * jnp.sqrt(r) * jnp.exp(-r * ahead)
            for m, r in enumerate(rates)
        )

        def piece(at, held):
            terms = list(held)
            while len(terms) > 1:
                terms = [sum(terms[j : j + 2]) for j in range(0, len(terms), 2)]
            value = query[tile, pl.ds(at, SUB), :] * (part[tile, pl.ds(at, SUB), :] + terms[0])
            return value, tuple(f * h for f, h in zip(fade, held))

        def step(out_ref, base, i, held):
            at = pl.multiple_of(i * 16, 16)
            one, held = piece(at + base, held)
            two, held = piece(at + base + SUB, held)
            out_ref[pl.ds(at, 16), lanes] = jnp.concatenate([one, two], 0).astype(BF16)
            return held

        held = lax.fori_loop(0, half // 16, partial(step, low_ref, 0), first, unroll=2)
        lax.fori_loop(0, half // 16, partial(step, high_ref, half), held, unroll=2)


def mix_kernel(me_ref, own, left, right, far, w_ref, *rest):
    out_ref = rest[-1]
    me = me_ref[0]
    depth = own.shape[1]
    total = jnp.zeros(out_ref.shape, F32)
    for block, step in ((own, 0), (left, 3), (right, 1), (far, 2)):
        start = pl.multiple_of(lax.rem(me + step, 4) * depth, depth)
        total += jnp.dot(block[...], w_ref[pl.ds(start, depth), :], preferred_element_type=F32)
    out_ref[...] = total.astype(BF16)


def mix(me, blocks, weights, half, earlier):
    rows = blocks[0].shape[0]
    depth, cols = weights.shape
    aliases = {} if earlier is None else {6: 0}
    extra = () if earlier is None else (earlier,)
    return pl.pallas_call(
        mix_kernel,
        out_shape=jax.ShapeDtypeStruct((2 * rows, cols), BF16),
        grid=(1,),
        in_specs=[smem()] + [vmem()] * 5 + [pl.BlockSpec(memory_space=pl.ANY)] * len(extra),
        out_specs=pl.BlockSpec((rows, cols), lambda i: (half, 0)),
        input_output_aliases=aliases,
        compiler_params=params(),
        cost_estimate=cost(2 * rows * depth * cols, 2 * MIB),
        name="mix",
    )(me, *[near(b) for b in blocks], near(weights), *extra)


def carry_in(end, decay, rows):
    place = lax.axis_index("seq")
    devices = lax.axis_size("seq")
    state = jnp.zeros_like(end)
    span = 1
    while span < devices:
        other = lax.ppermute(end, "seq", [(i, i ^ span) for i in range(devices)])
        upper = (place // span) % 2 == 1
        gone = (rows * (place % span)).astype(F32)
        state = state + jnp.where(upper, jnp.exp(-decay * gone) * other, 0.0)
        through = jnp.exp(-decay * float(rows * span))
        end = through * jnp.where(upper, other, end) + jnp.where(upper, end, other)
        span *= 2
    return state


def shards(tokens, w_in, short_filter, decay, residue, skip, w_out):
    rows = tokens.shape[0]
    channels = skip.shape[0]
    modes = decay.shape[0]
    half = rows // 2
    me = lax.axis_index("ch").astype(jnp.int32).reshape(1)
    weights = jnp.transpose(w_in, (1, 0, 2))
    low_tok, high_tok = ring(tokens[:half], tokens[half:])
    high = project(me, high_tok, weights)
    low = project(me, low_tok, weights)
    count = lax.axis_size("seq")
    halo = lax.ppermute(high[:, half - 16 :], "seq", [(i, i + 1) for i in range(count - 1)])
    tiled = (channels // LANES, rows, LANES)
    sig, sub, end = pl.pallas_call(
        state_kernel,
        out_shape=(
            pltpu.VMEM(tiled, F32),
            pltpu.VMEM((modes, SUB, channels), F32),
            pltpu.VMEM((modes, channels), F32),
        ),
        in_specs=[vmem()] * 5,
        out_specs=(vmem(),) * 3,
        scratch_shapes=[pltpu.VMEM((2, rows + SUB, channels), F32)],
        compiler_params=params(),
        cost_estimate=cost(2 * rows * channels * modes, 4 * MIB),
        name="state",
    )(near(low), near(high), near(halo), near(short_filter), near(decay))
    query, part = pl.pallas_call(
        local_kernel,
        out_shape=(pltpu.VMEM(tiled, F32), pltpu.VMEM(tiled, F32)),
        in_specs=[vmem()] * 9,
        out_specs=(vmem(),) * 2,
        scratch_shapes=[pltpu.VMEM((1, rows + SUB, channels), F32)],
        compiler_params=params(),
        cost_estimate=cost(4 * rows * channels * modes, 6 * MIB),
        name="local",
    )(
        near(low),
        near(high),
        near(halo),
        near(short_filter),
        near(decay),
        near(residue),
        near(skip.reshape(1, channels)),
        near(sig),
        near(sub),
    )
    state = carry_in(end, decay, rows)
    gated = pl.pallas_call(
        gate_kernel,
        out_shape=(pltpu.VMEM((half, channels), BF16), pltpu.VMEM((half, channels), BF16)),
        in_specs=[vmem()] * 5,
        out_specs=(vmem(),) * 2,
        compiler_params=params(),
        cost_estimate=cost(2 * rows * channels * modes, 3 * MIB),
        name="gate",
    )(near(query), near(part), near(state), near(decay), near(residue))
    low_gate, high_gate = ring(*gated)
    out = mix(me, low_gate, w_out, 0, None)
    return mix(me, high_gate, w_out, 1, out)


def solution(mesh):
    in_specs = (
        P("seq", "ch"),
        P(None, None, "ch"),
        P(None, None, "ch"),
        P(None, "ch"),
        P(None, "ch"),
        P("ch"),
        P(None, "ch"),
    )
    return jax.shard_map(
        shards, mesh=mesh, in_specs=in_specs, out_specs=P("seq", "ch"), check_vma=False
    )
```

profile of v0, /device:TPU:0, one launch (start us, length us, event | category | flops | bytes accessed | tf_op | source)
XLA Modules:
  0.0 85.7 jit_solution(9081345163223393039)
XLA Ops:
  0.0 1.1 %fusion = (bf16[256,512]{1,0:T(8,128)(2,1)S(1)}, bf16[256,512]{1,0:T(8,128)(2,1)S(1)}) fusion(bf16[512,512]{1,0:T(8,128)(2,1)} %param.7), kind=kLoop, calls=%fused_computation.5 | loop fusion | bytes 1048576 | tf_op jit(solution)/shard_map/slice | solution.py:246
  1.1 3.2 %collective-permute-start.4 = (bf16[256,512]{1,0:T(8,128)(2,1)S(1)}, bf16[256,512]{1,0:T(8,128)(2,1)S(1)}, u32[]{:S(2)}, u32[]{:S(2)}) collective-permute-start(bf16[256,512]{1,0:T(8,128)(2,1)S(1)} %get-tuple-element.19.own), channel_id=1, source_target_pairs={{0,3},{1,0},{2,1},{3,2},{4,7},{5,4},{6,5},{7,6},{8,11},{9,8},{10,9... | collective-permute-start | bytes 786440 | tf_op jit(solution)/shard_map/ppermute | solution.py:39
  4.2 0.0 collective-permute-start
  4.2 0.6 collective-permute-start.3
  4.8 5.0 %collective-permute-done.4.right = bf16[256,512]{1,0:T(8,128)(2,1)S(1)} collective-permute-done((bf16[256,512]{1,0:T(8,128)(2,1)S(1)}, bf16[256,512]{1,0:T(8,128)(2,1)S(1)}, u32[]{:S(2)}, u32[]{:S(2)}) %collective-permute-start.4) | collective-permute-done | bytes 262176 | tf_op jit(solution)/shard_map/ppermute | solution.py:39
  9.8 3.7 %collective-permute-start.5 = (bf16[256,512]{1,0:T(8,128)(2,1)S(1)}, bf16[256,512]{1,0:T(8,128)(2,1)S(1)}, u32[]{:S(2)}, u32[]{:S(2)}) collective-permute-start(bf16[256,512]{1,0:T(8,128)(2,1)S(1)} %collective-permute-done.4.right), channel_id=1, source_target_pairs={{0,3},{1,0},{2,1},{3,2},{4,7},{5,4},{6,5},{7,6},{8,11},{9,8},{10,9... | collective-permute-start | bytes 786440 | tf_op jit(solution)/shard_map/ppermute | solution.py:39
  13.5 0.0 collective-permute-start.1
  13.5 1.2 %collective-permute-done.left = bf16[256,512]{1,0:T(8,128)(2,1)S(1)} collective-permute-done((bf16[256,512]{1,0:T(8,128)(2,1)S(1)}, bf16[256,512]{1,0:T(8,128)(2,1)S(1)}, u32[]{:S(2)}, u32[]{:S(2)}) %collective-permute-start) | collective-permute-done | bytes 262176 | tf_op jit(solution)/shard_map/ppermute | solution.py:39
  14.7 0.8 collective-permute-start.2
  15.5 4.8 %collective-permute-done.3.left = bf16[256,512]{1,0:T(8,128)(2,1)S(1)} collective-permute-done((bf16[256,512]{1,0:T(8,128)(2,1)S(1)}, bf16[256,512]{1,0:T(8,128)(2,1)S(1)}, u32[]{:S(2)}, u32[]{:S(2)}) %collective-permute-start.3) | collective-permute-done | bytes 262176 | tf_op jit(solution)/shard_map/ppermute | solution.py:39
  20.3 0.0 collective-permute-done.5.far
  20.3 0.0 copy-start
  20.3 2.8 %copy-done = bf16[2048,3,512]{2,0,1:T(8,128)(2,1)S(1)} copy-done((bf16[2048,3,512]{2,0,1:T(8,128)(2,1)S(1)}, bf16[2048,3,512]{2,0,1:T(8,128)(2,1)}, u32[]{:S(2)}) %copy-start) | copy-done | bytes 6291480
  23.1 0.0 copy-start.1
  23.1 0.0 copy-start.5
  23.1 0.0 copy-start.9
  23.1 1.8 %project.3.high = bf16[3,256,512]{2,1,0:T(8,128)(2,1)S(1)} custom-call(s32[1]{0:T(128)} %bitcast.me_ref, bf16[256,512]{1,0:T(8,128)(2,1)S(1)} %get-tuple-element.19.own, bf16[256,512]{1,0:T(8,128)(2,1)S(1)} %collective-permute-done.3.left, bf16[256,512]{1,0:T(8,128)(2,1)S(1)} %collective-permute-done.4.right, ...), custom_call_target="tpu_custom_call" | custom-call | flops 1610612736 | bytes 4194304 | tf_op jit(solution)/shard_map/project/pallas_call | solution.py:66
  24.9 0.0 copy-start.8
  24.9 0.0 copy-start.10
  24.9 0.0 copy-start.2
  24.9 1.4 %collective-permute-start.6 = (bf16[3,16,512]{2,1,0:T(8,128)(2,1)S(1)}, bf16[3,16,512]{2,1,0:T(8,128)(2,1)S(1)}, u32[]{:S(2)}, u32[]{:S(2)}) collective-permute-start(bf16[3,16,512]{2,1,0:T(8,128)(2,1)S(1)} %slice.12), channel_id=1, source_target_pairs={{0,4},{4,8},{8,12},{12,16},{16,20},{20,24},{24,28},{28,32},{32,36}... | collective-permute-start | bytes 147464 | tf_op jit(solution)/shard_map/ppermute | solution.py:250
  26.4 0.0 collective-permute-done.1.right
  26.4 0.0 collective-permute-done.2.far
  26.4 0.0 copy-done.1
  26.4 2.8 %project.2.low = bf16[3,256,512]{2,1,0:T(8,128)(2,1)S(1)} custom-call(s32[1]{0:T(128)} %bitcast.me_ref, bf16[256,512]{1,0:T(8,128)(2,1)S(1)} %get-tuple-element.20.own, bf16[256,512]{1,0:T(8,128)(2,1)S(1)} %collective-permute-done.left, bf16[256,512]{1,0:T(8,128)(2,1)} %collective-permute-done.1.right, bf16[256,512]{1,0:T(8,128)(2,1)} %collective-permute-done.2.far, ...), custom_call_target="tpu_custom_call" | custom-call | flops 1610612736 | bytes 4194304 | tf_op jit(solution)/shard_map/project/pallas_call | solution.py:66
  29.2 0.0 collective-permute-done.6.halo
  29.2 0.0 copy-done.5
  29.2 0.0 copy-done.9
  29.2 2.7 %state.1 = (f32[4,512,128]{2,1,0:T(8,128)S(1)}, f32[16,8,512]{2,1,0:T(8,128)S(1)}, f32[16,512]{1,0:T(8,128)S(1)}) custom-call(bf16[3,256,512]{2,1,0:T(8,128)(2,1)S(1)} %project.2.low, bf16[3,256,512]{2,1,0:T(8,128)(2,1)S(1)} %project.3.high, bf16[3,16,512]{2,1,0:T(8,128)(2,1)S(1)} %collective-permute-done.6.halo, f32[3,3,512]{2,1,0:T(4,128)S(1)} %copy-done.9, ...), custom_call_target="tpu_custom_call" | custom-call | flops 8388608 | bytes 4194304 | tf_op jit(solution)/shard_map/state/pallas_call | solution.py:252
  32.0 0.0 copy-start.3
  32.0 0.9 %copy-done.3 = bf16[3,256,512]{2,1,0:T(8,128)(2,1)} copy-done((bf16[3,256,512]{2,1,0:T(8,128)(2,1)}, bf16[3,256,512]{2,1,0:T(8,128)(2,1)S(1)}, u32[]{:S(2)}) %copy-start.3) | copy-done | bytes 786456
  32.9 0.0 copy-start.6
  32.9 1.0 %copy-done.6 = f32[4,512,128]{2,1,0:T(8,128)} copy-done((f32[4,512,128]{2,1,0:T(8,128)}, f32[4,512,128]{2,1,0:T(8,128)S(1)}, u32[]{:S(2)}) %copy-start.6) | copy-done | bytes 1048600
  33.8 2.2 %collective-permute-start.7 = (f32[16,512]{1,0:T(8,128)S(1)}, f32[16,512]{1,0:T(8,128)S(1)}, u32[]{:S(2)}, u32[]{:S(2)}) collective-permute-start(f32[16,512]{1,0:T(8,128)S(1)} %get-tuple-element.16), channel_id=1, source_target_pairs={{0,4},{4,0},{8,12},{12,8},{16,20},{20,16},{24,28},{28,24},{32,36},... | collective-permute-start | bytes 98312 | tf_op jit(solution)/shard_map/ppermute | solution.py:229
  36.1 0.9 %collective-permute-done.7 = f32[16,512]{1,0:T(8,128)S(1)} collective-permute-done((f32[16,512]{1,0:T(8,128)S(1)}, f32[16,512]{1,0:T(8,128)S(1)}, u32[]{:S(2)}, u32[]{:S(2)}) %collective-permute-start.7) | collective-permute-done | bytes 32800 | tf_op jit(solution)/shard_map/ppermute | solution.py:229
  36.9 1.6 %collective-permute-start.8 = (f32[16,512]{1,0:T(8,128)S(1)}, f32[16,512]{1,0:T(8,128)S(1)}, u32[]{:S(2)}, u32[]{:S(2)}) collective-permute-start(f32[16,512]{1,0:T(8,128)S(1)} %select_add_fusion.4), channel_id=1, source_target_pairs={{0,8},{4,12},{8,0},{12,4},{16,24},{20,28},{24,16},{28,20},{32,40},... | collective-permute-start | bytes 98312 | tf_op jit(solution)/shard_map/ppermute | solution.py:229
  38.5 2.4 %collective-permute-done.8 = f32[16,512]{1,0:T(8,128)S(1)} collective-permute-done((f32[16,512]{1,0:T(8,128)S(1)}, f32[16,512]{1,0:T(8,128)S(1)}, u32[]{:S(2)}, u32[]{:S(2)}) %collective-permute-start.8) | collective-permute-done | bytes 32800 | tf_op jit(solution)/shard_map/ppermute | solution.py:229
  41.0 2.8 %collective-permute-start.9 = (f32[16,512]{1,0:T(8,128)S(1)}, f32[16,512]{1,0:T(8,128)S(1)}, u32[]{:S(2)}, u32[]{:S(2)}) collective-permute-start(f32[16,512]{1,0:T(8,128)S(1)} %select_add_fusion.3), channel_id=1, source_target_pairs={{0,16},{4,20},{8,24},{12,28},{16,0},{20,4},{24,8},{28,12},{32,48},... | collective-permute-start | bytes 98312 | tf_op jit(solution)/shard_map/ppermute | solution.py:229
  43.8 2.7 %collective-permute-done.9 = f32[16,512]{1,0:T(8,128)S(1)} collective-permute-done((f32[16,512]{1,0:T(8,128)S(1)}, f32[16,512]{1,0:T(8,128)S(1)}, u32[]{:S(2)}, u32[]{:S(2)}) %collective-permute-start.9) | collective-permute-done | bytes 32800 | tf_op jit(solution)/shard_map/ppermute | solution.py:229
  46.5 3.5 %collective-permute-start.10 = (f32[16,512]{1,0:T(8,128)S(1)}, f32[16,512]{1,0:T(8,128)S(1)}, u32[]{:S(2)}, u32[]{:S(2)}) collective-permute-start(f32[16,512]{1,0:T(8,128)S(1)} %select_add_fusion.2), channel_id=1, source_target_pairs={{0,32},{4,36},{8,40},{12,44},{16,48},{20,52},{24,56},{28,60},{32,0... | collective-permute-start | bytes 98312 | tf_op jit(solution)/shard_map/ppermute | solution.py:229
  49.9 1.9 %collective-permute-done.10 = f32[16,512]{1,0:T(8,128)S(1)} collective-permute-done((f32[16,512]{1,0:T(8,128)S(1)}, f32[16,512]{1,0:T(8,128)S(1)}, u32[]{:S(2)}, u32[]{:S(2)}) %collective-permute-start.10) | collective-permute-done | bytes 32800 | tf_op jit(solution)/shard_map/ppermute | solution.py:229
  51.8 4.3 %collective-permute-start.11 = (f32[16,512]{1,0:T(8,128)S(1)}, f32[16,512]{1,0:T(8,128)S(1)}, u32[]{:S(2)}, u32[]{:S(2)}) collective-permute-start(f32[16,512]{1,0:T(8,128)S(1)} %select_add_fusion.1), channel_id=1, source_target_pairs={{0,64},{4,68},{8,72},{12,76},{16,80},{20,84},{24,88},{28,92},{32,9... | collective-permute-start | bytes 98312 | tf_op jit(solution)/shard_map/ppermute | solution.py:229
  56.2 0.0 copy-done.8
  56.2 0.0 copy-done.10
  56.2 1.1 %copy-done.4 = bf16[3,256,512]{2,1,0:T(8,128)(2,1)S(1)} copy-done((bf16[3,256,512]{2,1,0:T(8,128)(2,1)S(1)}, bf16[3,256,512]{2,1,0:T(8,128)(2,1)}, u32[]{:S(2)}) %copy-start.4) | copy-done | bytes 786456
  57.3 1.2 %copy-done.7 = f32[4,512,128]{2,1,0:T(8,128)S(1)} copy-done((f32[4,512,128]{2,1,0:T(8,128)S(1)}, f32[4,512,128]{2,1,0:T(8,128)}, u32[]{:S(2)}) %copy-start.7) | copy-done | bytes 1048600
  58.5 4.2 %local.1 = (f32[4,512,128]{2,1,0:T(8,128)S(1)}, f32[4,512,128]{2,1,0:T(8,128)S(1)}) custom-call(bf16[3,256,512]{2,1,0:T(8,128)(2,1)S(1)} %copy-done.4, bf16[3,256,512]{2,1,0:T(8,128)(2,1)S(1)} %project.3.high, bf16[3,16,512]{2,1,0:T(8,128)(2,1)S(1)} %collective-permute-done.6.halo, f32[3,3,512]{2,1,0:T(4,128)S(1)} %copy-done.9, f32[16,512]{1,0:T(8,128)S(1)} %copy-done.5, ...), custom_call_target="tpu_custom_call" | custom-call | flops 16777216 | bytes 6291456 | tf_op jit(solution)/shard_map/local/pallas_call | solution.py:266
  62.8 0.0 collective-permute-done.11
  62.8 1.8 %gate.1 = (bf16[256,512]{1,0:T(8,128)(2,1)S(1)}, bf16[256,512]{1,0:T(8,128)(2,1)S(1)}) custom-call(f32[4,512,128]{2,1,0:T(8,128)S(1)} %get-tuple-element.14.query, f32[4,512,128]{2,1,0:T(8,128)S(1)} %get-tuple-element.15.part, f32[16,512]{1,0:T(8,128)S(1)} %select_add_fusion.state, f32[16,512]{1,0:T(8,128)S(1)} %copy-done.5, f32[16,512]{1,0:T(8,128)S(1)} %copy-done.8), custom_call_target="tpu_custom_call" | custom-call | flops 8388608 | bytes 3145728 | tf_op jit(solution)/shard_map/gate/pallas_call | solution.py:287
  64.6 0.1 collective-permute-start.15
  64.7 3.7 %collective-permute-start.13 = (bf16[256,512]{1,0:T(8,128)(2,1)S(1)}, bf16[256,512]{1,0:T(8,128)(2,1)S(1)}, u32[]{:S(2)}, u32[]{:S(2)}) collective-permute-start(bf16[256,512]{1,0:T(8,128)(2,1)S(1)} %get-tuple-element.17.own), channel_id=1, source_target_pairs={{0,3},{1,0},{2,1},{3,2},{4,7},{5,4},{6,5},{7,6},{8,11},{9,8},{10,9... | collective-permute-start | bytes 786440 | tf_op jit(solution)/shard_map/ppermute | solution.py:39
  68.4 1.9 %collective-permute-start.16 = (bf16[256,512]{1,0:T(8,128)(2,1)S(1)}, bf16[256,512]{1,0:T(8,128)(2,1)S(1)}, u32[]{:S(2)}, u32[]{:S(2)}) collective-permute-start(bf16[256,512]{1,0:T(8,128)(2,1)S(1)} %get-tuple-element.18.own), channel_id=1, source_target_pairs={{0,3},{1,0},{2,1},{3,2},{4,7},{5,4},{6,5},{7,6},{8,11},{9,8},{10,9... | collective-permute-start | bytes 786440 | tf_op jit(solution)/shard_map/ppermute | solution.py:39
  70.4 3.1 %collective-permute-done.15.left = bf16[256,512]{1,0:T(8,128)(2,1)S(1)} collective-permute-done((bf16[256,512]{1,0:T(8,128)(2,1)S(1)}, bf16[256,512]{1,0:T(8,128)(2,1)S(1)}, u32[]{:S(2)}, u32[]{:S(2)}) %collective-permute-start.15) | collective-permute-done | bytes 262176 | tf_op jit(solution)/shard_map/ppermute | solution.py:39
  73.5 0.0 collective-permute-start.17
  73.5 2.6 %collective-permute-start.12 = (bf16[256,512]{1,0:T(8,128)(2,1)S(1)}, bf16[256,512]{1,0:T(8,128)(2,1)S(1)}, u32[]{:S(2)}, u32[]{:S(2)}) collective-permute-start(bf16[256,512]{1,0:T(8,128)(2,1)S(1)} %get-tuple-element.17.own), channel_id=1, source_target_pairs={{0,1},{1,2},{2,3},{3,0},{4,5},{5,6},{6,7},{7,4},{8,9},{9,10},{10,1... | collective-permute-start | bytes 786440 | tf_op jit(solution)/shard_map/ppermute | solution.py:39
  76.1 0.0 collective-permute-done.13.right
  76.1 2.6 %collective-permute-start.14 = (bf16[256,512]{1,0:T(8,128)(2,1)S(1)}, bf16[256,512]{1,0:T(8,128)(2,1)S(1)}, u32[]{:S(2)}, u32[]{:S(2)}) collective-permute-start(bf16[256,512]{1,0:T(8,128)(2,1)S(1)} %collective-permute-done.13.right), channel_id=1, source_target_pairs={{0,3},{1,0},{2,1},{3,2},{4,7},{5,4},{6,5},{7,6},{8,11},{9,8},{10,9... | collective-permute-start | bytes 786440 | tf_op jit(solution)/shard_map/ppermute | solution.py:39
  78.7 0.0 collective-permute-done.16.right
  78.7 2.8 %collective-permute-done.17.far = bf16[256,512]{1,0:T(8,128)(2,1)S(1)} collective-permute-done((bf16[256,512]{1,0:T(8,128)(2,1)S(1)}, bf16[256,512]{1,0:T(8,128)(2,1)S(1)}, u32[]{:S(2)}, u32[]{:S(2)}) %collective-permute-start.17) | collective-permute-done | bytes 262176 | tf_op jit(solution)/shard_map/ppermute | solution.py:39
  81.5 0.0 copy-done.2
  81.5 1.4 %mix.2.rest_0_ = bf16[512,512]{1,0:T(8,128)(2,1)} custom-call(s32[1]{0:T(128)} %bitcast.me_ref, bf16[256,512]{1,0:T(8,128)(2,1)S(1)} %get-tuple-element.18.own, bf16[256,512]{1,0:T(8,128)(2,1)S(1)} %collective-permute-done.15.left, bf16[256,512]{1,0:T(8,128)(2,1)S(1)} %collective-permute-done.16.right, bf16[256,512]{1,0:T(8,128)(2,1)S(1)} %collective-permute-done.17.far, ...), custom_call_target="tpu_custom_call" | custom-call | flops 536870912 | bytes 2097152 | tf_op jit(solution)/shard_map/mix/pallas_call | solution.py:210
  82.9 1.4 %collective-permute-done.12.left = bf16[256,512]{1,0:T(8,128)(2,1)S(1)} collective-permute-done((bf16[256,512]{1,0:T(8,128)(2,1)S(1)}, bf16[256,512]{1,0:T(8,128)(2,1)S(1)}, u32[]{:S(2)}, u32[]{:S(2)}) %collective-permute-start.12) | collective-permute-done | bytes 262176 | tf_op jit(solution)/shard_map/ppermute | solution.py:39
  84.3 0.0 collective-permute-done.14.far
  84.3 1.4 %mix.3 = bf16[512,512]{1,0:T(8,128)(2,1)} custom-call(s32[1]{0:T(128)} %bitcast.me_ref, bf16[256,512]{1,0:T(8,128)(2,1)S(1)} %get-tuple-element.17.own, bf16[256,512]{1,0:T(8,128)(2,1)S(1)} %collective-permute-done.12.left, bf16[256,512]{1,0:T(8,128)(2,1)S(1)} %collective-permute-done.13.right, ...), custom_call_target="tpu_custom_call", output_to_operand_aliasing={{}: (6, {})} | custom-call | flops 536870912 | bytes 2097152 | tf_op jit(solution)/shard_map/mix/pallas_call | solution.py:210
  (8 shorter events, 0.1 us)
Async XLA Ops:
  1.1 8.7 %collective-permute-start.4 = (bf16[256,512]{1,0:T(8,128)(2,1)S(1)}, bf16[256,512]{1,0:T(8,128)(2,1)S(1)}, u32[]{:S(2)}, u32[]{:S(2)}) collective-permute-start(bf16[256,512]{1,0:T(8,128)(2,1)S(1)} %get-tuple-element.19.own), channel_id=1, source_target_pairs={{0,3},{1,0},{2,1},{3,2},{4,7},{5,4},{6,5},{7,6},{8,11},{9,8},{10,9... | collective-permute-start | bytes 786440 | tf_op jit(solution)/shard_map/ppermute | solution.py:39
  4.2 10.4 %collective-permute-start = (bf16[256,512]{1,0:T(8,128)(2,1)S(1)}, bf16[256,512]{1,0:T(8,128)(2,1)S(1)}, u32[]{:S(2)}, u32[]{:S(2)}) collective-permute-start(bf16[256,512]{1,0:T(8,128)(2,1)S(1)} %get-tuple-element.20.own), channel_id=1, source_target_pairs={{0,1},{1,2},{2,3},{3,0},{4,5},{5,6},{6,7},{7,4},{8,9},{9,10},{10,1... | collective-permute-start | bytes 786440 | tf_op jit(solution)/shard_map/ppermute | solution.py:39
  4.2 16.1 %collective-permute-start.3 = (bf16[256,512]{1,0:T(8,128)(2,1)S(1)}, bf16[256,512]{1,0:T(8,128)(2,1)S(1)}, u32[]{:S(2)}, u32[]{:S(2)}) collective-permute-start(bf16[256,512]{1,0:T(8,128)(2,1)S(1)} %get-tuple-element.19.own), channel_id=1, source_target_pairs={{0,1},{1,2},{2,3},{3,0},{4,5},{5,6},{6,7},{7,4},{8,9},{9,10},{10,1... | collective-permute-start | bytes 786440 | tf_op jit(solution)/shard_map/ppermute | solution.py:39
  9.8 10.5 %collective-permute-start.5 = (bf16[256,512]{1,0:T(8,128)(2,1)S(1)}, bf16[256,512]{1,0:T(8,128)(2,1)S(1)}, u32[]{:S(2)}, u32[]{:S(2)}) collective-permute-start(bf16[256,512]{1,0:T(8,128)(2,1)S(1)} %collective-permute-done.4.right), channel_id=1, source_target_pairs={{0,3},{1,0},{2,1},{3,2},{4,7},{5,4},{6,5},{7,6},{8,11},{9,8},{10,9... | collective-permute-start | bytes 786440 | tf_op jit(solution)/shard_map/ppermute | solution.py:39
  13.5 12.9 %collective-permute-start.1 = (bf16[256,512]{1,0:T(8,128)(2,1)S(1)}, bf16[256,512]{1,0:T(8,128)(2,1)}, u32[]{:S(2)}, u32[]{:S(2)}) collective-permute-start(bf16[256,512]{1,0:T(8,128)(2,1)S(1)} %get-tuple-element.20.own), channel_id=1, source_target_pairs={{0,3},{1,0},{2,1},{3,2},{4,7},{5,4},{6,5},{7,6},{8,11},{9,8},{10,9... | collective-permute-start | bytes 786440 | tf_op jit(solution)/shard_map/ppermute | solution.py:39
  14.7 11.7 %collective-permute-start.2 = (bf16[256,512]{1,0:T(8,128)(2,1)S(1)}, bf16[256,512]{1,0:T(8,128)(2,1)}, u32[]{:S(2)}, u32[]{:S(2)}) collective-permute-start(bf16[256,512]{1,0:T(8,128)(2,1)S(1)} %collective-permute-done.left), channel_id=1, source_target_pairs={{0,1},{1,2},{2,3},{3,0},{4,5},{5,6},{6,7},{7,4},{8,9},{9,10},{10,1... | collective-permute-start | bytes 786440 | tf_op jit(solution)/shard_map/ppermute | solution.py:39
  20.3 2.8 %copy-start = (bf16[2048,3,512]{2,0,1:T(8,128)(2,1)S(1)}, bf16[2048,3,512]{2,0,1:T(8,128)(2,1)}, u32[]{:S(2)}) copy-start(bf16[2048,3,512]{2,0,1:T(8,128)(2,1)} %param.8) | copy-start | bytes 18874372
  23.1 3.3 %copy-start.1 = (bf16[2048,3,512]{2,0,1:T(8,128)(2,1)S(1)}, bf16[2048,3,512]{2,0,1:T(8,128)(2,1)}, u32[]{:S(2)}) copy-start(bf16[2048,3,512]{2,0,1:T(8,128)(2,1)} %param.8) | copy-start | bytes 18874372
  23.1 6.1 %copy-start.5 = (f32[16,512]{1,0:T(8,128)S(1)}, f32[16,512]{1,0:T(8,128)}, u32[]{:S(2)}) copy-start(f32[16,512]{1,0:T(8,128)} %decay.5) | copy-start | bytes 98308
  23.1 6.2 %copy-start.9 = (f32[3,3,512]{2,1,0:T(4,128)S(1)}, f32[3,3,512]{2,1,0:T(4,128)}, u32[]{:S(2)}) copy-start(f32[3,3,512]{2,1,0:T(4,128)} %taps.3) | copy-start | bytes 55300
  24.9 31.3 %copy-start.8 = (f32[16,512]{1,0:T(8,128)S(1)}, f32[16,512]{1,0:T(8,128)}, u32[]{:S(2)}) copy-start(f32[16,512]{1,0:T(8,128)} %residue.3) | copy-start | bytes 98308
  24.9 31.3 %copy-start.10 = (f32[512]{0:T(512)S(1)}, f32[512]{0:T(512)}, u32[]{:S(2)}) copy-start(f32[512]{0:T(512)} %param.12) | copy-start | bytes 6148
  24.9 56.6 %copy-start.2 = (bf16[2048,512]{1,0:T(8,128)(2,1)S(1)}, bf16[2048,512]{1,0:T(8,128)(2,1)}, u32[]{:S(2)}) copy-start(bf16[2048,512]{1,0:T(8,128)(2,1)} %w_ref.3) | copy-start | bytes 6291460
  24.9 4.3 %collective-permute-start.6 = (bf16[3,16,512]{2,1,0:T(8,128)(2,1)S(1)}, bf16[3,16,512]{2,1,0:T(8,128)(2,1)S(1)}, u32[]{:S(2)}, u32[]{:S(2)}) collective-permute-start(bf16[3,16,512]{2,1,0:T(8,128)(2,1)S(1)} %slice.12), channel_id=1, source_target_pairs={{0,4},{4,8},{8,12},{12,16},{16,20},{20,24},{24,28},{28,32},{32,36}... | collective-permute-start | bytes 147464 | tf_op jit(solution)/shard_map/ppermute | solution.py:250
  32.0 0.9 %copy-start.3 = (bf16[3,256,512]{2,1,0:T(8,128)(2,1)}, bf16[3,256,512]{2,1,0:T(8,128)(2,1)S(1)}, u32[]{:S(2)}) copy-start(bf16[3,256,512]{2,1,0:T(8,128)(2,1)S(1)} %project.2.low) | copy-start | bytes 2359300
  32.9 1.0 %copy-start.6 = (f32[4,512,128]{2,1,0:T(8,128)}, f32[4,512,128]{2,1,0:T(8,128)S(1)}, u32[]{:S(2)}) copy-start(f32[4,512,128]{2,1,0:T(8,128)S(1)} %get-tuple-element.12.sig) | copy-start | bytes 3145732
  33.8 3.1 %collective-permute-start.7 = (f32[16,512]{1,0:T(8,128)S(1)}, f32[16,512]{1,0:T(8,128)S(1)}, u32[]{:S(2)}, u32[]{:S(2)}) collective-permute-start(f32[16,512]{1,0:T(8,128)S(1)} %get-tuple-element.16), channel_id=1, source_target_pairs={{0,4},{4,0},{8,12},{12,8},{16,20},{20,16},{24,28},{28,24},{32,36},... | collective-permute-start | bytes 98312 | tf_op jit(solution)/shard_map/ppermute | solution.py:229
  36.9 4.0 %collective-permute-start.8 = (f32[16,512]{1,0:T(8,128)S(1)}, f32[16,512]{1,0:T(8,128)S(1)}, u32[]{:S(2)}, u32[]{:S(2)}) collective-permute-start(f32[16,512]{1,0:T(8,128)S(1)} %select_add_fusion.4), channel_id=1, source_target_pairs={{0,8},{4,12},{8,0},{12,4},{16,24},{20,28},{24,16},{28,20},{32,40},... | collective-permute-start | bytes 98312 | tf_op jit(solution)/shard_map/ppermute | solution.py:229
  41.0 5.5 %collective-permute-start.9 = (f32[16,512]{1,0:T(8,128)S(1)}, f32[16,512]{1,0:T(8,128)S(1)}, u32[]{:S(2)}, u32[]{:S(2)}) collective-permute-start(f32[16,512]{1,0:T(8,128)S(1)} %select_add_fusion.3), channel_id=1, source_target_pairs={{0,16},{4,20},{8,24},{12,28},{16,0},{20,4},{24,8},{28,12},{32,48},... | collective-permute-start | bytes 98312 | tf_op jit(solution)/shard_map/ppermute | solution.py:229
  46.5 5.3 %collective-permute-start.10 = (f32[16,512]{1,0:T(8,128)S(1)}, f32[16,512]{1,0:T(8,128)S(1)}, u32[]{:S(2)}, u32[]{:S(2)}) collective-permute-start(f32[16,512]{1,0:T(8,128)S(1)} %select_add_fusion.2), channel_id=1, source_target_pairs={{0,32},{4,36},{8,40},{12,44},{16,48},{20,52},{24,56},{28,60},{32,0... | collective-permute-start | bytes 98312 | tf_op jit(solution)/shard_map/ppermute | solution.py:229
  51.8 10.9 %collective-permute-start.11 = (f32[16,512]{1,0:T(8,128)S(1)}, f32[16,512]{1,0:T(8,128)S(1)}, u32[]{:S(2)}, u32[]{:S(2)}) collective-permute-start(f32[16,512]{1,0:T(8,128)S(1)} %select_add_fusion.1), channel_id=1, source_target_pairs={{0,64},{4,68},{8,72},{12,76},{16,80},{20,84},{24,88},{28,92},{32,9... | collective-permute-start | bytes 98312 | tf_op jit(solution)/shard_map/ppermute | solution.py:229
  56.2 1.1 %copy-start.4 = (bf16[3,256,512]{2,1,0:T(8,128)(2,1)S(1)}, bf16[3,256,512]{2,1,0:T(8,128)(2,1)}, u32[]{:S(2)}) copy-start(bf16[3,256,512]{2,1,0:T(8,128)(2,1)} %copy-done.3) | copy-start | bytes 2359300
  57.3 1.2 %copy-start.7 = (f32[4,512,128]{2,1,0:T(8,128)S(1)}, f32[4,512,128]{2,1,0:T(8,128)}, u32[]{:S(2)}) copy-start(f32[4,512,128]{2,1,0:T(8,128)} %copy-done.6) | copy-start | bytes 3145732
  64.6 8.9 %collective-permute-start.15 = (bf16[256,512]{1,0:T(8,128)(2,1)S(1)}, bf16[256,512]{1,0:T(8,128)(2,1)S(1)}, u32[]{:S(2)}, u32[]{:S(2)}) collective-permute-start(bf16[256,512]{1,0:T(8,128)(2,1)S(1)} %get-tuple-element.18.own), channel_id=1, source_target_pairs={{0,1},{1,2},{2,3},{3,0},{4,5},{5,6},{6,7},{7,4},{8,9},{9,10},{10,1... | collective-permute-start | bytes 786440 | tf_op jit(solution)/shard_map/ppermute | solution.py:39
  64.7 11.4 %collective-permute-start.13 = (bf16[256,512]{1,0:T(8,128)(2,1)S(1)}, bf16[256,512]{1,0:T(8,128)(2,1)S(1)}, u32[]{:S(2)}, u32[]{:S(2)}) collective-permute-start(bf16[256,512]{1,0:T(8,128)(2,1)S(1)} %get-tuple-element.17.own), channel_id=1, source_target_pairs={{0,3},{1,0},{2,1},{3,2},{4,7},{5,4},{6,5},{7,6},{8,11},{9,8},{10,9... | collective-permute-start | bytes 786440 | tf_op jit(solution)/shard_map/ppermute | solution.py:39
  68.4 10.3 %collective-permute-start.16 = (bf16[256,512]{1,0:T(8,128)(2,1)S(1)}, bf16[256,512]{1,0:T(8,128)(2,1)S(1)}, u32[]{:S(2)}, u32[]{:S(2)}) collective-permute-start(bf16[256,512]{1,0:T(8,128)(2,1)S(1)} %get-tuple-element.18.own), channel_id=1, source_target_pairs={{0,3},{1,0},{2,1},{3,2},{4,7},{5,4},{6,5},{7,6},{8,11},{9,8},{10,9... | collective-permute-start | bytes 786440 | tf_op jit(solution)/shard_map/ppermute | solution.py:39
  73.5 8.0 %collective-permute-start.17 = (bf16[256,512]{1,0:T(8,128)(2,1)S(1)}, bf16[256,512]{1,0:T(8,128)(2,1)S(1)}, u32[]{:S(2)}, u32[]{:S(2)}) collective-permute-start(bf16[256,512]{1,0:T(8,128)(2,1)S(1)} %collective-permute-done.15.left), channel_id=1, source_target_pairs={{0,1},{1,2},{2,3},{3,0},{4,5},{5,6},{6,7},{7,4},{8,9},{9,10},{10,1... | collective-permute-start | bytes 786440 | tf_op jit(solution)/shard_map/ppermute | solution.py:39
  73.5 10.8 %collective-permute-start.12 = (bf16[256,512]{1,0:T(8,128)(2,1)S(1)}, bf16[256,512]{1,0:T(8,128)(2,1)S(1)}, u32[]{:S(2)}, u32[]{:S(2)}) collective-permute-start(bf16[256,512]{1,0:T(8,128)(2,1)S(1)} %get-tuple-element.17.own), channel_id=1, source_target_pairs={{0,1},{1,2},{2,3},{3,0},{4,5},{5,6},{6,7},{7,4},{8,9},{9,10},{10,1... | collective-permute-start | bytes 786440 | tf_op jit(solution)/shard_map/ppermute | solution.py:39
  76.1 8.2 %collective-permute-start.14 = (bf16[256,512]{1,0:T(8,128)(2,1)S(1)}, bf16[256,512]{1,0:T(8,128)(2,1)S(1)}, u32[]{:S(2)}, u32[]{:S(2)}) collective-permute-start(bf16[256,512]{1,0:T(8,128)(2,1)S(1)} %collective-permute-done.13.right), channel_id=1, source_target_pairs={{0,3},{1,0},{2,1},{3,2},{4,7},{5,4},{6,5},{7,6},{8,11},{9,8},{10,9... | collective-permute-start | bytes 786440 | tf_op jit(solution)/shard_map/ppermute | solution.py:39
where the time goes:
time: 86 us; the launch traced here: 85.7 us
  starting transfers between devices  35.1 us (41%)
  waiting for transfers between devices  26.1 us (30%)
  Pallas kernels  16.1 us (19%)
  local copies, waits for them, and re-layouts  8.12 us (9%)
    ppermute x12, starting transfers between devices, turn(): lax.ppermute(block, 'ch', [(i, (i + distance) % count) for i in range(cou...  19.3 us
    ppermute x12, waiting for transfers between devices, turn(): lax.ppermute(block, 'ch', [(i, (i + distance) % count) for i in range(cou...  18.2 us
    ppermute x5, starting transfers between devices, carry_in(): other = lax.ppermute(end, 'seq', [(i, i ^ span) for i in range(devices)])  14.4 us
    ppermute x5, waiting for transfers between devices, carry_in(): other = lax.ppermute(end, 'seq', [(i, i ^ span) for i in range(devices)])  7.87 us
    unnamed x22, local copies, waits for them, and re-layouts  7.05 us
    pallas_call x2, Pallas kernels, project(): pl.pallas_call(project_kernel, out_shape=pltpu.VMEM((streams, rows, cols)...  4.6 us
    pallas_call x1, Pallas kernels, shards(): pl.pallas_call(local_kernel, out_shape=(pltpu.VMEM(tiled, F32), pltpu.VME...  4.23 us
    pallas_call x2, Pallas kernels, mix(): pl.pallas_call(mix_kernel, out_shape=jax.ShapeDtypeStruct((2 * rows, cols...  2.83 us
  transfers between devices with their start and end apart: 18, of which 10 were waited for; matrix products, arithmetic and copies ran while one was open for 0% of the time, Pallas kernels for 12%

commit v1 on v0

v1 whole, which is shorter than its diff:
```python
from functools import partial

import jax
import jax.numpy as jnp
from jax import lax
from jax.experimental import pallas as pl
from jax.experimental.pallas import tpu as pltpu
from jax.sharding import PartitionSpec as P

LANES = 128
SUB = 8
F32 = jnp.float32
BF16 = jnp.bfloat16
MIB = 1 << 20


def vmem():
    return pl.BlockSpec(memory_space=pltpu.VMEM)


def near(x):
    return pltpu.with_memory_space_constraint(x, pltpu.VMEM)


def params(mib=24):
    return pltpu.CompilerParams(vmem_limit_bytes=mib * MIB)


def cost(flops, nbytes, exps=0):
    return pl.CostEstimate(flops=flops, bytes_accessed=nbytes, transcendentals=exps)


def turn(block, distance):
    count = lax.axis_size("ch")
    return lax.ppermute(block, "ch", [(i, (i + distance) % count) for i in range(count)])


def ring(low, high, work=None):
    low_left, low_right = turn(low, 1), turn(low, -1)
    high_left, high_right = turn(high, 1), turn(high, -1)
    done = None
    if work is not None:
        done = work(low, high)
        done, high_right = lax.optimization_barrier((done, high_right))
    high_far = turn(high_right, -1)
    low_far = turn(low_left, 1)
    return (low, low_left, low_right, low_far), (high, high_left, high_right, high_far), done


def source(step, depth):
    owner = lax.rem(lax.axis_index("ch") + step, 4)
    return pl.ds(pl.multiple_of(owner * depth, depth), depth)


def own_kernel(low, high, w_ref, low_ref, high_ref):
    depth = low.shape[1]
    for stream in range(w_ref.shape[0]):
        part = w_ref[stream, source(0, depth), :]
        low_ref[stream] = jnp.dot(low[...], part, preferred_element_type=F32)
        high_ref[stream] = jnp.dot(high[...], part, preferred_element_type=F32)


def near_kernel(part, left, right, w_ref, out_ref):
    depth = left.shape[1]
    for stream in range(w_ref.shape[0]):
        total = part[stream]
        for block, step in ((left, 3), (right, 1)):
            total += jnp.dot(
                block[...], w_ref[stream, source(step, depth), :], preferred_element_type=F32
            )
        out_ref[stream] = total


def high_kernel(part, left, right, far, w_ref, out_ref):
    depth = left.shape[1]
    for stream in range(w_ref.shape[0]):
        total = part[stream]
        for block, step in ((left, 3), (right, 1), (far, 2)):
            total += jnp.dot(
                block[...], w_ref[stream, source(step, depth), :], preferred_element_type=F32
            )
        out_ref[stream] = total.astype(BF16)


def filtered(ext, slot, taps, stream, at, size, lanes, width):
    total = taps[stream, 0:1, lanes] * ext[slot, pl.ds(at + SUB, size), width]
    for lag in range(1, 3):
        total += taps[stream, lag : lag + 1, lanes] * ext[slot, pl.ds(at + SUB - lag, size), width]
    return total


def tile_of(tile):
    return slice(tile * LANES, (tile + 1) * LANES)


def spread(ref, row, lanes):
    return jnp.broadcast_to(ref[row : row + 1, lanes], (SUB, LANES))


def tree(terms):
    while len(terms) > 1:
        terms = [sum(terms[j : j + 2]) for j in range(0, len(terms), 2)]
    return terms[0]


def scan_ends(sig_ref, sub_ref, end_ref, decay, tile, rows):
    lanes = tile_of(tile)
    modes = decay.shape[0]
    steps = rows // SUB
    rates = [spread(decay, m, lanes) for m in range(modes)]
    fade = [jnp.exp(-r) for r in rates]

    def step(i, held):
        now = sig_ref[tile, pl.ds(i, SUB, stride=steps), :]
        return tuple(f * h + now for f, h in zip(fade, held))

    zero = tuple(jnp.zeros((SUB, LANES), F32) for _ in range(modes))
    held = lax.fori_loop(0, steps, step, zero, unroll=8)
    later = (SUB - 1 - lax.broadcasted_iota(jnp.int32, (SUB, LANES), 0)).astype(F32) * steps
    for m in range(modes):
        sub_ref[m, :, lanes] = held[m]
        end_ref[m : m + 1, lanes] = jnp.sum(
            held[m] * jnp.exp(-rates[m] * later), axis=0, keepdims=True
        )


def late_kernel(high, taps, decay, sig_ref, sub_ref, end_ref, ext):
    tiles, rows, _ = sig_ref.shape
    ext[:, 0:SUB, :] = jnp.zeros((2, SUB, ext.shape[2]), F32)
    for slot in range(2):
        for at in range(0, rows, 64):
            ext[slot, pl.ds(at + SUB, 64), :] = high[slot + 1, pl.ds(at, 64), :].astype(F32)
    kept = lax.broadcasted_iota(jnp.int32, (64, LANES), 0) >= 2
    for tile in range(tiles):
        lanes = tile_of(tile)
        for at in range(0, rows, 64):
            value = filtered(ext, 0, taps, 1, at, 64, lanes, lanes)
            value *= filtered(ext, 1, taps, 2, at, 64, lanes, lanes)
            if at == 0:
                value = jnp.where(kept, value, 0.0)
            sig_ref[tile, pl.ds(at, 64), :] = value
        scan_ends(sig_ref, sub_ref, end_ref, decay, tile, rows)


def early_kernel(
    part, far, w_ref, high, halo, taps, decay, late_end, sig_ref, sub_ref, mid_ref, end_ref, ext
):
    tiles, rows, _ = sig_ref.shape
    rows -= SUB
    depth = far.shape[1]
    for slot in range(2):
        total = part[slot + 1] + jnp.dot(
            far[...], w_ref[slot + 1, source(2, depth), :], preferred_element_type=F32
        )
        ext[slot, pl.ds(SUB, rows), :] = total.astype(BF16).astype(F32)
        ext[slot, 0:SUB, :] = halo[slot + 1, 8:16, :].astype(F32)
        ext[slot, pl.ds(SUB + rows, SUB), :] = high[slot + 1, 0:16, :].astype(F32)[0:SUB]
    for tile in range(tiles):
        lanes = tile_of(tile)
        for at in range(0, rows + SUB, 64):
            size = min(64, rows + SUB - at)
            value = filtered(ext, 0, taps, 1, at, size, lanes, lanes)
            sig_ref[tile, pl.ds(at, size), :] = value * filtered(
                ext, 1, taps, 2, at, size, lanes, lanes
            )
        scan_ends(sig_ref, sub_ref, mid_ref, decay, tile, rows)
        rate = decay[:, lanes]
        end_ref[:, lanes] = (
            jnp.exp(-float(rows) * rate) * mid_ref[:, lanes]
            + late_end[:, lanes]
            + jnp.exp(-float(rows - 1) * rate) * sig_ref[tile, rows : rows + 1, :]
            + jnp.exp(-float(rows - 2) * rate) * sig_ref[tile, rows + 1 : rows + 2, :]
        )


def local_kernel(
    tile,
    part,
    far,
    w_ref,
    high,
    halo,
    taps,
    decay,
    residue,
    skip,
    low_sig,
    low_sub,
    mid,
    high_sig,
    high_sub,
    query_ref,
    out_ref,
    ext,
):
    lanes = tile_of(tile)
    whole = slice(0, LANES)
    modes = decay.shape[0]
    rows = high_sig.shape[1]
    steps = rows // SUB
    depth = far.shape[1]
    total = part[0, :, lanes] + jnp.dot(
        far[...], w_ref[0, source(2, depth), lanes], preferred_element_type=F32
    )
    ext[0, pl.ds(SUB, rows), :] = total.astype(BF16).astype(F32)
    ext[0, 0:SUB, :] = halo[0, 8:16, lanes].astype(F32)
    ext[0, pl.ds(SUB + rows, rows), :] = high[0, :, lanes].astype(F32)
    for at in range(0, 2 * rows, 64):
        query_ref[pl.ds(at, 64), :] = filtered(ext, 0, taps, 0, at, 64, lanes, whole)

    place = lax.broadcasted_iota(jnp.int32, (SUB, LANES), 0)
    rates = [spread(decay, m, lanes) for m in range(modes)]
    fade = [jnp.exp(-r) for r in rates]
    gain = [residue[m : m + 1, lanes] * jnp.sqrt(r) for m, r in enumerate(rates)]
    direct = spread(skip, 0, lanes)
    one = low_sig[tile, rows : rows + 1, :]
    two = low_sig[tile, rows + 1 : rows + 2, :]

    def entering(sub, first, m):
        run = jnp.where(place >= 1, pltpu.roll(sub, 1, 0), first)
        for shift in (1, 2, 4):
            before = jnp.where(place >= shift, pltpu.roll(run, shift, 0), 0.0)
            run = run + jnp.exp(-rates[m] * float(steps * shift)) * before
        return run

    def advance(held, now, at):
        held = tuple(f * h + now for f, h in zip(fade, held))
        out_ref[pl.ds(at, SUB, stride=steps), :] = tree(
            [g * h for g, h in zip(gain, held)] + [direct * now]
        )
        return held

    held = tuple(entering(low_sub[m, :, lanes], 0.0, m) for m in range(modes))
    lax.fori_loop(
        0,
        steps,
        lambda i, h: advance(h, low_sig[tile, pl.ds(i, SUB, stride=steps), :], i),
        held,
        unroll=4,
    )
    held = []
    for m in range(modes):
        sub = high_sub[m, :, lanes]
        extra = jnp.exp(-rates[m] * float(steps - 1)) * one + jnp.exp(-rates[m] * float(steps - 2)) * two
        held.append(entering(sub + jnp.where(place == 0, extra, 0.0), mid[m : m + 1, lanes], m))
    held = tuple(held)
    for i, row in ((0, one), (1, two)):
        now = high_sig[tile, pl.ds(i, SUB, stride=steps), :]
        held = advance(held, now + jnp.where(place == 0, row, 0.0), rows + i)
    lax.fori_loop(
        2,
        steps,
        lambda i, h: advance(h, high_sig[tile, pl.ds(i, SUB, stride=steps), :], rows + i),
        held,
        unroll=3,
    )


def gate_kernel(base, *refs):
    tiles = 4
    query, part = refs[:tiles], refs[tiles : 2 * tiles]
    state, decay, residue, out_ref = refs[2 * tiles :]
    modes = decay.shape[0]
    rows = out_ref.shape[0]
    ahead = float(base + 1) + lax.broadcasted_iota(jnp.int32, (SUB, LANES), 0).astype(F32)
    for tile in range(tiles):
        lanes = tile_of(tile)
        rates = [spread(decay, m, lanes) for m in range(modes)]
        fade = [jnp.exp(-float(SUB) * r) for r in rates]
        first = tuple(
            residue[m : m + 1, lanes] * state[m : m + 1, lanes] * jnp.sqrt(r) * jnp.exp(-r * ahead)
            for m, r in enumerate(rates)
        )

        def piece(at, held):
            value = query[tile][pl.ds(at + base, SUB), :] * (
                part[tile][pl.ds(at + base, SUB), :] + tree(list(held))
            )
            return value, tuple(f * h for f, h in zip(fade, held))

        def step(i, held):
            at = pl.multiple_of(i * 16, 16)
            one, held = piece(at, held)
            two, held = piece(at + SUB, held)
            out_ref[pl.ds(at, 16), lanes] = jnp.concatenate([one, two], 0).astype(BF16)
            return held

        lax.fori_loop(0, rows // 16, step, first, unroll=4)


def mix_kernel(plan, w_ref, *refs):
    blocks, rest = refs[: len(plan)], refs[len(plan) :]
    out_ref = rest[-1]
    depth = blocks[0].shape[1]
    total = None if len(rest) == 1 or rest[0].dtype != F32 else rest[0][...]
    for block, step in zip(blocks, plan):
        term = jnp.dot(block[...], w_ref[source(step, depth), :], preferred_element_type=F32)
        total = term if total is None else total + term
    out_ref[...] = total.astype(out_ref.dtype)


def mix(weights, blocks, plan):
    rows, depth = blocks[0].shape
    cols = weights.shape[1]
    return pl.pallas_call(
        partial(mix_kernel, plan),
        out_shape=pltpu.VMEM((rows, cols), F32),
        in_specs=[vmem()] * (1 + len(plan)),
        out_specs=vmem(),
        compiler_params=params(),
        cost_estimate=cost(2 * rows * depth * cols * len(plan), 2 * MIB),
        name="mix_part",
    )(weights, *[near(b) for b in blocks])


def mix_out(weights, blocks, plan, half, partial_sum, earlier):
    rows, depth = blocks[0].shape
    cols = weights.shape[1]
    args = [weights, *[near(b) for b in blocks]]
    specs = [vmem()] * (1 + len(plan))
    if partial_sum is not None:
        args.append(partial_sum)
        specs.append(vmem())
    aliases = {}
    if earlier is not None:
        aliases = {len(args): 0}
        args.append(earlier)
        specs.append(pl.BlockSpec(memory_space=pl.ANY))
    return pl.pallas_call(
        partial(mix_kernel, plan),
        out_shape=jax.ShapeDtypeStruct((2 * rows, cols), BF16),
        grid=(1,),
        in_specs=specs,
        out_specs=pl.BlockSpec((rows, cols), lambda i: (half, 0)),
        input_output_aliases=aliases,
        compiler_params=params(),
        cost_estimate=cost(2 * rows * depth * cols * len(plan), 2 * MIB),
        name="mix",
    )(*args)


def merge_kernel(span, radix, rows, end, decay, *refs):
    others, earlier, (state_ref, end_ref) = refs[: radix - 1], refs[radix - 1 : -2], refs[-2:]
    place = lax.axis_index("seq")
    mine = lax.rem(lax.div(place, span), radix)
    inner = rows * lax.rem(place, span)
    unit = rows * span
    rate = decay[...]

    def faded(count):
        return jnp.exp(-rate * jnp.full(rate.shape, count).astype(F32))

    state = earlier[0][...] if earlier else jnp.zeros(rate.shape, F32)
    total = faded(unit * (radix - 1 - mine)) * end[...]
    for step, other in enumerate(others, 1):
        theirs = lax.rem(mine + step, radix)
        value = other[...]
        ahead = jnp.full(rate.shape, mine - theirs) > 0
        state += jnp.where(ahead, faded(jnp.maximum(unit * (mine - theirs - 1), 0) + inner) * value, 0.0)
        total += faded(unit * (radix - 1 - theirs)) * value
    state_ref[...] = state
    end_ref[...] = total


def carry_in(end, decay, rows, work):
    devices = lax.axis_size("seq")
    shape = pltpu.VMEM(end.shape, F32)
    state, results, span = (), [], 1
    for radix in (2, 4, 4):
        others = []
        for step in range(1, radix):
            route = []
            for i in range(devices):
                inside = i // span % radix
                route.append((i + ((inside + step) % radix - inside) * span, i))
            others.append(near(lax.ppermute(end, "seq", route)))
        made = [work(len(results) + j, end) for j in range(2)] if span > 1 else []
        now, after = call(
            partial(merge_kernel, span, radix, rows),
            "merge",
            (shape, shape),
            (end, decay, *others, *state),
            16 * end.size,
            MIB,
        )
        if made and span * radix < devices:
            after, made = lax.optimization_barrier((after, made))
        results += made
        end, state = after, (now,)
        span *= radix
    return state[0], results


def call(kernel, name, out_shape, args, work, nbytes, scratch=()):
    specs = [vmem() for _ in args]
    return pl.pallas_call(
        kernel,
        out_shape=out_shape,
        in_specs=specs,
        out_specs=jax.tree.map(lambda _: vmem(), out_shape),
        scratch_shapes=list(scratch),
        compiler_params=params(),
        cost_estimate=cost(work, nbytes),
        name=name,
    )(*args)


def shards(tokens, w_in, short_filter, decay, residue, skip, w_out):
    rows = tokens.shape[0]
    channels = skip.shape[0]
    modes = decay.shape[0]
    half = rows // 2
    tiles = channels // LANES
    weights = near(jnp.transpose(w_in, (1, 0, 2)))
    streams, depth, _ = weights.shape
    taps, decay, residue = near(short_filter), near(decay), near(residue)
    skip = near(skip.reshape(1, channels))
    full = 2 * half * depth * streams * channels
    sums = (streams, half, channels)

    def own(low, high):
        return call(
            own_kernel,
            "own",
            (pltpu.VMEM(sums, F32), pltpu.VMEM(sums, F32)),
            (near(low), near(high), weights),
            full // 2,
            8 * MIB,
        )

    low_tok, high_tok, (low_own, high_own) = ring(tokens[:half], tokens[half:], own)
    low_tok, high_tok = [near(b) for b in low_tok], [near(b) for b in high_tok]
    high = call(
        high_kernel,
        "high",
        pltpu.VMEM(sums, BF16),
        (high_own, *high_tok[1:], weights),
        3 * full // 4,
        8 * MIB,
    )
    low_part = call(
        near_kernel,
        "near",
        pltpu.VMEM(sums, F32),
        (low_own, *low_tok[1:3], weights),
        full // 2,
        8 * MIB,
    )
    count = lax.axis_size("seq")
    halo = near(
        lax.ppermute(high[:, half - 16 :], "seq", [(i, i + 1) for i in range(count - 1)])
    )
    state_shape = pltpu.VMEM((modes, channels), F32)
    sub_shape = pltpu.VMEM((modes, SUB, channels), F32)
    high_sig, high_sub, late_end = call(
        late_kernel,
        "late",
        (pltpu.VMEM((tiles, half, LANES), F32), sub_shape, state_shape),
        (high, taps, decay),
        2 * half * channels * modes,
        3 * MIB,
        [pltpu.VMEM((2, half + SUB, channels), F32)],
    )
    low_sig, low_sub, mid, end = call(
        early_kernel,
        "early",
        (pltpu.VMEM((tiles, half + SUB, LANES), F32), sub_shape, state_shape, state_shape),
        (low_part, low_tok[3], weights, high, halo, taps, decay, late_end),
        full // 4,
        6 * MIB,
        [pltpu.VMEM((2, half + 2 * SUB, channels), F32)],
    )

    def work(tile, gate):
        sig, _ = lax.optimization_barrier((low_sig, gate))
        return call(
            partial(local_kernel, tile),
            "local",
            (pltpu.VMEM((rows, LANES), F32), pltpu.VMEM((rows, LANES), F32)),
            (
                low_part,
                low_tok[3],
                weights,
                high,
                halo,
                taps,
                decay,
                residue,
                skip,
                sig,
                low_sub,
                mid,
                high_sig,
                high_sub,
            ),
            8 * rows * channels * modes,
            4 * MIB,
            [pltpu.VMEM((1, rows + SUB, LANES), F32)],
        )

    state, local = carry_in(end, decay, rows, work)
    gates = [
        call(
            partial(gate_kernel, base),
            "gate",
            pltpu.VMEM((half, channels), BF16),
            (*[q for q, _ in local], *[p for _, p in local], state, decay, residue),
            half * channels * modes,
            2 * MIB,
        )
        for base in (0, half)
    ]
    low_gate, high_gate, _ = ring(*gates)
    w_out = near(w_out)
    out = mix_out(w_out, low_gate, (0, 3, 1, 2), 0, None, None)
    total = mix(w_out, high_gate[:3], (0, 3, 1))
    return mix_out(w_out, high_gate[3:], (2,), 1, total, out)


def solution(mesh):
    in_specs = (
        P("seq", "ch"),
        P(None, None, "ch"),
        P(None, None, "ch"),
        P(None, "ch"),
        P(None, "ch"),
        P("ch"),
        P(None, "ch"),
    )
    return jax.shard_map(
        shards, mesh=mesh, in_specs=in_specs, out_specs=P("seq", "ch"), check_vma=False
    )
```

time: 86 us -> 72.1 us (0.84)
  waiting for transfers between devices: 26.1 us -> 18.5 us
  local copies, waits for them, and re-layouts: 8.12 us -> 3.88 us
  starting transfers between devices: 35.1 us -> 32.2 us
  Pallas kernels: 16.1 us -> 17.1 us
    ppermute x5 -> x7, waiting for transfers between devices: 7.87 us -> 1.55 us  [carry_in(): others.append(near(lax.ppermute(end, 'seq', route)))]
    unnamed x22 -> x14, local copies, waits for them, and re-layouts: 7.05 us -> 2.81 us
    ppermute x5 -> x7, starting transfers between devices: 14.4 us -> 12.7 us  [carry_in(): others.append(near(lax.ppermute(end, 'seq', route)))]
    ppermute x12, waiting for transfers between devices: 18.2 us -> 16.9 us  [turn(): lax.ppermute(block, 'ch', [(i, (i + distance) % count) for i in range(cou...]
    ppermute x12, starting transfers between devices: 19.3 us -> 18.2 us  [turn(): lax.ppermute(block, 'ch', [(i, (i + distance) % count) for i in range(cou...]
    pallas_call x7 -> x17, Pallas kernels: 16.1 us -> 17.1 us  [the longest x14 14.1 us: call(): pl.pallas_call(kernel, out_shape=out_shape, in_specs=specs, out_specs=jax...]
  transfers between devices with their start and end apart: 18 -> 20, of which waited for: 10 -> 13; matrix products, arithmetic and copies ran while one was open for 0% -> 0% of each run, Pallas kernels for 12% -> 18%
where the time goes in v1:
time: 72.1 us; the launch traced here: 71.8 us
  starting transfers between devices  32.2 us (45%)
  waiting for transfers between devices  18.5 us (26%)
  Pallas kernels  17.1 us (24%)
  local copies, waits for them, and re-layouts  3.88 us (5%)
    ppermute x12, starting transfers between devices, turn(): lax.ppermute(block, 'ch', [(i, (i + distance) % count) for i in range(cou...  18.2 us
    ppermute x12, waiting for transfers between devices, turn(): lax.ppermute(block, 'ch', [(i, (i + distance) % count) for i in range(cou...  16.9 us
    pallas_call x14, Pallas kernels, call(): pl.pallas_call(kernel, out_shape=out_shape, in_specs=specs, out_specs=jax...  14.1 us
    ppermute x7, starting transfers between devices, carry_in(): others.append(near(lax.ppermute(end, 'seq', route)))  12.7 us
    unnamed x14, local copies, waits for them, and re-layouts  2.81 us
    pallas_call x2, Pallas kernels, mix_out(): pl.pallas_call(partial(mix_kernel, plan), out_shape=jax.ShapeDtypeStruct(...  2.42 us
    ppermute x7, waiting for transfers between devices, carry_in(): others.append(near(lax.ppermute(end, 'seq', route)))  1.55 us
  transfers between devices with their start and end apart: 20, of which 13 were waited for; matrix products, arithmetic and copies ran while one was open for 0% of the time, Pallas kernels for 18%

profile of v1, /device:TPU:0, one launch (start us, length us, event | category | flops | bytes accessed | tf_op | source)
XLA Modules:
  0.0 71.8 jit_solution(12463174660177086438)
XLA Ops:
  0.0 1.1 %fusion = (bf16[256,512]{1,0:T(8,128)(2,1)S(1)}, bf16[256,512]{1,0:T(8,128)(2,1)S(1)}) fusion(bf16[512,512]{1,0:T(8,128)(2,1)} %param.7), kind=kLoop, calls=%fused_computation | loop fusion | bytes 1048576 | tf_op jit(solution)/shard_map/slice | solution.py:431
  1.1 3.2 %collective-permute-start = (bf16[256,512]{1,0:T(8,128)(2,1)S(1)}, bf16[256,512]{1,0:T(8,128)(2,1)S(1)}, u32[]{:S(2)}, u32[]{:S(2)}) collective-permute-start(bf16[256,512]{1,0:T(8,128)(2,1)S(1)} %get-tuple-element.69.high), channel_id=1, source_target_pairs={{0,3},{1,0},{2,1},{3,2},{4,7},{5,4},{6,5},{7,6},{8,11},{9,8},{10,9... | collective-permute-start | bytes 786440 | tf_op jit(solution)/shard_map/ppermute | solution.py:35
  4.2 0.0 collective-permute-start.4
  4.2 0.6 collective-permute-start.1
  4.8 2.8 %copy-done = bf16[2048,3,512]{2,0,1:T(8,128)(2,1)S(1)} copy-done((bf16[2048,3,512]{2,0,1:T(8,128)(2,1)S(1)}, bf16[2048,3,512]{2,0,1:T(8,128)(2,1)}, u32[]{:S(2)}) %copy-start) | copy-done | bytes 6291480
  7.6 1.0 %own.1 = (f32[3,256,512]{2,1,0:T(8,128)S(1)}, f32[3,256,512]{2,1,0:T(8,128)S(1)}) custom-call(bf16[256,512]{1,0:T(8,128)(2,1)S(1)} %get-tuple-element.70.low, bf16[256,512]{1,0:T(8,128)(2,1)S(1)} %get-tuple-element.69.high, bf16[3,2048,512]{2,1,0:T(8,128)(2,1)S(1)} %bitcast.2), custom_call_target="tpu_custom_call" | custom-call | flops 805306368 | bytes 8388608 | tf_op jit(solution)/shard_map/own/pallas_call | solution.py:396
  8.6 1.2 %collective-permute-done.right = bf16[256,512]{1,0:T(8,128)(2,1)S(1)} collective-permute-done((bf16[256,512]{1,0:T(8,128)(2,1)S(1)}, bf16[256,512]{1,0:T(8,128)(2,1)S(1)}, u32[]{:S(2)}, u32[]{:S(2)}) %collective-permute-start) | collective-permute-done | bytes 262176 | tf_op jit(solution)/shard_map/ppermute | solution.py:35
  9.8 3.7 %collective-permute-start.5 = (bf16[256,512]{1,0:T(8,128)(2,1)S(1)}, bf16[256,512]{1,0:T(8,128)(2,1)S(1)}, u32[]{:S(2)}, u32[]{:S(2)}) collective-permute-start(bf16[256,512]{1,0:T(8,128)(2,1)S(1)} %collective-permute-done.right), channel_id=1, source_target_pairs={{0,3},{1,0},{2,1},{3,2},{4,7},{5,4},{6,5},{7,6},{8,11},{9,8},{10,9... | collective-permute-start | bytes 786440 | tf_op jit(solution)/shard_map/ppermute | solution.py:35
  13.5 0.0 collective-permute-start.2
  13.5 5.3 %collective-permute-done.1.left = bf16[256,512]{1,0:T(8,128)(2,1)S(1)} collective-permute-done((bf16[256,512]{1,0:T(8,128)(2,1)S(1)}, bf16[256,512]{1,0:T(8,128)(2,1)S(1)}, u32[]{:S(2)}, u32[]{:S(2)}) %collective-permute-start.1) | collective-permute-done | bytes 262176 | tf_op jit(solution)/shard_map/ppermute | solution.py:35
  18.8 0.0 collective-permute-start.3
  18.8 0.0 collective-permute-done.4.left
  18.8 1.4 %collective-permute-done.5.far = bf16[256,512]{1,0:T(8,128)(2,1)S(1)} collective-permute-done((bf16[256,512]{1,0:T(8,128)(2,1)S(1)}, bf16[256,512]{1,0:T(8,128)(2,1)S(1)}, u32[]{:S(2)}, u32[]{:S(2)}) %collective-permute-start.5) | collective-permute-done | bytes 262176 | tf_op jit(solution)/shard_map/ppermute | solution.py:35
  20.3 0.0 copy-done.1
  20.3 1.4 %high.1 = bf16[3,256,512]{2,1,0:T(8,128)(2,1)S(1)} custom-call(f32[3,256,512]{2,1,0:T(8,128)S(1)} %get-tuple-element.40.part, bf16[256,512]{1,0:T(8,128)(2,1)S(1)} %collective-permute-done.4.left, bf16[256,512]{1,0:T(8,128)(2,1)S(1)} %collective-permute-done.right, bf16[256,512]{1,0:T(8,128)(2,1)S(1)} %collective-permute-done.5.far, ...), custom_call_target="tpu_custom_call" | custom-call | flops 1207959552 | bytes 8388608 | tf_op jit(solution)/shard_map/high/pallas_call | solution.py:396
  21.7 0.0 copy-start.3
  21.7 0.0 copy-start.5
  21.7 1.3 %collective-permute-start.6 = (bf16[3,16,512]{2,1,0:T(8,128)(2,1)S(1)}, bf16[3,16,512]{2,1,0:T(8,128)(2,1)S(1)}, u32[]{:S(2)}, u32[]{:S(2)}) collective-permute-start(bf16[3,16,512]{2,1,0:T(8,128)(2,1)S(1)} %slice.12), channel_id=1, source_target_pairs={{0,4},{4,8},{8,12},{12,16},{16,20},{20,24},{24,28},{28,32},{32,36}... | collective-permute-start | bytes 147464 | tf_op jit(solution)/shard_map/ppermute | solution.py:451
  23.0 0.8 %collective-permute-done.2.right = bf16[256,512]{1,0:T(8,128)(2,1)S(1)} collective-permute-done((bf16[256,512]{1,0:T(8,128)(2,1)S(1)}, bf16[256,512]{1,0:T(8,128)(2,1)S(1)}, u32[]{:S(2)}, u32[]{:S(2)}) %collective-permute-start.2) | collective-permute-done | bytes 262176 | tf_op jit(solution)/shard_map/ppermute | solution.py:35
  23.8 1.0 %near.1.part = f32[3,256,512]{2,1,0:T(8,128)S(1)} custom-call(f32[3,256,512]{2,1,0:T(8,128)S(1)} %get-tuple-element.39.part, bf16[256,512]{1,0:T(8,128)(2,1)S(1)} %collective-permute-done.1.left, bf16[256,512]{1,0:T(8,128)(2,1)S(1)} %collective-permute-done.2.right, bf16[3,2048,512]{2,1,0:T(8,128)(2,1)S(1)} %bitcast.4), custom_call_target="tpu_custom_call" | custom-call | flops 805306368 | bytes 8388608 | tf_op jit(solution)/shard_map/near/pallas_call | solution.py:396
  24.8 0.0 copy-done.3
  24.8 1.4 %late.1 = (f32[4,256,128]{2,1,0:T(8,128)S(1)}, f32[16,8,512]{2,1,0:T(8,128)S(1)}, f32[16,512]{1,0:T(8,128)S(1)}) custom-call(bf16[3,256,512]{2,1,0:T(8,128)(2,1)S(1)} %high.1, f32[3,3,512]{2,1,0:T(4,128)S(1)} %copy-done.5, f32[16,512]{1,0:T(8,128)S(1)} %copy-done.3), custom_call_target="tpu_custom_call" | custom-call | flops 4194304 | bytes 3145728 | tf_op jit(solution)/shard_map/late/pallas_call | solution.py:396
  26.2 0.7 collective-permute-done.3.far
  26.9 0.0 collective-permute-done.6.halo
  26.9 1.7 %early.1 = (f32[4,264,128]{2,1,0:T(8,128)S(1)}, f32[16,8,512]{2,1,0:T(8,128)S(1)}, f32[16,512]{1,0:T(8,128)S(1)}, f32[16,512]{1,0:T(8,128)S(1)}) custom-call(f32[3,256,512]{2,1,0:T(8,128)S(1)} %near.1.part, bf16[256,512]{1,0:T(8,128)(2,1)S(1)} %collective-permute-done.3.far, bf16[3,2048,512]{2,1,0:T(8,128)(2,1)S(1)} %bitcast.5, ...), custom_call_target="tpu_custom_call" | custom-call | flops 402653184 | bytes 6291456 | tf_op jit(solution)/shard_map/early/pallas_call | solution.py:396
  28.6 0.8 %collective-permute-start.7 = (f32[16,512]{1,0:T(8,128)S(1)}, f32[16,512]{1,0:T(8,128)S(1)}, u32[]{:S(2)}, u32[]{:S(2)}) collective-permute-start(f32[16,512]{1,0:T(8,128)S(1)} %get-tuple-element.43.end), channel_id=1, source_target_pairs={{4,0},{0,4},{12,8},{8,12},{20,16},{16,20},{28,24},{24,28},{36,32},... | collective-permute-start | bytes 98312 | tf_op jit(solution)/shard_map/ppermute | solution.py:376
  29.5 0.9 %collective-permute-done.7.refs_0_ = f32[16,512]{1,0:T(8,128)S(1)} collective-permute-done((f32[16,512]{1,0:T(8,128)S(1)}, f32[16,512]{1,0:T(8,128)S(1)}, u32[]{:S(2)}, u32[]{:S(2)}) %collective-permute-start.7) | collective-permute-done | bytes 32800 | tf_op jit(solution)/shard_map/ppermute | solution.py:376
  30.4 1.6 %collective-permute-start.10 = (f32[16,512]{1,0:T(8,128)S(1)}, f32[16,512]{1,0:T(8,128)S(1)}, u32[]{:S(2)}, u32[]{:S(2)}) collective-permute-start(f32[16,512]{1,0:T(8,128)S(1)} %get-tuple-element.44.end), channel_id=1, source_target_pairs={{24,0},{28,4},{0,8},{4,12},{8,16},{12,20},{16,24},{20,28},{56,32},... | collective-permute-start | bytes 98312 | tf_op jit(solution)/shard_map/ppermute | solution.py:376
  31.9 3.1 %collective-permute-start.9 = (f32[16,512]{1,0:T(8,128)S(1)}, f32[16,512]{1,0:T(8,128)S(1)}, u32[]{:S(2)}, u32[]{:S(2)}) collective-permute-start(f32[16,512]{1,0:T(8,128)S(1)} %get-tuple-element.44.end), channel_id=1, source_target_pairs={{16,0},{20,4},{24,8},{28,12},{0,16},{4,20},{8,24},{12,28},{48,32},... | collective-permute-start | bytes 98312 | tf_op jit(solution)/shard_map/ppermute | solution.py:376
  35.0 0.9 %collective-permute-start.8 = (f32[16,512]{1,0:T(8,128)S(1)}, f32[16,512]{1,0:T(8,128)S(1)}, u32[]{:S(2)}, u32[]{:S(2)}) collective-permute-start(f32[16,512]{1,0:T(8,128)S(1)} %get-tuple-element.44.end), channel_id=1, source_target_pairs={{8,0},{12,4},{16,8},{20,12},{24,16},{28,20},{0,24},{4,28},{40,32},... | collective-permute-start | bytes 98312 | tf_op jit(solution)/shard_map/ppermute | solution.py:376
  35.9 0.0 copy-done.4
  35.9 1.3 %local.5 = (f32[512,128]{1,0:T(8,128)S(1)}, f32[512,128]{1,0:T(8,128)S(1)}) custom-call(f32[3,256,512]{2,1,0:T(8,128)S(1)} %near.1.part, bf16[256,512]{1,0:T(8,128)(2,1)S(1)} %collective-permute-done.3.far, bf16[3,2048,512]{2,1,0:T(8,128)(2,1)S(1)} %bitcast.6, bf16[3,256,512]{2,1,0:T(8,128)(2,1)S(1)} %high.1, ...), custom_call_target="tpu_custom_call" | custom-call | flops 33554432 | bytes 4194304 | tf_op jit(solution)/shard_map/local/pallas_call | solution.py:396
  37.2 1.3 %local.4 = (f32[512,128]{1,0:T(8,128)S(1)}, f32[512,128]{1,0:T(8,128)S(1)}) custom-call(f32[3,256,512]{2,1,0:T(8,128)S(1)} %near.1.part, bf16[256,512]{1,0:T(8,128)(2,1)S(1)} %collective-permute-done.3.far, bf16[3,2048,512]{2,1,0:T(8,128)(2,1)S(1)} %bitcast.7, bf16[3,256,512]{2,1,0:T(8,128)(2,1)S(1)} %high.1, ...), custom_call_target="tpu_custom_call" | custom-call | flops 33554432 | bytes 4194304 | tf_op jit(solution)/shard_map/local/pallas_call | solution.py:396
  38.5 0.0 collective-permute-done.10.refs_2_
  38.5 0.0 collective-permute-done.9.refs_1_
  38.5 0.4 collective-permute-done.8.refs_0_
  38.9 0.1 merge.4
  39.0 2.0 %collective-permute-start.13 = (f32[16,512]{1,0:T(8,128)S(1)}, f32[16,512]{1,0:T(8,128)S(1)}, u32[]{:S(2)}, u32[]{:S(2)}) collective-permute-start(f32[16,512]{1,0:T(8,128)S(1)} %get-tuple-element.59.end), channel_id=1, source_target_pairs={{96,0},{100,4},{104,8},{108,12},{112,16},{116,20},{120,24},{124,28... | collective-permute-start | bytes 98312 | tf_op jit(solution)/shard_map/ppermute | solution.py:376
  41.0 3.3 %collective-permute-start.12 = (f32[16,512]{1,0:T(8,128)S(1)}, f32[16,512]{1,0:T(8,128)S(1)}, u32[]{:S(2)}, u32[]{:S(2)}) collective-permute-start(f32[16,512]{1,0:T(8,128)S(1)} %get-tuple-element.59.end), channel_id=1, source_target_pairs={{64,0},{68,4},{72,8},{76,12},{80,16},{84,20},{88,24},{92,28},{96,3... | collective-permute-start | bytes 98312 | tf_op jit(solution)/shard_map/ppermute | solution.py:376
  44.3 1.0 %collective-permute-start.11 = (f32[16,512]{1,0:T(8,128)S(1)}, f32[16,512]{1,0:T(8,128)S(1)}, u32[]{:S(2)}, u32[]{:S(2)}) collective-permute-start(f32[16,512]{1,0:T(8,128)S(1)} %get-tuple-element.59.end), channel_id=1, source_target_pairs={{32,0},{36,4},{40,8},{44,12},{48,16},{52,20},{56,24},{60,28},{64,3... | collective-permute-start | bytes 98312 | tf_op jit(solution)/shard_map/ppermute | solution.py:376
  45.3 1.3 %local.7 = (f32[512,128]{1,0:T(8,128)S(1)}, f32[512,128]{1,0:T(8,128)S(1)}) custom-call(f32[3,256,512]{2,1,0:T(8,128)S(1)} %near.1.part, bf16[256,512]{1,0:T(8,128)(2,1)S(1)} %collective-permute-done.3.far, bf16[3,2048,512]{2,1,0:T(8,128)(2,1)S(1)} %bitcast.8, bf16[3,256,512]{2,1,0:T(8,128)(2,1)S(1)} %high.1, ...), custom_call_target="tpu_custom_call" | custom-call | flops 33554432 | bytes 4194304 | tf_op jit(solution)/shard_map/local/pallas_call | solution.py:396
  46.6 1.3 %local.6 = (f32[512,128]{1,0:T(8,128)S(1)}, f32[512,128]{1,0:T(8,128)S(1)}) custom-call(f32[3,256,512]{2,1,0:T(8,128)S(1)} %near.1.part, bf16[256,512]{1,0:T(8,128)(2,1)S(1)} %collective-permute-done.3.far, bf16[3,2048,512]{2,1,0:T(8,128)(2,1)S(1)} %bitcast.9, bf16[3,256,512]{2,1,0:T(8,128)(2,1)S(1)} %high.1, ...), custom_call_target="tpu_custom_call" | custom-call | flops 33554432 | bytes 4194304 | tf_op jit(solution)/shard_map/local/pallas_call | solution.py:396
  47.9 0.0 collective-permute-done.13.refs_2_
  47.9 0.0 collective-permute-done.12.refs_1_
  47.9 0.3 collective-permute-done.11.refs_0_
  48.2 0.6 merge.5
  48.9 0.8 %gate.3.refs_0_ = bf16[256,512]{1,0:T(8,128)(2,1)S(1)} custom-call(f32[512,128]{1,0:T(8,128)S(1)} %get-tuple-element.57.refs_0_, f32[512,128]{1,0:T(8,128)S(1)} %get-tuple-element.58.refs_1_, f32[512,128]{1,0:T(8,128)S(1)} %get-tuple-element.61.refs_2_, f32[512,128]{1,0:T(8,128)S(1)} %get-tuple-element.62.refs_3_, f32[512,128]{1,0:T(8,128)S(1)} %get-tuple-element.63.refs_4_, ...), custom_call_target="tpu_custom_call" | custom-call | flops 2097152 | bytes 2097152 | tf_op jit(solution)/shard_map/gate/pallas_call | solution.py:396
  49.7 0.0 copy-start.2
  49.7 0.1 collective-permute-start.17
  49.8 0.9 %gate.2.refs_0_ = bf16[256,512]{1,0:T(8,128)(2,1)S(1)} custom-call(f32[512,128]{1,0:T(8,128)S(1)} %get-tuple-element.57.refs_0_, f32[512,128]{1,0:T(8,128)S(1)} %get-tuple-element.58.refs_1_, f32[512,128]{1,0:T(8,128)S(1)} %get-tuple-element.61.refs_2_, f32[512,128]{1,0:T(8,128)S(1)} %get-tuple-element.62.refs_3_, f32[512,128]{1,0:T(8,128)S(1)} %get-tuple-element.63.refs_4_, ...), custom_call_target="tpu_custom_call" | custom-call | flops 2097152 | bytes 2097152 | tf_op jit(solution)/shard_map/gate/pallas_call | solution.py:396
  50.7 3.8 %collective-permute-start.14 = (bf16[256,512]{1,0:T(8,128)(2,1)S(1)}, bf16[256,512]{1,0:T(8,128)(2,1)S(1)}, u32[]{:S(2)}, u32[]{:S(2)}) collective-permute-start(bf16[256,512]{1,0:T(8,128)(2,1)S(1)} %gate.2.refs_0_), channel_id=1, source_target_pairs={{0,3},{1,0},{2,1},{3,2},{4,7},{5,4},{6,5},{7,6},{8,11},{9,8},{10,9... | collective-permute-start | bytes 786440 | tf_op jit(solution)/shard_map/ppermute | solution.py:35
  54.4 0.0 collective-permute-start.16
  54.4 3.2 %collective-permute-start.18 = (bf16[256,512]{1,0:T(8,128)(2,1)S(1)}, bf16[256,512]{1,0:T(8,128)(2,1)S(1)}, u32[]{:S(2)}, u32[]{:S(2)}) collective-permute-start(bf16[256,512]{1,0:T(8,128)(2,1)S(1)} %gate.3.refs_0_), channel_id=1, source_target_pairs={{0,3},{1,0},{2,1},{3,2},{4,7},{5,4},{6,5},{7,6},{8,11},{9,8},{10,9... | collective-permute-start | bytes 786440 | tf_op jit(solution)/shard_map/ppermute | solution.py:35
  57.7 2.5 %collective-permute-done.17.refs_1_ = bf16[256,512]{1,0:T(8,128)(2,1)S(1)} collective-permute-done((bf16[256,512]{1,0:T(8,128)(2,1)S(1)}, bf16[256,512]{1,0:T(8,128)(2,1)S(1)}, u32[]{:S(2)}, u32[]{:S(2)}) %collective-permute-start.17) | collective-permute-done | bytes 262176 | tf_op jit(solution)/shard_map/ppermute | solution.py:35
  60.2 0.0 collective-permute-start.19
  60.2 1.0 %collective-permute-done.14.refs_2_ = bf16[256,512]{1,0:T(8,128)(2,1)S(1)} collective-permute-done((bf16[256,512]{1,0:T(8,128)(2,1)S(1)}, bf16[256,512]{1,0:T(8,128)(2,1)S(1)}, u32[]{:S(2)}, u32[]{:S(2)}) %collective-permute-start.14) | collective-permute-done | bytes 262176 | tf_op jit(solution)/shard_map/ppermute | solution.py:35
  61.2 3.7 %collective-permute-start.15 = (bf16[256,512]{1,0:T(8,128)(2,1)S(1)}, bf16[256,512]{1,0:T(8,128)(2,1)S(1)}, u32[]{:S(2)}, u32[]{:S(2)}) collective-permute-start(bf16[256,512]{1,0:T(8,128)(2,1)S(1)} %collective-permute-done.14.refs_2_), channel_id=1, source_target_pairs={{0,3},{1,0},{2,1},{3,2},{4,7},{5,4},{6,5},{7,6},{8,11},{9,8},{10,9... | collective-permute-start | bytes 786440 | tf_op jit(solution)/shard_map/ppermute | solution.py:35
  64.9 0.9 %collective-permute-done.16.refs_1_ = bf16[256,512]{1,0:T(8,128)(2,1)S(1)} collective-permute-done((bf16[256,512]{1,0:T(8,128)(2,1)S(1)}, bf16[256,512]{1,0:T(8,128)(2,1)S(1)}, u32[]{:S(2)}, u32[]{:S(2)}) %collective-permute-start.16) | collective-permute-done | bytes 262176 | tf_op jit(solution)/shard_map/ppermute | solution.py:35
  65.8 0.6 mix_part.1.refs_1_
  66.4 0.4 collective-permute-done.18.refs_2_
  66.8 2.6 %collective-permute-done.19.refs_3_ = bf16[256,512]{1,0:T(8,128)(2,1)S(1)} collective-permute-done((bf16[256,512]{1,0:T(8,128)(2,1)S(1)}, bf16[256,512]{1,0:T(8,128)(2,1)S(1)}, u32[]{:S(2)}, u32[]{:S(2)}) %collective-permute-start.19) | collective-permute-done | bytes 262176 | tf_op jit(solution)/shard_map/ppermute | solution.py:35
  69.4 1.4 %mix.2.refs_2_ = bf16[512,512]{1,0:T(8,128)(2,1)} custom-call(bf16[2048,512]{1,0:T(8,128)(2,1)S(1)} %copy-done.2, bf16[256,512]{1,0:T(8,128)(2,1)S(1)} %gate.3.refs_0_, bf16[256,512]{1,0:T(8,128)(2,1)S(1)} %collective-permute-done.17.refs_1_, bf16[256,512]{1,0:T(8,128)(2,1)S(1)} %collective-permute-done.18.refs_2_, ...), custom_call_target="tpu_custom_call" | custom-call | flops 536870912 | bytes 2097152 | tf_op jit(solution)/shard_map/mix/pallas_call | solution.py:329
  70.8 0.0 collective-permute-done.15.refs_0_
  70.8 1.0 %mix.3 = bf16[512,512]{1,0:T(8,128)(2,1)} custom-call(bf16[2048,512]{1,0:T(8,128)(2,1)S(1)} %copy-done.2, bf16[256,512]{1,0:T(8,128)(2,1)S(1)} %collective-permute-done.15.refs_0_, f32[256,512]{1,0:T(8,128)S(1)} %mix_part.1.refs_1_, bf16[512,512]{1,0:T(8,128)(2,1)} %mix.2.refs_2_), custom_call_target="tpu_custom_call", output_to_operand_aliasing={{}: (3, {})} | custom-call | flops 134217728 | bytes 2097152 | tf_op jit(solution)/shard_map/mix/pallas_call | solution.py:329
  (9 shorter events, 0.0 us)
Async XLA Ops:
  1.1 8.7 %collective-permute-start = (bf16[256,512]{1,0:T(8,128)(2,1)S(1)}, bf16[256,512]{1,0:T(8,128)(2,1)S(1)}, u32[]{:S(2)}, u32[]{:S(2)}) collective-permute-start(bf16[256,512]{1,0:T(8,128)(2,1)S(1)} %get-tuple-element.69.high), channel_id=1, source_target_pairs={{0,3},{1,0},{2,1},{3,2},{4,7},{5,4},{6,5},{7,6},{8,11},{9,8},{10,9... | collective-permute-start | bytes 786440 | tf_op jit(solution)/shard_map/ppermute | solution.py:35
  4.2 14.6 %collective-permute-start.4 = (bf16[256,512]{1,0:T(8,128)(2,1)S(1)}, bf16[256,512]{1,0:T(8,128)(2,1)S(1)}, u32[]{:S(2)}, u32[]{:S(2)}) collective-permute-start(bf16[256,512]{1,0:T(8,128)(2,1)S(1)} %get-tuple-element.69.high), channel_id=1, source_target_pairs={{0,1},{1,2},{2,3},{3,0},{4,5},{5,6},{6,7},{7,4},{8,9},{9,10},{10,1... | collective-permute-start | bytes 786440 | tf_op jit(solution)/shard_map/ppermute | solution.py:35
  4.2 14.6 %collective-permute-start.1 = (bf16[256,512]{1,0:T(8,128)(2,1)S(1)}, bf16[256,512]{1,0:T(8,128)(2,1)S(1)}, u32[]{:S(2)}, u32[]{:S(2)}) collective-permute-start(bf16[256,512]{1,0:T(8,128)(2,1)S(1)} %get-tuple-element.70.low), channel_id=1, source_target_pairs={{0,1},{1,2},{2,3},{3,0},{4,5},{5,6},{6,7},{7,4},{8,9},{9,10},{10,1... | collective-permute-start | bytes 786440 | tf_op jit(solution)/shard_map/ppermute | solution.py:35
  4.8 2.8 %copy-start = (bf16[2048,3,512]{2,0,1:T(8,128)(2,1)S(1)}, bf16[2048,3,512]{2,0,1:T(8,128)(2,1)}, u32[]{:S(2)}) copy-start(bf16[2048,3,512]{2,0,1:T(8,128)(2,1)} %param.8) | copy-start | bytes 18874372
  7.6 12.6 %copy-start.1 = (bf16[2048,3,512]{2,0,1:T(8,128)(2,1)S(1)}, bf16[2048,3,512]{2,0,1:T(8,128)(2,1)}, u32[]{:S(2)}) copy-start(bf16[2048,3,512]{2,0,1:T(8,128)(2,1)} %param.8) | copy-start | bytes 18874372
  9.8 10.5 %collective-permute-start.5 = (bf16[256,512]{1,0:T(8,128)(2,1)S(1)}, bf16[256,512]{1,0:T(8,128)(2,1)S(1)}, u32[]{:S(2)}, u32[]{:S(2)}) collective-permute-start(bf16[256,512]{1,0:T(8,128)(2,1)S(1)} %collective-permute-done.right), channel_id=1, source_target_pairs={{0,3},{1,0},{2,1},{3,2},{4,7},{5,4},{6,5},{7,6},{8,11},{9,8},{10,9... | collective-permute-start | bytes 786440 | tf_op jit(solution)/shard_map/ppermute | solution.py:35
  13.5 10.3 %collective-permute-start.2 = (bf16[256,512]{1,0:T(8,128)(2,1)S(1)}, bf16[256,512]{1,0:T(8,128)(2,1)S(1)}, u32[]{:S(2)}, u32[]{:S(2)}) collective-permute-start(bf16[256,512]{1,0:T(8,128)(2,1)S(1)} %get-tuple-element.70.low), channel_id=1, source_target_pairs={{0,3},{1,0},{2,1},{3,2},{4,7},{5,4},{6,5},{7,6},{8,11},{9,8},{10,9... | collective-permute-start | bytes 786440 | tf_op jit(solution)/shard_map/ppermute | solution.py:35
  18.8 8.1 %collective-permute-start.3 = (bf16[256,512]{1,0:T(8,128)(2,1)S(1)}, bf16[256,512]{1,0:T(8,128)(2,1)S(1)}, u32[]{:S(2)}, u32[]{:S(2)}) collective-permute-start(bf16[256,512]{1,0:T(8,128)(2,1)S(1)} %collective-permute-done.1.left), channel_id=1, source_target_pairs={{0,1},{1,2},{2,3},{3,0},{4,5},{5,6},{6,7},{7,4},{8,9},{9,10},{10,1... | collective-permute-start | bytes 786440 | tf_op jit(solution)/shard_map/ppermute | solution.py:35
  21.7 3.1 %copy-start.3 = (f32[16,512]{1,0:T(8,128)S(1)}, f32[16,512]{1,0:T(8,128)}, u32[]{:S(2)}) copy-start(f32[16,512]{1,0:T(8,128)} %refs_9_.3) | copy-start | bytes 98308
  21.7 3.1 %copy-start.5 = (f32[3,3,512]{2,1,0:T(4,128)S(1)}, f32[3,3,512]{2,1,0:T(4,128)}, u32[]{:S(2)}) copy-start(f32[3,3,512]{2,1,0:T(4,128)} %taps.11) | copy-start | bytes 55300
  21.7 5.2 %collective-permute-start.6 = (bf16[3,16,512]{2,1,0:T(8,128)(2,1)S(1)}, bf16[3,16,512]{2,1,0:T(8,128)(2,1)S(1)}, u32[]{:S(2)}, u32[]{:S(2)}) collective-permute-start(bf16[3,16,512]{2,1,0:T(8,128)(2,1)S(1)} %slice.12), channel_id=1, source_target_pairs={{0,4},{4,8},{8,12},{12,16},{16,20},{20,24},{24,28},{28,32},{32,36}... | collective-permute-start | bytes 147464 | tf_op jit(solution)/shard_map/ppermute | solution.py:451
  26.9 9.0 %copy-start.4 = (f32[16,512]{1,0:T(8,128)S(1)}, f32[16,512]{1,0:T(8,128)}, u32[]{:S(2)}) copy-start(f32[16,512]{1,0:T(8,128)} %refs_10_.3) | copy-start | bytes 98308
  26.9 9.0 %copy-start.6 = (f32[512]{0:T(512)S(1)}, f32[512]{0:T(512)}, u32[]{:S(2)}) copy-start(f32[512]{0:T(512)} %param.12) | copy-start | bytes 6148
  28.6 1.7 %collective-permute-start.7 = (f32[16,512]{1,0:T(8,128)S(1)}, f32[16,512]{1,0:T(8,128)S(1)}, u32[]{:S(2)}, u32[]{:S(2)}) collective-permute-start(f32[16,512]{1,0:T(8,128)S(1)} %get-tuple-element.43.end), channel_id=1, source_target_pairs={{4,0},{0,4},{12,8},{8,12},{20,16},{16,20},{28,24},{24,28},{36,32},... | collective-permute-start | bytes 98312 | tf_op jit(solution)/shard_map/ppermute | solution.py:376
  30.4 8.1 %collective-permute-start.10 = (f32[16,512]{1,0:T(8,128)S(1)}, f32[16,512]{1,0:T(8,128)S(1)}, u32[]{:S(2)}, u32[]{:S(2)}) collective-permute-start(f32[16,512]{1,0:T(8,128)S(1)} %get-tuple-element.44.end), channel_id=1, source_target_pairs={{24,0},{28,4},{0,8},{4,12},{8,16},{12,20},{16,24},{20,28},{56,32},... | collective-permute-start | bytes 98312 | tf_op jit(solution)/shard_map/ppermute | solution.py:376
  31.9 6.6 %collective-permute-start.9 = (f32[16,512]{1,0:T(8,128)S(1)}, f32[16,512]{1,0:T(8,128)S(1)}, u32[]{:S(2)}, u32[]{:S(2)}) collective-permute-start(f32[16,512]{1,0:T(8,128)S(1)} %get-tuple-element.44.end), channel_id=1, source_target_pairs={{16,0},{20,4},{24,8},{28,12},{0,16},{4,20},{8,24},{12,28},{48,32},... | collective-permute-start | bytes 98312 | tf_op jit(solution)/shard_map/ppermute | solution.py:376
  35.0 3.9 %collective-permute-start.8 = (f32[16,512]{1,0:T(8,128)S(1)}, f32[16,512]{1,0:T(8,128)S(1)}, u32[]{:S(2)}, u32[]{:S(2)}) collective-permute-start(f32[16,512]{1,0:T(8,128)S(1)} %get-tuple-element.44.end), channel_id=1, source_target_pairs={{8,0},{12,4},{16,8},{20,12},{24,16},{28,20},{0,24},{4,28},{40,32},... | collective-permute-start | bytes 98312 | tf_op jit(solution)/shard_map/ppermute | solution.py:376
  39.0 8.9 %collective-permute-start.13 = (f32[16,512]{1,0:T(8,128)S(1)}, f32[16,512]{1,0:T(8,128)S(1)}, u32[]{:S(2)}, u32[]{:S(2)}) collective-permute-start(f32[16,512]{1,0:T(8,128)S(1)} %get-tuple-element.59.end), channel_id=1, source_target_pairs={{96,0},{100,4},{104,8},{108,12},{112,16},{116,20},{120,24},{124,28... | collective-permute-start | bytes 98312 | tf_op jit(solution)/shard_map/ppermute | solution.py:376
  41.0 7.0 %collective-permute-start.12 = (f32[16,512]{1,0:T(8,128)S(1)}, f32[16,512]{1,0:T(8,128)S(1)}, u32[]{:S(2)}, u32[]{:S(2)}) collective-permute-start(f32[16,512]{1,0:T(8,128)S(1)} %get-tuple-element.59.end), channel_id=1, source_target_pairs={{64,0},{68,4},{72,8},{76,12},{80,16},{84,20},{88,24},{92,28},{96,3... | collective-permute-start | bytes 98312 | tf_op jit(solution)/shard_map/ppermute | solution.py:376
  44.3 3.9 %collective-permute-start.11 = (f32[16,512]{1,0:T(8,128)S(1)}, f32[16,512]{1,0:T(8,128)S(1)}, u32[]{:S(2)}, u32[]{:S(2)}) collective-permute-start(f32[16,512]{1,0:T(8,128)S(1)} %get-tuple-element.59.end), channel_id=1, source_target_pairs={{32,0},{36,4},{40,8},{44,12},{48,16},{52,20},{56,24},{60,28},{64,3... | collective-permute-start | bytes 98312 | tf_op jit(solution)/shard_map/ppermute | solution.py:376
  49.7 16.1 %copy-start.2 = (bf16[2048,512]{1,0:T(8,128)(2,1)S(1)}, bf16[2048,512]{1,0:T(8,128)(2,1)}, u32[]{:S(2)}) copy-start(bf16[2048,512]{1,0:T(8,128)(2,1)} %w_ref.5) | copy-start | bytes 6291460
  49.7 10.4 %collective-permute-start.17 = (bf16[256,512]{1,0:T(8,128)(2,1)S(1)}, bf16[256,512]{1,0:T(8,128)(2,1)S(1)}, u32[]{:S(2)}, u32[]{:S(2)}) collective-permute-start(bf16[256,512]{1,0:T(8,128)(2,1)S(1)} %gate.3.refs_0_), channel_id=1, source_target_pairs={{0,1},{1,2},{2,3},{3,0},{4,5},{5,6},{6,7},{7,4},{8,9},{9,10},{10,1... | collective-permute-start | bytes 786440 | tf_op jit(solution)/shard_map/ppermute | solution.py:35
  50.7 10.5 %collective-permute-start.14 = (bf16[256,512]{1,0:T(8,128)(2,1)S(1)}, bf16[256,512]{1,0:T(8,128)(2,1)S(1)}, u32[]{:S(2)}, u32[]{:S(2)}) collective-permute-start(bf16[256,512]{1,0:T(8,128)(2,1)S(1)} %gate.2.refs_0_), channel_id=1, source_target_pairs={{0,3},{1,0},{2,1},{3,2},{4,7},{5,4},{6,5},{7,6},{8,11},{9,8},{10,9... | collective-permute-start | bytes 786440 | tf_op jit(solution)/shard_map/ppermute | solution.py:35
  54.4 11.4 %collective-permute-start.16 = (bf16[256,512]{1,0:T(8,128)(2,1)S(1)}, bf16[256,512]{1,0:T(8,128)(2,1)S(1)}, u32[]{:S(2)}, u32[]{:S(2)}) collective-permute-start(bf16[256,512]{1,0:T(8,128)(2,1)S(1)} %gate.2.refs_0_), channel_id=1, source_target_pairs={{0,1},{1,2},{2,3},{3,0},{4,5},{5,6},{6,7},{7,4},{8,9},{9,10},{10,1... | collective-permute-start | bytes 786440 | tf_op jit(solution)/shard_map/ppermute | solution.py:35
  54.4 12.4 %collective-permute-start.18 = (bf16[256,512]{1,0:T(8,128)(2,1)S(1)}, bf16[256,512]{1,0:T(8,128)(2,1)S(1)}, u32[]{:S(2)}, u32[]{:S(2)}) collective-permute-start(bf16[256,512]{1,0:T(8,128)(2,1)S(1)} %gate.3.refs_0_), channel_id=1, source_target_pairs={{0,3},{1,0},{2,1},{3,2},{4,7},{5,4},{6,5},{7,6},{8,11},{9,8},{10,9... | collective-permute-start | bytes 786440 | tf_op jit(solution)/shard_map/ppermute | solution.py:35
  60.2 9.2 %collective-permute-start.19 = (bf16[256,512]{1,0:T(8,128)(2,1)S(1)}, bf16[256,512]{1,0:T(8,128)(2,1)S(1)}, u32[]{:S(2)}, u32[]{:S(2)}) collective-permute-start(bf16[256,512]{1,0:T(8,128)(2,1)S(1)} %collective-permute-done.17.refs_1_), channel_id=1, source_target_pairs={{0,1},{1,2},{2,3},{3,0},{4,5},{5,6},{6,7},{7,4},{8,9},{9,10},{10,1... | collective-permute-start | bytes 786440 | tf_op jit(solution)/shard_map/ppermute | solution.py:35
  61.2 9.6 %collective-permute-start.15 = (bf16[256,512]{1,0:T(8,128)(2,1)S(1)}, bf16[256,512]{1,0:T(8,128)(2,1)S(1)}, u32[]{:S(2)}, u32[]{:S(2)}) collective-permute-start(bf16[256,512]{1,0:T(8,128)(2,1)S(1)} %collective-permute-done.14.refs_2_), channel_id=1, source_target_pairs={{0,3},{1,0},{2,1},{3,2},{4,7},{5,4},{6,5},{7,6},{8,11},{9,8},{10,9... | collective-permute-start | bytes 786440 | tf_op jit(solution)/shard_map/ppermute | solution.py:35

commit v2 on v1

v2 whole, which is shorter than its diff:
```python
from functools import partial

import jax
import jax.numpy as jnp
from jax import lax
from jax.experimental import pallas as pl
from jax.experimental.pallas import tpu as pltpu
from jax.sharding import PartitionSpec as P

LANES = 128
SUB = 8
F32 = jnp.float32
BF16 = jnp.bfloat16
MIB = 1 << 20


def vmem():
    return pl.BlockSpec(memory_space=pltpu.VMEM)


def near(x):
    return pltpu.with_memory_space_constraint(x, pltpu.VMEM)


def params(mib=24):
    return pltpu.CompilerParams(vmem_limit_bytes=mib * MIB)


def cost(flops, nbytes, exps=0):
    return pl.CostEstimate(flops=flops, bytes_accessed=nbytes, transcendentals=exps)


def swap(block, flip):
    return lax.ppermute(block, "ch", [(i, i ^ flip) for i in range(lax.axis_size("ch"))])


def gather(low, high, work):
    low_three, high_one = swap(low, 3), swap(high, 1)
    done, low, high = lax.optimization_barrier((work(low, high), low, high))
    high_three, low_one = swap(high, 3), swap(low, 1)
    low_two, high_two = swap(low_three, 1), swap(high_one, 3)
    return (low, low_three, low_one, low_two), (high, high_three, high_one, high_two), done


def source(step, depth):
    owner = lax.bitwise_xor(lax.axis_index("ch"), step)
    return pl.ds(pl.multiple_of(owner * depth, depth), depth)


def own_kernel(block, w_ref, out_ref):
    depth = block.shape[1]
    for stream in range(w_ref.shape[0]):
        part = w_ref[stream, source(0, depth), :]
        out_ref[stream] = jnp.dot(block[...], part, preferred_element_type=F32)


def near_kernel(low_part, high_part, low_left, low_right, high_left, high_right, w_ref, low_ref, high_ref):
    depth = low_left.shape[1]
    for stream in range(w_ref.shape[0]):
        left = w_ref[stream, source(3, depth), :]
        right = w_ref[stream, source(1, depth), :]
        low_ref[stream] = (
            low_part[stream]
            + jnp.dot(low_left[...], left, preferred_element_type=F32)
            + jnp.dot(low_right[...], right, preferred_element_type=F32)
        )
        high_ref[stream] = (
            high_part[stream]
            + jnp.dot(high_left[...], left, preferred_element_type=F32)
            + jnp.dot(high_right[...], right, preferred_element_type=F32)
        )


def far_kernel(low_part, high_part, low_far, high_far, w_ref, out_ref):
    half, depth = low_far.shape
    for stream in range(w_ref.shape[0]):
        weights = w_ref[stream, source(2, depth), :]
        for base, part, far in ((0, low_part, low_far), (half, high_part, high_far)):
            total = part[stream] + jnp.dot(far[...], weights, preferred_element_type=F32)
            out_ref[stream, pl.ds(base, half), :] = total.astype(BF16)


def filtered(ext, slot, taps, stream, at, size, lanes, width):
    total = taps[stream, 0:1, lanes] * ext[slot, pl.ds(at + SUB, size), width]
    for lag in range(1, 3):
        total += taps[stream, lag : lag + 1, lanes] * ext[slot, pl.ds(at + SUB - lag, size), width]
    return total


def tile_of(tile):
    return slice(tile * LANES, (tile + 1) * LANES)


def spread(ref, row, lanes):
    return jnp.broadcast_to(ref[row : row + 1, lanes], (SUB, LANES))


def tree(terms):
    while len(terms) > 1:
        terms = [sum(terms[j : j + 2]) for j in range(0, len(terms), 2)]
    return terms[0]


def prepare_kernel(decay, residue, fade_ref, remain_ref, stride_ref, lead_ref, *, steps):
    rate = decay[...]
    fade_ref[...] = jnp.exp(-rate)
    stride_ref[...] = jnp.exp(-float(SUB) * rate)
    place = lax.broadcasted_iota(jnp.int32, (SUB, rate.shape[1]), 0)
    later = (SUB - 1 - place).astype(F32) * steps
    ahead = (1 + place).astype(F32)
    for m in range(rate.shape[0]):
        one = jnp.broadcast_to(decay[m : m + 1, :], place.shape)
        remain_ref[m] = jnp.exp(-one * later)
        lead_ref[m] = residue[m : m + 1, :] * jnp.sqrt(one) * jnp.exp(-one * ahead)


def early_kernel(proj, taps, fade_in, remain, sig, sub_ref, end_ref, ext):
    tiles, rows, _ = sig.shape
    modes = fade_in.shape[0]
    steps = rows // SUB
    for slot in range(2):
        ext[slot, 0:SUB, :] = jnp.zeros((SUB, ext.shape[2]), F32)
        for at in range(0, rows, 64):
            ext[slot, pl.ds(at + SUB, 64), :] = proj[slot + 1, pl.ds(at, 64), :].astype(F32)
    kept = lax.broadcasted_iota(jnp.int32, (64, LANES), 0) >= 2
    for tile in range(tiles):
        lanes = tile_of(tile)
        for at in range(0, rows, 64):
            value = filtered(ext, 0, taps, 1, at, 64, lanes, lanes)
            value *= filtered(ext, 1, taps, 2, at, 64, lanes, lanes)
            if at == 0:
                value = jnp.where(kept, value, 0.0)
            sig[tile, pl.ds(at, 64), :] = value
        fade = [spread(fade_in, m, lanes) for m in range(modes)]

        def step(i, held):
            now = sig[tile, pl.ds(i, SUB, stride=steps), :]
            return tuple(f * h + now for f, h in zip(fade, held))

        zero = tuple(jnp.zeros((SUB, LANES), F32) for _ in range(modes))
        held = lax.fori_loop(0, steps, step, zero, unroll=8)
        for m in range(modes):
            sub_ref[m, :, lanes] = held[m]
            end_ref[m : m + 1, lanes] = jnp.sum(
                held[m] * remain[m, :, lanes], axis=0, keepdims=True
            )


def preceding(halo, stream, lanes):
    value = halo[stream, 8:16, lanes].astype(F32)
    return jnp.where(jnp.full(value.shape, lax.axis_index("seq")) > 0, value, 0.0)


def edge_kernel(rows, proj, halo, taps, decay, end, edge_ref, out_ref):
    value = None
    for stream in (1, 2):
        first = proj[stream, 0:16, :].astype(F32)[0:SUB]
        joined = jnp.concatenate([preceding(halo, stream, slice(None)), first], 0)
        total = taps[stream, 0:1, :] * joined[SUB:]
        for lag in range(1, 3):
            total += taps[stream, lag : lag + 1, :] * joined[SUB - lag : 2 * SUB - lag]
        value = total if value is None else value * total
    edge_ref[...] = value
    rate = decay[...]
    out_ref[...] = (
        end[...]
        + jnp.exp(-float(rows - 1) * rate) * value[0:1]
        + jnp.exp(-float(rows - 2) * rate) * value[1:2]
    )


def local_kernel(
    tile, proj, halo, taps, decay, residue, skip, sig, sub, edge, query_ref, out_ref, ext
):
    lanes = tile_of(tile)
    whole = slice(0, LANES)
    modes = decay.shape[0]
    rows = sig.shape[1]
    steps = rows // SUB
    ext[0, 0:SUB, :] = preceding(halo, 0, lanes)
    for at in range(0, rows, 64):
        ext[0, pl.ds(at + SUB, 64), :] = proj[0, pl.ds(at, 64), lanes].astype(F32)
    for at in range(0, rows, 64):
        query_ref[pl.ds(at, 64), :] = filtered(ext, 0, taps, 0, at, 64, lanes, whole)

    place = lax.broadcasted_iota(jnp.int32, (SUB, LANES), 0)
    rates = [spread(decay, m, lanes) for m in range(modes)]
    fade = [jnp.exp(-r) for r in rates]
    gain = [residue[m : m + 1, lanes] * jnp.sqrt(r) for m, r in enumerate(rates)]
    direct = spread(skip, 0, lanes)
    one, two = edge[0:1, lanes], edge[1:2, lanes]
    start = []
    for m in range(modes):
        extra = jnp.exp(-rates[m] * float(steps - 1)) * one + jnp.exp(-rates[m] * float(steps - 2)) * two
        first = sub[m, :, lanes] + jnp.where(place == 0, extra, 0.0)
        run = jnp.where(place >= 1, pltpu.roll(first, 1, 0), 0.0)
        for shift in (1, 2, 4):
            before = jnp.where(place >= shift, pltpu.roll(run, shift, 0), 0.0)
            run = run + jnp.exp(-rates[m] * float(steps * shift)) * before
        start.append(run)

    def advance(i, held, more=None):
        at = pl.ds(i, SUB, stride=steps)
        now = sig[tile, at, :]
        if more is not None:
            now += jnp.where(place == 0, more, 0.0)
        held = tuple(f * h + now for f, h in zip(fade, held))
        out_ref[at, :] = tree([g * h for g, h in zip(gain, held)] + [direct * now])
        return held

    held = advance(1, advance(0, tuple(start), one), two)
    lax.fori_loop(2, steps, advance, held, unroll=2)


def gate_kernel(*refs):
    tiles = 4
    query, part = refs[:tiles], refs[tiles : 2 * tiles]
    state, stride, lead, low_ref, high_ref = refs[2 * tiles :]
    modes = state.shape[0]
    rows = low_ref.shape[0]
    for tile in range(tiles):
        lanes = tile_of(tile)
        fade = [spread(stride, m, lanes) for m in range(modes)]
        first = tuple(lead[m, :, lanes] * spread(state, m, lanes) for m in range(modes))

        def piece(at, held):
            value = query[tile][pl.ds(at, SUB), :] * (
                part[tile][pl.ds(at, SUB), :] + tree(list(held))
            )
            return value, tuple(f * h for f, h in zip(fade, held))

        def step(base, out_ref, i, held):
            at = pl.multiple_of(i * 16, 16)
            one, held = piece(at + base, held)
            two, held = piece(at + base + SUB, held)
            out_ref[pl.ds(at, 16), lanes] = jnp.concatenate([one, two], 0).astype(BF16)
            return held

        held = lax.fori_loop(0, rows // 16, partial(step, 0, low_ref), first, unroll=4)
        lax.fori_loop(0, rows // 16, partial(step, rows, high_ref), held, unroll=4)


def mix_kernel(plan, w_ref, *refs):
    blocks, rest = refs[: len(plan)], refs[len(plan) :]
    out_ref = rest[-1]
    depth = blocks[0].shape[1]
    total = None if len(rest) == 1 else rest[0][...]
    for block, step in zip(blocks, plan):
        term = jnp.dot(block[...], w_ref[source(step, depth), :], preferred_element_type=F32)
        total = term if total is None else total + term
    out_ref[...] = total


def last_kernel(w_ref, low, high, low_part, high_part, out_ref):
    rows, depth = low.shape
    weights = w_ref[source(2, depth), :]
    for at, block, part in ((0, low, low_part), (rows, high, high_part)):
        total = part[...] + jnp.dot(block[...], weights, preferred_element_type=F32)
        out_ref[pl.ds(at, rows), :] = total.astype(BF16)


def merge_kernel(span, radix, rows, end, decay, *refs):
    others, rest = refs[: radix - 1], list(refs[radix - 1 :])
    earlier = [rest.pop(0)] if span > 1 else []
    state_ref = rest.pop(0)
    place = lax.axis_index("seq")
    mine = lax.rem(lax.div(place, span), radix)
    inner = rows * lax.rem(place, span)
    unit = rows * span
    rate = decay[...]

    def faded(count):
        return jnp.exp(-rate * jnp.full(rate.shape, count).astype(F32))

    state = earlier[0][...] if earlier else jnp.zeros(rate.shape, F32)
    total = faded(unit * (radix - 1 - mine)) * end[...]
    for step, other in enumerate(others, 1):
        theirs = lax.rem(mine + step, radix)
        value = other[...]
        ahead = jnp.full(rate.shape, mine - theirs) > 0
        state += jnp.where(ahead, faded(jnp.maximum(unit * (mine - theirs - 1), 0) + inner) * value, 0.0)
        total += faded(unit * (radix - 1 - theirs)) * value
    state_ref[...] = state
    if rest:
        rest[0][...] = total


def carry_in(end, decay, rows, work):
    devices = lax.axis_size("seq")
    shape = pltpu.VMEM(end.shape, F32)
    state, results, span = (), [], 1
    for radix in (2, 4, 4):
        others = []
        for step in range(1, radix):
            route = []
            for i in range(devices):
                inside = i // span % radix
                route.append((i + ((inside + step) % radix - inside) * span, i))
            others.append(near(lax.ppermute(end, "seq", route)))
        made = [work(len(results) + j, end) for j in range(2)] if span > 1 else []
        final = span * radix == devices
        now, *after = call(
            partial(merge_kernel, span, radix, rows),
            "merge",
            (shape,) if final else (shape, shape),
            (end, decay, *others, *state),
            16 * end.size,
            MIB,
        )
        if made and not final:
            after, made = lax.optimization_barrier((after, made))
        results += made
        end, state = after[0] if after else None, (now,)
        span *= radix
    return state[0], results


def call(kernel, name, out_shape, args, work, nbytes, scratch=()):
    specs = [vmem() for _ in args]
    return pl.pallas_call(
        kernel,
        out_shape=out_shape,
        in_specs=specs,
        out_specs=jax.tree.map(lambda _: vmem(), out_shape),
        scratch_shapes=list(scratch),
        compiler_params=params(),
        cost_estimate=cost(work, nbytes),
        name=name,
    )(*args)


def shards(tokens, w_in, short_filter, decay, residue, skip, w_out):
    rows = tokens.shape[0]
    channels = skip.shape[0]
    modes = decay.shape[0]
    half = rows // 2
    tiles = channels // LANES
    weights = near(jnp.transpose(w_in, (1, 0, 2)))
    streams, depth, _ = weights.shape
    taps, decay, residue = near(short_filter), near(decay), near(residue)
    skip = near(skip.reshape(1, channels))
    full = 2 * half * depth * streams * channels
    sums = pltpu.VMEM((streams, half, channels), F32)
    rates = pltpu.VMEM((modes, channels), F32)
    ranks = pltpu.VMEM((modes, SUB, channels), F32)
    fade, remain, stride, lead = call(
        partial(prepare_kernel, steps=rows // SUB),
        "prepare",
        (rates, ranks, rates, ranks),
        (decay, residue),
        16 * SUB * channels,
        MIB,
    )

    def own(block):
        return call(own_kernel, "own", sums, (near(block), weights), full // 4, 8 * MIB)

    low_tok, high_tok, low_own = gather(tokens[:half], tokens[half:], lambda low, high: own(low))
    high_own = own(high_tok[0])
    low_tok, high_tok = [near(b) for b in low_tok], [near(b) for b in high_tok]
    low_part, high_part = call(
        near_kernel,
        "near",
        (sums, sums),
        (low_own, high_own, *low_tok[1:3], *high_tok[1:3], weights),
        full,
        8 * MIB,
    )
    proj = call(
        far_kernel,
        "far",
        pltpu.VMEM((streams, rows, channels), BF16),
        (low_part, high_part, low_tok[3], high_tok[3], weights),
        full // 2,
        6 * MIB,
    )
    count = lax.axis_size("seq")
    tail = proj[:, rows - 16 :]
    halo = near(lax.ppermute(tail, "seq", [(i, (i + 1) % count) for i in range(count)]))
    proj, _ = lax.optimization_barrier((proj, tail))
    sig, sub, end = call(
        early_kernel,
        "early",
        (
            pltpu.VMEM((tiles, rows, LANES), F32),
            pltpu.VMEM((modes, SUB, channels), F32),
            pltpu.VMEM((modes, channels), F32),
        ),
        (proj, taps, fade, remain),
        full // 2,
        6 * MIB,
        [pltpu.VMEM((2, rows + SUB, channels), F32)],
    )
    edge, end = call(
        partial(edge_kernel, rows),
        "edge",
        (pltpu.VMEM((SUB, channels), F32), pltpu.VMEM((modes, channels), F32)),
        (proj, halo, taps, decay, end),
        modes * channels,
        MIB,
    )

    def work(tile, gate):
        own_sig, _ = lax.optimization_barrier((sig, gate))
        return call(
            partial(local_kernel, tile),
            "local",
            (pltpu.VMEM((rows, LANES), F32), pltpu.VMEM((rows, LANES), F32)),
            (proj, halo, taps, decay, residue, skip, own_sig, sub, edge),
            8 * rows * channels * modes,
            4 * MIB,
            [pltpu.VMEM((1, rows + SUB, LANES), F32)],
        )

    state, local = carry_in(end, decay, rows, work)
    gates = call(
        gate_kernel,
        "gate",
        (pltpu.VMEM((half, channels), BF16), pltpu.VMEM((half, channels), BF16)),
        (*[q for q, _ in local], *[p for _, p in local], state, stride, lead),
        rows * channels * modes,
        4 * MIB,
    )
    w_out = near(w_out)
    totals = pltpu.VMEM((half, w_out.shape[1]), F32)

    def mix(blocks, plan, *earlier):
        return call(
            partial(mix_kernel, plan),
            "mix",
            totals,
            (w_out, *[near(block) for block in blocks], *earlier),
            2 * half * channels * channels * len(plan),
            2 * MIB,
        )

    low_gate, high_gate, (low_sum, high_sum) = gather(
        *gates, lambda low, high: [mix([block], (0,)) for block in (low, high)]
    )
    return call(
        last_kernel,
        "last",
        jax.ShapeDtypeStruct((rows, w_out.shape[1]), BF16),
        (
            w_out,
            near(low_gate[3]),
            near(high_gate[3]),
            mix(low_gate[1:3], (3, 1), low_sum),
            mix(high_gate[1:3], (3, 1), high_sum),
        ),
        4 * half * channels * channels,
        2 * MIB,
    )


def solution(mesh):
    in_specs = (
        P("seq", "ch"),
        P(None, None, "ch"),
        P(None, None, "ch"),
        P(None, "ch"),
        P(None, "ch"),
        P("ch"),
        P(None, "ch"),
    )
    return jax.shard_map(
        shards, mesh=mesh, in_specs=in_specs, out_specs=P("seq", "ch"), check_vma=False
    )
```

time: 72.1 us -> 71 us (0.985)
  waiting for transfers between devices: 18.5 us -> 30.4 us
  starting transfers between devices: 32.2 us -> 20.7 us
  Pallas kernels: 17.1 us -> 15.6 us
    ppermute x13, waiting for transfers between devices: 16.9 us -> 24.3 us  [the longest x12 20 us: swap(): lax.ppermute(block, 'ch', [(i, i ^ flip) for i in range(lax.axis_size('ch...]
    ppermute x13, starting transfers between devices: 19.5 us -> 13.2 us  [the longest x12 13.1 us: swap(): lax.ppermute(block, 'ch', [(i, i ^ flip) for i in range(lax.axis_size('ch...]
    ppermute x7, starting transfers between devices: 12.7 us -> 7.54 us  [carry_in(): others.append(near(lax.ppermute(end, 'seq', route)))]
    ppermute x7, waiting for transfers between devices: 1.55 us -> 6.07 us  [carry_in(): others.append(near(lax.ppermute(end, 'seq', route)))]
    pallas_call x3 -> x0, Pallas kernels: 2.98 us -> none  [the longest x2 2.42 us: mix_out(): pl.pallas_call(partial(mix_kernel, plan), out_shape=jax.ShapeDtypeStruct(...]
    pallas_call x14 -> x20, Pallas kernels: 14.1 us -> 15.6 us  [call(): pl.pallas_call(kernel, out_shape=out_shape, in_specs=specs, out_specs=jax...]
  transfers between devices with their start and end apart: 20 -> 20, of which waited for: 13 -> 14; matrix products, arithmetic and copies ran while one was open for 0% -> 0% of each run, Pallas kernels for 18% -> 17%
where the time goes in v2:
time: 71 us; the launch traced here: 70.8 us
  waiting for transfers between devices  30.4 us (43%)
  starting transfers between devices  20.7 us (29%)
  Pallas kernels  15.6 us (22%)
  local copies, waits for them, and re-layouts  3.88 us (5%)
    ppermute x12, waiting for transfers between devices, swap(): lax.ppermute(block, 'ch', [(i, i ^ flip) for i in range(lax.axis_size('ch...  20 us
    pallas_call x20, Pallas kernels, call(): pl.pallas_call(kernel, out_shape=out_shape, in_specs=specs, out_specs=jax...  15.6 us
    ppermute x12, starting transfers between devices, swap(): lax.ppermute(block, 'ch', [(i, i ^ flip) for i in range(lax.axis_size('ch...  13.1 us
    ppermute x7, starting transfers between devices, carry_in(): others.append(near(lax.ppermute(end, 'seq', route)))  7.54 us
    ppermute x7, waiting for transfers between devices, carry_in(): others.append(near(lax.ppermute(end, 'seq', route)))  6.07 us
    ppermute x1, waiting for transfers between devices, shards(): lax.ppermute(tail, 'seq', [(i, (i + 1) % count) for i in range(count)])  4.3 us
    unnamed x14, local copies, waits for them, and re-layouts  2.81 us
  transfers between devices with their start and end apart: 20, of which 14 were waited for; matrix products, arithmetic and copies ran while one was open for 0% of the time, Pallas kernels for 17%

profile of v2, /device:TPU:0, one launch (start us, length us, event | category | flops | bytes accessed | tf_op | source)
XLA Modules:
  0.0 70.8 jit_solution(8490432997780219821)
XLA Ops:
  0.0 1.1 %fusion = (bf16[256,512]{1,0:T(8,128)(2,1)S(1)}, bf16[256,512]{1,0:T(8,128)(2,1)S(1)}) fusion(bf16[512,512]{1,0:T(8,128)(2,1)} %param.7), kind=kLoop, calls=%fused_computation | loop fusion | bytes 1048576 | tf_op jit(solution)/shard_map/slice | solution.py:358
  1.1 3.2 %collective-permute-start = (bf16[256,512]{1,0:T(8,128)(2,1)S(1)}, bf16[256,512]{1,0:T(8,128)(2,1)S(1)}, u32[]{:S(2)}, u32[]{:S(2)}) collective-permute-start(bf16[256,512]{1,0:T(8,128)(2,1)S(1)} %get-tuple-element.47.block), channel_id=1, source_target_pairs={{0,3},{1,2},{2,1},{3,0},{4,7},{5,6},{6,5},{7,4},{8,11},{9,10},{10,... | collective-permute-start | bytes 786440 | tf_op jit(solution)/shard_map/ppermute | solution.py:34
  4.2 0.1 collective-permute-start.3
  4.4 2.8 %copy-done = bf16[2048,3,512]{2,0,1:T(8,128)(2,1)S(1)} copy-done((bf16[2048,3,512]{2,0,1:T(8,128)(2,1)S(1)}, bf16[2048,3,512]{2,0,1:T(8,128)(2,1)}, u32[]{:S(2)}) %copy-start) | copy-done | bytes 6291480
  7.2 0.6 own.2.low_part
  7.7 1.1 %collective-permute-start.2 = (bf16[256,512]{1,0:T(8,128)(2,1)S(1)}, bf16[256,512]{1,0:T(8,128)(2,1)S(1)}, u32[]{:S(2)}, u32[]{:S(2)}) collective-permute-start(bf16[256,512]{1,0:T(8,128)(2,1)S(1)} %get-tuple-element.46.block), channel_id=1, source_target_pairs={{0,3},{1,2},{2,1},{3,0},{4,7},{5,6},{6,5},{7,4},{8,11},{9,10},{10,... | collective-permute-start | bytes 786440 | tf_op jit(solution)/shard_map/ppermute | solution.py:34
  8.9 0.9 %collective-permute-start.1 = (bf16[256,512]{1,0:T(8,128)(2,1)S(1)}, bf16[256,512]{1,0:T(8,128)(2,1)S(1)}, u32[]{:S(2)}, u32[]{:S(2)}) collective-permute-start(bf16[256,512]{1,0:T(8,128)(2,1)S(1)} %get-tuple-element.47.block), channel_id=1, source_target_pairs={{0,1},{1,0},{2,3},{3,2},{4,5},{5,4},{6,7},{7,6},{8,9},{9,8},{10,11... | collective-permute-start | bytes 786440 | tf_op jit(solution)/shard_map/ppermute | solution.py:34
  9.8 1.1 %collective-permute-done.low_left = bf16[256,512]{1,0:T(8,128)(2,1)S(1)} collective-permute-done((bf16[256,512]{1,0:T(8,128)(2,1)S(1)}, bf16[256,512]{1,0:T(8,128)(2,1)S(1)}, u32[]{:S(2)}, u32[]{:S(2)}) %collective-permute-start) | collective-permute-done | bytes 262176 | tf_op jit(solution)/shard_map/ppermute | solution.py:34
  11.0 0.0 collective-permute-start.4
  11.0 2.5 %collective-permute-done.3.high_right = bf16[256,512]{1,0:T(8,128)(2,1)S(1)} collective-permute-done((bf16[256,512]{1,0:T(8,128)(2,1)S(1)}, bf16[256,512]{1,0:T(8,128)(2,1)S(1)}, u32[]{:S(2)}, u32[]{:S(2)}) %collective-permute-start.3) | collective-permute-done | bytes 262176 | tf_op jit(solution)/shard_map/ppermute | solution.py:34
  13.5 1.2 %collective-permute-start.5 = (bf16[256,512]{1,0:T(8,128)(2,1)S(1)}, bf16[256,512]{1,0:T(8,128)(2,1)S(1)}, u32[]{:S(2)}, u32[]{:S(2)}) collective-permute-start(bf16[256,512]{1,0:T(8,128)(2,1)S(1)} %collective-permute-done.3.high_right), channel_id=1, source_target_pairs={{0,3},{1,2},{2,1},{3,0},{4,7},{5,6},{6,5},{7,4},{8,11},{9,10},{10,... | collective-permute-start | bytes 786440 | tf_op jit(solution)/shard_map/ppermute | solution.py:34
  14.7 0.0 copy-done.3
  14.7 0.1 prepare.1
  14.8 0.0 copy-done.1
  14.8 0.6 own.3.high_part
  15.4 2.9 %collective-permute-done.2.high_left = bf16[256,512]{1,0:T(8,128)(2,1)S(1)} collective-permute-done((bf16[256,512]{1,0:T(8,128)(2,1)S(1)}, bf16[256,512]{1,0:T(8,128)(2,1)S(1)}, u32[]{:S(2)}, u32[]{:S(2)}) %collective-permute-start.2) | collective-permute-done | bytes 262176 | tf_op jit(solution)/shard_map/ppermute | solution.py:34
  18.3 0.8 %collective-permute-done.1.low_right = bf16[256,512]{1,0:T(8,128)(2,1)S(1)} collective-permute-done((bf16[256,512]{1,0:T(8,128)(2,1)S(1)}, bf16[256,512]{1,0:T(8,128)(2,1)S(1)}, u32[]{:S(2)}, u32[]{:S(2)}) %collective-permute-start.1) | collective-permute-done | bytes 262176 | tf_op jit(solution)/shard_map/ppermute | solution.py:34
  19.1 1.8 %near.1 = (f32[3,256,512]{2,1,0:T(8,128)S(1)}, f32[3,256,512]{2,1,0:T(8,128)S(1)}) custom-call(f32[3,256,512]{2,1,0:T(8,128)S(1)} %own.2.low_part, f32[3,256,512]{2,1,0:T(8,128)S(1)} %own.3.high_part, bf16[256,512]{1,0:T(8,128)(2,1)S(1)} %collective-permute-done.low_left, bf16[256,512]{1,0:T(8,128)(2,1)S(1)} %collective-permute-done.1.low_right, ...), custom_call_target="tpu_custom_call" | custom-call | flops 1610612736 | bytes 8388608 | tf_op jit(solution)/shard_map/near/pallas_call | solution.py:320
  20.9 2.4 %collective-permute-done.4.low_far = bf16[256,512]{1,0:T(8,128)(2,1)S(1)} collective-permute-done((bf16[256,512]{1,0:T(8,128)(2,1)S(1)}, bf16[256,512]{1,0:T(8,128)(2,1)S(1)}, u32[]{:S(2)}, u32[]{:S(2)}) %collective-permute-start.4) | collective-permute-done | bytes 262176 | tf_op jit(solution)/shard_map/ppermute | solution.py:34
  23.2 0.0 collective-permute-done.5.high_far
  23.3 1.0 %far.1.proj = bf16[3,512,512]{2,1,0:T(8,128)(2,1)S(1)} custom-call(f32[3,256,512]{2,1,0:T(8,128)S(1)} %get-tuple-element.48.low_part, f32[3,256,512]{2,1,0:T(8,128)S(1)} %get-tuple-element.49.high_part, bf16[256,512]{1,0:T(8,128)(2,1)S(1)} %collective-permute-done.4.low_far, bf16[256,512]{1,0:T(8,128)(2,1)S(1)} %collective-permute-done.5.high_far, ...), custom_call_target="tpu_custom_call" | custom-call | flops 805306368 | bytes 6291456 | tf_op jit(solution)/shard_map/far/pallas_call | solution.py:320
  24.3 0.1 collective-permute-start.6
  24.3 0.0 copy-done.5
  24.3 2.5 %early.1 = (f32[4,512,128]{2,1,0:T(8,128)S(1)}, f32[16,8,512]{2,1,0:T(8,128)S(1)}, f32[16,512]{1,0:T(8,128)S(1)}) custom-call(bf16[3,512,512]{2,1,0:T(8,128)(2,1)S(1)} %far.1.proj, f32[3,3,512]{2,1,0:T(4,128)S(1)} %copy-done.5, f32[16,512]{1,0:T(8,128)S(1)} %get-tuple-element.51.fade_in, f32[16,8,512]{2,1,0:T(8,128)S(1)} %get-tuple-element.52.remain), custom_call_target="tpu_custom_call" | custom-call | flops 805306368 | bytes 6291456 | tf_op jit(solution)/shard_map/early/pallas_call | solution.py:320
  26.8 0.0 copy-start.6
  26.9 4.3 %collective-permute-done.6.halo = bf16[3,16,512]{2,1,0:T(8,128)(2,1)S(1)} collective-permute-done((bf16[3,16,512]{2,1,0:T(8,128)(2,1)S(1)}, bf16[3,16,512]{2,1,0:T(8,128)(2,1)S(1)}, u32[]{:S(2)}, u32[]{:S(2)}) %collective-permute-start.6) | collective-permute-done | bytes 49184 | tf_op jit(solution)/shard_map/ppermute | solution.py:379
  31.2 0.1 collective-permute-start.7
  31.3 1.2 %collective-permute-done.7.refs_0_ = f32[16,512]{1,0:T(8,128)S(1)} collective-permute-done((f32[16,512]{1,0:T(8,128)S(1)}, f32[16,512]{1,0:T(8,128)S(1)}, u32[]{:S(2)}, u32[]{:S(2)}) %collective-permute-start.7) | collective-permute-done | bytes 32800 | tf_op jit(solution)/shard_map/ppermute | solution.py:299
  32.5 0.1 collective-permute-start.10
  32.6 3.2 %collective-permute-start.8 = (f32[16,512]{1,0:T(8,128)S(1)}, f32[16,512]{1,0:T(8,128)S(1)}, u32[]{:S(2)}, u32[]{:S(2)}) collective-permute-start(f32[16,512]{1,0:T(8,128)S(1)} %get-tuple-element.55.end), channel_id=1, source_target_pairs={{8,0},{12,4},{16,8},{20,12},{24,16},{28,20},{0,24},{4,28},{40,32},... | collective-permute-start | bytes 98312 | tf_op jit(solution)/shard_map/ppermute | solution.py:299
  35.8 0.0 collective-permute-start.9
  35.8 1.2 %local.5 = (f32[512,128]{1,0:T(8,128)S(1)}, f32[512,128]{1,0:T(8,128)S(1)}) custom-call(bf16[3,512,512]{2,1,0:T(8,128)(2,1)S(1)} %far.1.proj, bf16[3,16,512]{2,1,0:T(8,128)(2,1)S(1)} %collective-permute-done.6.halo, f32[3,3,512]{2,1,0:T(4,128)S(1)} %copy-done.5, f32[16,512]{1,0:T(8,128)S(1)} %copy-done.3, f32[16,512]{1,0:T(8,128)S(1)} %copy-done.4, ...), custom_call_target="tpu_custom_call" | custom-call | flops 33554432 | bytes 4194304 | tf_op jit(solution)/shard_map/local/pallas_call | solution.py:320
  37.0 1.2 %local.4 = (f32[512,128]{1,0:T(8,128)S(1)}, f32[512,128]{1,0:T(8,128)S(1)}) custom-call(bf16[3,512,512]{2,1,0:T(8,128)(2,1)S(1)} %far.1.proj, bf16[3,16,512]{2,1,0:T(8,128)(2,1)S(1)} %collective-permute-done.6.halo, f32[3,3,512]{2,1,0:T(4,128)S(1)} %copy-done.5, f32[16,512]{1,0:T(8,128)S(1)} %copy-done.3, f32[16,512]{1,0:T(8,128)S(1)} %copy-done.4, ...), custom_call_target="tpu_custom_call" | custom-call | flops 33554432 | bytes 4194304 | tf_op jit(solution)/shard_map/local/pallas_call | solution.py:320
  38.2 0.0 collective-permute-done.10.refs_2_
  38.2 0.0 collective-permute-done.8.refs_0_
  38.2 3.0 %collective-permute-done.9.refs_1_ = f32[16,512]{1,0:T(8,128)S(1)} collective-permute-done((f32[16,512]{1,0:T(8,128)S(1)}, f32[16,512]{1,0:T(8,128)S(1)}, u32[]{:S(2)}, u32[]{:S(2)}) %collective-permute-start.9) | collective-permute-done | bytes 32800 | tf_op jit(solution)/shard_map/ppermute | solution.py:299
  41.2 0.1 merge.4
  41.3 2.9 %collective-permute-start.11 = (f32[16,512]{1,0:T(8,128)S(1)}, f32[16,512]{1,0:T(8,128)S(1)}, u32[]{:S(2)}, u32[]{:S(2)}) collective-permute-start(f32[16,512]{1,0:T(8,128)S(1)} %get-tuple-element.68.end), channel_id=1, source_target_pairs={{32,0},{36,4},{40,8},{44,12},{48,16},{52,20},{56,24},{60,28},{64,3... | collective-permute-start | bytes 98312 | tf_op jit(solution)/shard_map/ppermute | solution.py:299
  44.2 0.0 collective-permute-start.12
  44.2 1.3 %collective-permute-start.13 = (f32[16,512]{1,0:T(8,128)S(1)}, f32[16,512]{1,0:T(8,128)S(1)}, u32[]{:S(2)}, u32[]{:S(2)}) collective-permute-start(f32[16,512]{1,0:T(8,128)S(1)} %get-tuple-element.68.end), channel_id=1, source_target_pairs={{96,0},{100,4},{104,8},{108,12},{112,16},{116,20},{120,24},{124,28... | collective-permute-start | bytes 98312 | tf_op jit(solution)/shard_map/ppermute | solution.py:299
  45.5 1.2 %local.7 = (f32[512,128]{1,0:T(8,128)S(1)}, f32[512,128]{1,0:T(8,128)S(1)}) custom-call(bf16[3,512,512]{2,1,0:T(8,128)(2,1)S(1)} %far.1.proj, bf16[3,16,512]{2,1,0:T(8,128)(2,1)S(1)} %collective-permute-done.6.halo, f32[3,3,512]{2,1,0:T(4,128)S(1)} %copy-done.5, f32[16,512]{1,0:T(8,128)S(1)} %copy-done.3, f32[16,512]{1,0:T(8,128)S(1)} %copy-done.4, ...), custom_call_target="tpu_custom_call" | custom-call | flops 33554432 | bytes 4194304 | tf_op jit(solution)/shard_map/local/pallas_call | solution.py:320
  46.6 1.2 %local.6 = (f32[512,128]{1,0:T(8,128)S(1)}, f32[512,128]{1,0:T(8,128)S(1)}) custom-call(bf16[3,512,512]{2,1,0:T(8,128)(2,1)S(1)} %far.1.proj, bf16[3,16,512]{2,1,0:T(8,128)(2,1)S(1)} %collective-permute-done.6.halo, f32[3,3,512]{2,1,0:T(4,128)S(1)} %copy-done.5, f32[16,512]{1,0:T(8,128)S(1)} %copy-done.3, f32[16,512]{1,0:T(8,128)S(1)} %copy-done.4, ...), custom_call_target="tpu_custom_call" | custom-call | flops 33554432 | bytes 4194304 | tf_op jit(solution)/shard_map/local/pallas_call | solution.py:320
  47.8 0.0 copy-start.2
  47.8 0.0 collective-permute-done.11.refs_0_
  47.8 1.8 %collective-permute-done.12.refs_1_ = f32[16,512]{1,0:T(8,128)S(1)} collective-permute-done((f32[16,512]{1,0:T(8,128)S(1)}, f32[16,512]{1,0:T(8,128)S(1)}, u32[]{:S(2)}, u32[]{:S(2)}) %collective-permute-start.12) | collective-permute-done | bytes 32800 | tf_op jit(solution)/shard_map/ppermute | solution.py:299
  49.7 0.0 collective-permute-done.13.refs_2_
  49.7 1.5 %gate.1 = (bf16[256,512]{1,0:T(8,128)(2,1)S(1)}, bf16[256,512]{1,0:T(8,128)(2,1)S(1)}) custom-call(f32[512,128]{1,0:T(8,128)S(1)} %get-tuple-element.66.refs_0_, f32[512,128]{1,0:T(8,128)S(1)} %get-tuple-element.67.refs_1_, f32[512,128]{1,0:T(8,128)S(1)} %get-tuple-element.70.refs_2_, f32[512,128]{1,0:T(8,128)S(1)} %get-tuple-element.71.refs_3_, ...), custom_call_target="tpu_custom_call" | custom-call | flops 4194304 | bytes 4194304 | tf_op jit(solution)/shard_map/gate/pallas_call | solution.py:320
  51.2 1.6 %collective-permute-start.14 = (bf16[256,512]{1,0:T(8,128)(2,1)S(1)}, bf16[256,512]{1,0:T(8,128)(2,1)S(1)}, u32[]{:S(2)}, u32[]{:S(2)}) collective-permute-start(bf16[256,512]{1,0:T(8,128)(2,1)S(1)} %get-tuple-element.81.refs_0_), channel_id=1, source_target_pairs={{0,3},{1,2},{2,1},{3,0},{4,7},{5,6},{6,5},{7,4},{8,11},{9,10},{10,... | collective-permute-start | bytes 786440 | tf_op jit(solution)/shard_map/ppermute | solution.py:34
  52.8 0.0 collective-permute-start.16
  52.8 0.3 mix.4.refs_2_
  53.1 0.3 mix.5.refs_2_
  53.4 1.8 %collective-permute-start.19 = (bf16[256,512]{1,0:T(8,128)(2,1)S(1)}, bf16[256,512]{1,0:T(8,128)(2,1)S(1)}, u32[]{:S(2)}, u32[]{:S(2)}) collective-permute-start(bf16[256,512]{1,0:T(8,128)(2,1)S(1)} %get-tuple-element.83.refs_0_), channel_id=1, source_target_pairs={{0,3},{1,2},{2,1},{3,0},{4,7},{5,6},{6,5},{7,4},{8,11},{9,10},{10,... | collective-permute-start | bytes 786440 | tf_op jit(solution)/shard_map/ppermute | solution.py:34
  55.2 1.4 %collective-permute-start.18 = (bf16[256,512]{1,0:T(8,128)(2,1)S(1)}, bf16[256,512]{1,0:T(8,128)(2,1)S(1)}, u32[]{:S(2)}, u32[]{:S(2)}) collective-permute-start(bf16[256,512]{1,0:T(8,128)(2,1)S(1)} %get-tuple-element.81.refs_0_), channel_id=1, source_target_pairs={{0,1},{1,0},{2,3},{3,2},{4,5},{5,4},{6,7},{7,6},{8,9},{9,8},{10,11... | collective-permute-start | bytes 786440 | tf_op jit(solution)/shard_map/ppermute | solution.py:34
  56.6 5.1 %collective-permute-done.14.refs_0_ = bf16[256,512]{1,0:T(8,128)(2,1)S(1)} collective-permute-done((bf16[256,512]{1,0:T(8,128)(2,1)S(1)}, bf16[256,512]{1,0:T(8,128)(2,1)S(1)}, u32[]{:S(2)}, u32[]{:S(2)}) %collective-permute-start.14) | collective-permute-done | bytes 262176 | tf_op jit(solution)/shard_map/ppermute | solution.py:34
  61.7 0.0 collective-permute-start.15
  61.7 0.3 collective-permute-done.16.refs_1_
  62.0 1.8 %collective-permute-start.17 = (bf16[256,512]{1,0:T(8,128)(2,1)S(1)}, bf16[256,512]{1,0:T(8,128)(2,1)S(1)}, u32[]{:S(2)}, u32[]{:S(2)}) collective-permute-start(bf16[256,512]{1,0:T(8,128)(2,1)S(1)} %collective-permute-done.16.refs_1_), channel_id=1, source_target_pairs={{0,3},{1,2},{2,1},{3,0},{4,7},{5,6},{6,5},{7,4},{8,11},{9,10},{10,... | collective-permute-start | bytes 786440 | tf_op jit(solution)/shard_map/ppermute | solution.py:34
  63.8 2.4 %collective-permute-done.19.refs_0_ = bf16[256,512]{1,0:T(8,128)(2,1)S(1)} collective-permute-done((bf16[256,512]{1,0:T(8,128)(2,1)S(1)}, bf16[256,512]{1,0:T(8,128)(2,1)S(1)}, u32[]{:S(2)}, u32[]{:S(2)}) %collective-permute-start.19) | collective-permute-done | bytes 262176 | tf_op jit(solution)/shard_map/ppermute | solution.py:34
  66.1 0.4 mix.7.high_part
  66.6 0.0 collective-permute-done.18.refs_1_
  66.6 0.4 mix.6.low_part
  67.0 1.9 %collective-permute-done.15.low = bf16[256,512]{1,0:T(8,128)(2,1)S(1)} collective-permute-done((bf16[256,512]{1,0:T(8,128)(2,1)S(1)}, bf16[256,512]{1,0:T(8,128)(2,1)S(1)}, u32[]{:S(2)}, u32[]{:S(2)}) %collective-permute-start.15) | collective-permute-done | bytes 262176 | tf_op jit(solution)/shard_map/ppermute | solution.py:34
  68.9 0.6 collective-permute-done.17.high
  69.6 1.2 %last.1 = bf16[512,512]{1,0:T(8,128)(2,1)} custom-call(bf16[2048,512]{1,0:T(8,128)(2,1)S(1)} %copy-done.2, bf16[256,512]{1,0:T(8,128)(2,1)S(1)} %collective-permute-done.15.low, bf16[256,512]{1,0:T(8,128)(2,1)S(1)} %collective-permute-done.17.high, f32[256,512]{1,0:T(8,128)S(1)} %mix.6.low_part, f32[256,512]{1,0:T(8,128)S(1)} %mix.7.high_part), custom_call_target="tpu_custom_call" | custom-call | flops 268435456 | bytes 2097152 | tf_op jit(solution)/shard_map/last/pallas_call | solution.py:320
  (12 shorter events, 0.1 us)
Async XLA Ops:
  1.1 9.9 %collective-permute-start = (bf16[256,512]{1,0:T(8,128)(2,1)S(1)}, bf16[256,512]{1,0:T(8,128)(2,1)S(1)}, u32[]{:S(2)}, u32[]{:S(2)}) collective-permute-start(bf16[256,512]{1,0:T(8,128)(2,1)S(1)} %get-tuple-element.47.block), channel_id=1, source_target_pairs={{0,3},{1,2},{2,1},{3,0},{4,7},{5,6},{6,5},{7,4},{8,11},{9,10},{10,... | collective-permute-start | bytes 786440 | tf_op jit(solution)/shard_map/ppermute | solution.py:34
  4.2 9.2 %collective-permute-start.3 = (bf16[256,512]{1,0:T(8,128)(2,1)S(1)}, bf16[256,512]{1,0:T(8,128)(2,1)S(1)}, u32[]{:S(2)}, u32[]{:S(2)}) collective-permute-start(bf16[256,512]{1,0:T(8,128)(2,1)S(1)} %get-tuple-element.46.block), channel_id=1, source_target_pairs={{0,1},{1,0},{2,3},{3,2},{4,5},{5,4},{6,7},{7,6},{8,9},{9,8},{10,11... | collective-permute-start | bytes 786440 | tf_op jit(solution)/shard_map/ppermute | solution.py:34
  4.4 2.8 %copy-start = (bf16[2048,3,512]{2,0,1:T(8,128)(2,1)S(1)}, bf16[2048,3,512]{2,0,1:T(8,128)(2,1)}, u32[]{:S(2)}) copy-start(bf16[2048,3,512]{2,0,1:T(8,128)(2,1)} %param.8) | copy-start | bytes 18874372
  7.2 7.5 %copy-start.3 = (f32[16,512]{1,0:T(8,128)S(1)}, f32[16,512]{1,0:T(8,128)}, u32[]{:S(2)}) copy-start(f32[16,512]{1,0:T(8,128)} %decay.17) | copy-start | bytes 98308
  7.2 7.5 %copy-start.4 = (f32[16,512]{1,0:T(8,128)S(1)}, f32[16,512]{1,0:T(8,128)}, u32[]{:S(2)}) copy-start(f32[16,512]{1,0:T(8,128)} %residue.9) | copy-start | bytes 98308
  7.2 7.6 %copy-start.1 = (bf16[2048,3,512]{2,0,1:T(8,128)(2,1)S(1)}, bf16[2048,3,512]{2,0,1:T(8,128)(2,1)}, u32[]{:S(2)}) copy-start(bf16[2048,3,512]{2,0,1:T(8,128)(2,1)} %param.8) | copy-start | bytes 18874372
  7.7 10.5 %collective-permute-start.2 = (bf16[256,512]{1,0:T(8,128)(2,1)S(1)}, bf16[256,512]{1,0:T(8,128)(2,1)S(1)}, u32[]{:S(2)}, u32[]{:S(2)}) collective-permute-start(bf16[256,512]{1,0:T(8,128)(2,1)S(1)} %get-tuple-element.46.block), channel_id=1, source_target_pairs={{0,3},{1,2},{2,1},{3,0},{4,7},{5,6},{6,5},{7,4},{8,11},{9,10},{10,... | collective-permute-start | bytes 786440 | tf_op jit(solution)/shard_map/ppermute | solution.py:34
  8.9 10.2 %collective-permute-start.1 = (bf16[256,512]{1,0:T(8,128)(2,1)S(1)}, bf16[256,512]{1,0:T(8,128)(2,1)S(1)}, u32[]{:S(2)}, u32[]{:S(2)}) collective-permute-start(bf16[256,512]{1,0:T(8,128)(2,1)S(1)} %get-tuple-element.47.block), channel_id=1, source_target_pairs={{0,1},{1,0},{2,3},{3,2},{4,5},{5,4},{6,7},{7,6},{8,9},{9,8},{10,11... | collective-permute-start | bytes 786440 | tf_op jit(solution)/shard_map/ppermute | solution.py:34
  11.0 12.3 %collective-permute-start.4 = (bf16[256,512]{1,0:T(8,128)(2,1)S(1)}, bf16[256,512]{1,0:T(8,128)(2,1)S(1)}, u32[]{:S(2)}, u32[]{:S(2)}) collective-permute-start(bf16[256,512]{1,0:T(8,128)(2,1)S(1)} %collective-permute-done.low_left), channel_id=1, source_target_pairs={{0,1},{1,0},{2,3},{3,2},{4,5},{5,4},{6,7},{7,6},{8,9},{9,8},{10,11... | collective-permute-start | bytes 786440 | tf_op jit(solution)/shard_map/ppermute | solution.py:34
  13.5 9.8 %collective-permute-start.5 = (bf16[256,512]{1,0:T(8,128)(2,1)S(1)}, bf16[256,512]{1,0:T(8,128)(2,1)S(1)}, u32[]{:S(2)}, u32[]{:S(2)}) collective-permute-start(bf16[256,512]{1,0:T(8,128)(2,1)S(1)} %collective-permute-done.3.high_right), channel_id=1, source_target_pairs={{0,3},{1,2},{2,1},{3,0},{4,7},{5,6},{6,5},{7,4},{8,11},{9,10},{10,... | collective-permute-start | bytes 786440 | tf_op jit(solution)/shard_map/ppermute | solution.py:34
  23.2 1.1 %copy-start.5 = (f32[3,3,512]{2,1,0:T(4,128)S(1)}, f32[3,3,512]{2,1,0:T(4,128)}, u32[]{:S(2)}) copy-start(f32[3,3,512]{2,1,0:T(4,128)} %taps.11) | copy-start | bytes 55300
  24.3 6.9 %collective-permute-start.6 = (bf16[3,16,512]{2,1,0:T(8,128)(2,1)S(1)}, bf16[3,16,512]{2,1,0:T(8,128)(2,1)S(1)}, u32[]{:S(2)}, u32[]{:S(2)}) collective-permute-start(bf16[3,16,512]{2,1,0:T(8,128)(2,1)S(1)} %slice.12), channel_id=1, source_target_pairs={{0,4},{4,8},{8,12},{12,16},{16,20},{20,24},{24,28},{28,32},{32,36}... | collective-permute-start | bytes 147464 | tf_op jit(solution)/shard_map/ppermute | solution.py:379
  26.8 9.0 %copy-start.6 = (f32[512]{0:T(512)S(1)}, f32[512]{0:T(512)}, u32[]{:S(2)}) copy-start(f32[512]{0:T(512)} %param.12) | copy-start | bytes 6148
  31.2 1.3 %collective-permute-start.7 = (f32[16,512]{1,0:T(8,128)S(1)}, f32[16,512]{1,0:T(8,128)S(1)}, u32[]{:S(2)}, u32[]{:S(2)}) collective-permute-start(f32[16,512]{1,0:T(8,128)S(1)} %get-tuple-element.54.end), channel_id=1, source_target_pairs={{4,0},{0,4},{12,8},{8,12},{20,16},{16,20},{28,24},{24,28},{36,32},... | collective-permute-start | bytes 98312 | tf_op jit(solution)/shard_map/ppermute | solution.py:299
  32.5 5.7 %collective-permute-start.10 = (f32[16,512]{1,0:T(8,128)S(1)}, f32[16,512]{1,0:T(8,128)S(1)}, u32[]{:S(2)}, u32[]{:S(2)}) collective-permute-start(f32[16,512]{1,0:T(8,128)S(1)} %get-tuple-element.55.end), channel_id=1, source_target_pairs={{24,0},{28,4},{0,8},{4,12},{8,16},{12,20},{16,24},{20,28},{56,32},... | collective-permute-start | bytes 98312 | tf_op jit(solution)/shard_map/ppermute | solution.py:299
  32.6 5.6 %collective-permute-start.8 = (f32[16,512]{1,0:T(8,128)S(1)}, f32[16,512]{1,0:T(8,128)S(1)}, u32[]{:S(2)}, u32[]{:S(2)}) collective-permute-start(f32[16,512]{1,0:T(8,128)S(1)} %get-tuple-element.55.end), channel_id=1, source_target_pairs={{8,0},{12,4},{16,8},{20,12},{24,16},{28,20},{0,24},{4,28},{40,32},... | collective-permute-start | bytes 98312 | tf_op jit(solution)/shard_map/ppermute | solution.py:299
  35.8 5.4 %collective-permute-start.9 = (f32[16,512]{1,0:T(8,128)S(1)}, f32[16,512]{1,0:T(8,128)S(1)}, u32[]{:S(2)}, u32[]{:S(2)}) collective-permute-start(f32[16,512]{1,0:T(8,128)S(1)} %get-tuple-element.55.end), channel_id=1, source_target_pairs={{16,0},{20,4},{24,8},{28,12},{0,16},{4,20},{8,24},{12,28},{48,32},... | collective-permute-start | bytes 98312 | tf_op jit(solution)/shard_map/ppermute | solution.py:299
  41.3 6.5 %collective-permute-start.11 = (f32[16,512]{1,0:T(8,128)S(1)}, f32[16,512]{1,0:T(8,128)S(1)}, u32[]{:S(2)}, u32[]{:S(2)}) collective-permute-start(f32[16,512]{1,0:T(8,128)S(1)} %get-tuple-element.68.end), channel_id=1, source_target_pairs={{32,0},{36,4},{40,8},{44,12},{48,16},{52,20},{56,24},{60,28},{64,3... | collective-permute-start | bytes 98312 | tf_op jit(solution)/shard_map/ppermute | solution.py:299
  44.2 5.5 %collective-permute-start.12 = (f32[16,512]{1,0:T(8,128)S(1)}, f32[16,512]{1,0:T(8,128)S(1)}, u32[]{:S(2)}, u32[]{:S(2)}) collective-permute-start(f32[16,512]{1,0:T(8,128)S(1)} %get-tuple-element.68.end), channel_id=1, source_target_pairs={{64,0},{68,4},{72,8},{76,12},{80,16},{84,20},{88,24},{92,28},{96,3... | collective-permute-start | bytes 98312 | tf_op jit(solution)/shard_map/ppermute | solution.py:299
  44.2 5.5 %collective-permute-start.13 = (f32[16,512]{1,0:T(8,128)S(1)}, f32[16,512]{1,0:T(8,128)S(1)}, u32[]{:S(2)}, u32[]{:S(2)}) collective-permute-start(f32[16,512]{1,0:T(8,128)S(1)} %get-tuple-element.68.end), channel_id=1, source_target_pairs={{96,0},{100,4},{104,8},{108,12},{112,16},{116,20},{120,24},{124,28... | collective-permute-start | bytes 98312 | tf_op jit(solution)/shard_map/ppermute | solution.py:299
  47.8 4.9 %copy-start.2 = (bf16[2048,512]{1,0:T(8,128)(2,1)S(1)}, bf16[2048,512]{1,0:T(8,128)(2,1)}, u32[]{:S(2)}) copy-start(bf16[2048,512]{1,0:T(8,128)(2,1)} %w_ref.9) | copy-start | bytes 6291460
  51.2 10.5 %collective-permute-start.14 = (bf16[256,512]{1,0:T(8,128)(2,1)S(1)}, bf16[256,512]{1,0:T(8,128)(2,1)S(1)}, u32[]{:S(2)}, u32[]{:S(2)}) collective-permute-start(bf16[256,512]{1,0:T(8,128)(2,1)S(1)} %get-tuple-element.81.refs_0_), channel_id=1, source_target_pairs={{0,3},{1,2},{2,1},{3,0},{4,7},{5,6},{6,5},{7,4},{8,11},{9,10},{10,... | collective-permute-start | bytes 786440 | tf_op jit(solution)/shard_map/ppermute | solution.py:34
  52.8 9.2 %collective-permute-start.16 = (bf16[256,512]{1,0:T(8,128)(2,1)S(1)}, bf16[256,512]{1,0:T(8,128)(2,1)S(1)}, u32[]{:S(2)}, u32[]{:S(2)}) collective-permute-start(bf16[256,512]{1,0:T(8,128)(2,1)S(1)} %get-tuple-element.83.refs_0_), channel_id=1, source_target_pairs={{0,1},{1,0},{2,3},{3,2},{4,5},{5,4},{6,7},{7,6},{8,9},{9,8},{10,11... | collective-permute-start | bytes 786440 | tf_op jit(solution)/shard_map/ppermute | solution.py:34
  53.4 12.8 %collective-permute-start.19 = (bf16[256,512]{1,0:T(8,128)(2,1)S(1)}, bf16[256,512]{1,0:T(8,128)(2,1)S(1)}, u32[]{:S(2)}, u32[]{:S(2)}) collective-permute-start(bf16[256,512]{1,0:T(8,128)(2,1)S(1)} %get-tuple-element.83.refs_0_), channel_id=1, source_target_pairs={{0,3},{1,2},{2,1},{3,0},{4,7},{5,6},{6,5},{7,4},{8,11},{9,10},{10,... | collective-permute-start | bytes 786440 | tf_op jit(solution)/shard_map/ppermute | solution.py:34
  55.2 11.4 %collective-permute-start.18 = (bf16[256,512]{1,0:T(8,128)(2,1)S(1)}, bf16[256,512]{1,0:T(8,128)(2,1)S(1)}, u32[]{:S(2)}, u32[]{:S(2)}) collective-permute-start(bf16[256,512]{1,0:T(8,128)(2,1)S(1)} %get-tuple-element.81.refs_0_), channel_id=1, source_target_pairs={{0,1},{1,0},{2,3},{3,2},{4,5},{5,4},{6,7},{7,6},{8,9},{9,8},{10,11... | collective-permute-start | bytes 786440 | tf_op jit(solution)/shard_map/ppermute | solution.py:34
  61.7 7.2 %collective-permute-start.15 = (bf16[256,512]{1,0:T(8,128)(2,1)S(1)}, bf16[256,512]{1,0:T(8,128)(2,1)S(1)}, u32[]{:S(2)}, u32[]{:S(2)}) collective-permute-start(bf16[256,512]{1,0:T(8,128)(2,1)S(1)} %collective-permute-done.14.refs_0_), channel_id=1, source_target_pairs={{0,1},{1,0},{2,3},{3,2},{4,5},{5,4},{6,7},{7,6},{8,9},{9,8},{10,11... | collective-permute-start | bytes 786440 | tf_op jit(solution)/shard_map/ppermute | solution.py:34
  62.0 7.6 %collective-permute-start.17 = (bf16[256,512]{1,0:T(8,128)(2,1)S(1)}, bf16[256,512]{1,0:T(8,128)(2,1)S(1)}, u32[]{:S(2)}, u32[]{:S(2)}) collective-permute-start(bf16[256,512]{1,0:T(8,128)(2,1)S(1)} %collective-permute-done.16.refs_1_), channel_id=1, source_target_pairs={{0,3},{1,2},{2,1},{3,0},{4,7},{5,6},{6,5},{7,4},{8,11},{9,10},{10,... | collective-permute-start | bytes 786440 | tf_op jit(solution)/shard_map/ppermute | solution.py:34

commit v3 on v2

--- a/solution.py
+++ b/solution.py
@@ -138,7 +138,7 @@
             return tuple(f * h + now for f, h in zip(fade, held))
 
         zero = tuple(jnp.zeros((SUB, LANES), F32) for _ in range(modes))
-        held = lax.fori_loop(0, steps, step, zero, unroll=8)
+        held = lax.fori_loop(0, steps, step, zero, unroll=16)
         for m in range(modes):
             sub_ref[m, :, lanes] = held[m]
             end_ref[m : m + 1, lanes] = jnp.sum(
@@ -236,8 +236,8 @@
             out_ref[pl.ds(at, 16), lanes] = jnp.concatenate([one, two], 0).astype(BF16)
             return held
 
-        held = lax.fori_loop(0, rows // 16, partial(step, 0, low_ref), first, unroll=4)
-        lax.fori_loop(0, rows // 16, partial(step, rows, high_ref), held, unroll=4)
+        held = lax.fori_loop(0, rows // 16, partial(step, 0, low_ref), first, unroll=8)
+        lax.fori_loop(0, rows // 16, partial(step, rows, high_ref), held, unroll=8)
 
 
 def mix_kernel(plan, w_ref, *refs):

time: 71 us -> 70.9 us (level)
  transfers between devices with their start and end apart: 20 -> 20, of which waited for: 14 -> 14; matrix products, arithmetic and copies ran while one was open for 0% -> 0% of each run, Pallas kernels for 17% -> 16%
where the time goes in v3:
time: 70.9 us; the launch traced here: 70.7 us
  waiting for transfers between devices  30.5 us (43%)
  starting transfers between devices  20.7 us (29%)
  Pallas kernels  15.3 us (22%)
  local copies, waits for them, and re-layouts  3.88 us (5%)
    ppermute x12, waiting for transfers between devices, swap(): lax.ppermute(block, 'ch', [(i, i ^ flip) for i in range(lax.axis_size('ch...  20 us
    pallas_call x20, Pallas kernels, call(): pl.pallas_call(kernel, out_shape=out_shape, in_specs=specs, out_specs=jax...  15.3 us
    ppermute x12, starting transfers between devices, swap(): lax.ppermute(block, 'ch', [(i, i ^ flip) for i in range(lax.axis_size('ch...  13.1 us
    ppermute x7, starting transfers between devices, carry_in(): others.append(near(lax.ppermute(end, 'seq', route)))  7.54 us
    ppermute x7, waiting for transfers between devices, carry_in(): others.append(near(lax.ppermute(end, 'seq', route)))  6.07 us
    ppermute x1, waiting for transfers between devices, shards(): lax.ppermute(tail, 'seq', [(i, (i + 1) % count) for i in range(count)])  4.45 us
    unnamed x14, local copies, waits for them, and re-layouts  2.81 us
  transfers between devices with their start and end apart: 20, of which 14 were waited for; matrix products, arithmetic and copies ran while one was open for 0% of the time, Pallas kernels for 16%

profile of v3, /device:TPU:0, one launch (start us, length us, event | category | flops | bytes accessed | tf_op | source)
XLA Modules:
  0.0 70.7 jit_solution(5507675071458950614)
XLA Ops:
  0.0 1.1 %fusion = (bf16[256,512]{1,0:T(8,128)(2,1)S(1)}, bf16[256,512]{1,0:T(8,128)(2,1)S(1)}) fusion(bf16[512,512]{1,0:T(8,128)(2,1)} %param.7), kind=kLoop, calls=%fused_computation | loop fusion | bytes 1048576 | tf_op jit(solution)/shard_map/slice | solution.py:358
  1.1 3.2 %collective-permute-start = (bf16[256,512]{1,0:T(8,128)(2,1)S(1)}, bf16[256,512]{1,0:T(8,128)(2,1)S(1)}, u32[]{:S(2)}, u32[]{:S(2)}) collective-permute-start(bf16[256,512]{1,0:T(8,128)(2,1)S(1)} %get-tuple-element.47.block), channel_id=1, source_target_pairs={{0,3},{1,2},{2,1},{3,0},{4,7},{5,6},{6,5},{7,4},{8,11},{9,10},{10,... | collective-permute-start | bytes 786440 | tf_op jit(solution)/shard_map/ppermute | solution.py:34
  4.2 0.1 collective-permute-start.3
  4.4 2.8 %copy-done = bf16[2048,3,512]{2,0,1:T(8,128)(2,1)S(1)} copy-done((bf16[2048,3,512]{2,0,1:T(8,128)(2,1)S(1)}, bf16[2048,3,512]{2,0,1:T(8,128)(2,1)}, u32[]{:S(2)}) %copy-start) | copy-done | bytes 6291480
  7.2 0.6 own.2.low_part
  7.7 1.1 %collective-permute-start.2 = (bf16[256,512]{1,0:T(8,128)(2,1)S(1)}, bf16[256,512]{1,0:T(8,128)(2,1)S(1)}, u32[]{:S(2)}, u32[]{:S(2)}) collective-permute-start(bf16[256,512]{1,0:T(8,128)(2,1)S(1)} %get-tuple-element.46.block), channel_id=1, source_target_pairs={{0,3},{1,2},{2,1},{3,0},{4,7},{5,6},{6,5},{7,4},{8,11},{9,10},{10,... | collective-permute-start | bytes 786440 | tf_op jit(solution)/shard_map/ppermute | solution.py:34
  8.9 0.9 %collective-permute-start.1 = (bf16[256,512]{1,0:T(8,128)(2,1)S(1)}, bf16[256,512]{1,0:T(8,128)(2,1)S(1)}, u32[]{:S(2)}, u32[]{:S(2)}) collective-permute-start(bf16[256,512]{1,0:T(8,128)(2,1)S(1)} %get-tuple-element.47.block), channel_id=1, source_target_pairs={{0,1},{1,0},{2,3},{3,2},{4,5},{5,4},{6,7},{7,6},{8,9},{9,8},{10,11... | collective-permute-start | bytes 786440 | tf_op jit(solution)/shard_map/ppermute | solution.py:34
  9.8 1.1 %collective-permute-done.low_left = bf16[256,512]{1,0:T(8,128)(2,1)S(1)} collective-permute-done((bf16[256,512]{1,0:T(8,128)(2,1)S(1)}, bf16[256,512]{1,0:T(8,128)(2,1)S(1)}, u32[]{:S(2)}, u32[]{:S(2)}) %collective-permute-start) | collective-permute-done | bytes 262176 | tf_op jit(solution)/shard_map/ppermute | solution.py:34
  11.0 0.0 collective-permute-start.4
  11.0 2.5 %collective-permute-done.3.high_right = bf16[256,512]{1,0:T(8,128)(2,1)S(1)} collective-permute-done((bf16[256,512]{1,0:T(8,128)(2,1)S(1)}, bf16[256,512]{1,0:T(8,128)(2,1)S(1)}, u32[]{:S(2)}, u32[]{:S(2)}) %collective-permute-start.3) | collective-permute-done | bytes 262176 | tf_op jit(solution)/shard_map/ppermute | solution.py:34
  13.5 1.2 %collective-permute-start.5 = (bf16[256,512]{1,0:T(8,128)(2,1)S(1)}, bf16[256,512]{1,0:T(8,128)(2,1)S(1)}, u32[]{:S(2)}, u32[]{:S(2)}) collective-permute-start(bf16[256,512]{1,0:T(8,128)(2,1)S(1)} %collective-permute-done.3.high_right), channel_id=1, source_target_pairs={{0,3},{1,2},{2,1},{3,0},{4,7},{5,6},{6,5},{7,4},{8,11},{9,10},{10,... | collective-permute-start | bytes 786440 | tf_op jit(solution)/shard_map/ppermute | solution.py:34
  14.7 0.1 prepare.1
  14.8 0.0 copy-done.1
  14.8 0.6 own.3.high_part
  15.4 2.9 %collective-permute-done.2.high_left = bf16[256,512]{1,0:T(8,128)(2,1)S(1)} collective-permute-done((bf16[256,512]{1,0:T(8,128)(2,1)S(1)}, bf16[256,512]{1,0:T(8,128)(2,1)S(1)}, u32[]{:S(2)}, u32[]{:S(2)}) %collective-permute-start.2) | collective-permute-done | bytes 262176 | tf_op jit(solution)/shard_map/ppermute | solution.py:34
  18.3 0.8 %collective-permute-done.1.low_right = bf16[256,512]{1,0:T(8,128)(2,1)S(1)} collective-permute-done((bf16[256,512]{1,0:T(8,128)(2,1)S(1)}, bf16[256,512]{1,0:T(8,128)(2,1)S(1)}, u32[]{:S(2)}, u32[]{:S(2)}) %collective-permute-start.1) | collective-permute-done | bytes 262176 | tf_op jit(solution)/shard_map/ppermute | solution.py:34
  19.1 1.8 %near.1 = (f32[3,256,512]{2,1,0:T(8,128)S(1)}, f32[3,256,512]{2,1,0:T(8,128)S(1)}) custom-call(f32[3,256,512]{2,1,0:T(8,128)S(1)} %own.2.low_part, f32[3,256,512]{2,1,0:T(8,128)S(1)} %own.3.high_part, bf16[256,512]{1,0:T(8,128)(2,1)S(1)} %collective-permute-done.low_left, bf16[256,512]{1,0:T(8,128)(2,1)S(1)} %collective-permute-done.1.low_right, ...), custom_call_target="tpu_custom_call" | custom-call | flops 1610612736 | bytes 8388608 | tf_op jit(solution)/shard_map/near/pallas_call | solution.py:320
  20.9 2.4 %collective-permute-done.4.low_far = bf16[256,512]{1,0:T(8,128)(2,1)S(1)} collective-permute-done((bf16[256,512]{1,0:T(8,128)(2,1)S(1)}, bf16[256,512]{1,0:T(8,128)(2,1)S(1)}, u32[]{:S(2)}, u32[]{:S(2)}) %collective-permute-start.4) | collective-permute-done | bytes 262176 | tf_op jit(solution)/shard_map/ppermute | solution.py:34
  23.2 0.0 collective-permute-done.5.high_far
  23.3 1.0 %far.1.proj = bf16[3,512,512]{2,1,0:T(8,128)(2,1)S(1)} custom-call(f32[3,256,512]{2,1,0:T(8,128)S(1)} %get-tuple-element.48.low_part, f32[3,256,512]{2,1,0:T(8,128)S(1)} %get-tuple-element.49.high_part, bf16[256,512]{1,0:T(8,128)(2,1)S(1)} %collective-permute-done.4.low_far, bf16[256,512]{1,0:T(8,128)(2,1)S(1)} %collective-permute-done.5.high_far, ...), custom_call_target="tpu_custom_call" | custom-call | flops 805306368 | bytes 6291456 | tf_op jit(solution)/shard_map/far/pallas_call | solution.py:320
  24.3 0.1 collective-permute-start.6
  24.3 0.0 copy-done.5
  24.3 2.3 %early.1 = (f32[4,512,128]{2,1,0:T(8,128)S(1)}, f32[16,8,512]{2,1,0:T(8,128)S(1)}, f32[16,512]{1,0:T(8,128)S(1)}) custom-call(bf16[3,512,512]{2,1,0:T(8,128)(2,1)S(1)} %far.1.proj, f32[3,3,512]{2,1,0:T(4,128)S(1)} %copy-done.5, f32[16,512]{1,0:T(8,128)S(1)} %get-tuple-element.51.fade_in, f32[16,8,512]{2,1,0:T(8,128)S(1)} %get-tuple-element.52.remain), custom_call_target="tpu_custom_call" | custom-call | flops 805306368 | bytes 6291456 | tf_op jit(solution)/shard_map/early/pallas_call | solution.py:320
  26.7 0.0 copy-start.6
  26.7 4.5 %collective-permute-done.6.halo = bf16[3,16,512]{2,1,0:T(8,128)(2,1)S(1)} collective-permute-done((bf16[3,16,512]{2,1,0:T(8,128)(2,1)S(1)}, bf16[3,16,512]{2,1,0:T(8,128)(2,1)S(1)}, u32[]{:S(2)}, u32[]{:S(2)}) %collective-permute-start.6) | collective-permute-done | bytes 49184 | tf_op jit(solution)/shard_map/ppermute | solution.py:379
  31.2 0.1 collective-permute-start.7
  31.3 1.2 %collective-permute-done.7.refs_0_ = f32[16,512]{1,0:T(8,128)S(1)} collective-permute-done((f32[16,512]{1,0:T(8,128)S(1)}, f32[16,512]{1,0:T(8,128)S(1)}, u32[]{:S(2)}, u32[]{:S(2)}) %collective-permute-start.7) | collective-permute-done | bytes 32800 | tf_op jit(solution)/shard_map/ppermute | solution.py:299
  32.5 0.1 collective-permute-start.10
  32.6 3.2 %collective-permute-start.8 = (f32[16,512]{1,0:T(8,128)S(1)}, f32[16,512]{1,0:T(8,128)S(1)}, u32[]{:S(2)}, u32[]{:S(2)}) collective-permute-start(f32[16,512]{1,0:T(8,128)S(1)} %get-tuple-element.55.end), channel_id=1, source_target_pairs={{8,0},{12,4},{16,8},{20,12},{24,16},{28,20},{0,24},{4,28},{40,32},... | collective-permute-start | bytes 98312 | tf_op jit(solution)/shard_map/ppermute | solution.py:299
  35.8 0.0 collective-permute-start.9
  35.8 1.2 %local.5 = (f32[512,128]{1,0:T(8,128)S(1)}, f32[512,128]{1,0:T(8,128)S(1)}) custom-call(bf16[3,512,512]{2,1,0:T(8,128)(2,1)S(1)} %far.1.proj, bf16[3,16,512]{2,1,0:T(8,128)(2,1)S(1)} %collective-permute-done.6.halo, f32[3,3,512]{2,1,0:T(4,128)S(1)} %copy-done.5, f32[16,512]{1,0:T(8,128)S(1)} %copy-done.3, f32[16,512]{1,0:T(8,128)S(1)} %copy-done.4, ...), custom_call_target="tpu_custom_call" | custom-call | flops 33554432 | bytes 4194304 | tf_op jit(solution)/shard_map/local/pallas_call | solution.py:320
  37.0 1.2 %local.4 = (f32[512,128]{1,0:T(8,128)S(1)}, f32[512,128]{1,0:T(8,128)S(1)}) custom-call(bf16[3,512,512]{2,1,0:T(8,128)(2,1)S(1)} %far.1.proj, bf16[3,16,512]{2,1,0:T(8,128)(2,1)S(1)} %collective-permute-done.6.halo, f32[3,3,512]{2,1,0:T(4,128)S(1)} %copy-done.5, f32[16,512]{1,0:T(8,128)S(1)} %copy-done.3, f32[16,512]{1,0:T(8,128)S(1)} %copy-done.4, ...), custom_call_target="tpu_custom_call" | custom-call | flops 33554432 | bytes 4194304 | tf_op jit(solution)/shard_map/local/pallas_call | solution.py:320
  38.2 0.0 collective-permute-done.10.refs_2_
  38.2 0.0 collective-permute-done.8.refs_0_
  38.2 3.0 %collective-permute-done.9.refs_1_ = f32[16,512]{1,0:T(8,128)S(1)} collective-permute-done((f32[16,512]{1,0:T(8,128)S(1)}, f32[16,512]{1,0:T(8,128)S(1)}, u32[]{:S(2)}, u32[]{:S(2)}) %collective-permute-start.9) | collective-permute-done | bytes 32800 | tf_op jit(solution)/shard_map/ppermute | solution.py:299
  41.2 0.1 merge.4
  41.3 2.9 %collective-permute-start.11 = (f32[16,512]{1,0:T(8,128)S(1)}, f32[16,512]{1,0:T(8,128)S(1)}, u32[]{:S(2)}, u32[]{:S(2)}) collective-permute-start(f32[16,512]{1,0:T(8,128)S(1)} %get-tuple-element.68.end), channel_id=1, source_target_pairs={{32,0},{36,4},{40,8},{44,12},{48,16},{52,20},{56,24},{60,28},{64,3... | collective-permute-start | bytes 98312 | tf_op jit(solution)/shard_map/ppermute | solution.py:299
  44.2 0.0 collective-permute-start.12
  44.2 1.3 %collective-permute-start.13 = (f32[16,512]{1,0:T(8,128)S(1)}, f32[16,512]{1,0:T(8,128)S(1)}, u32[]{:S(2)}, u32[]{:S(2)}) collective-permute-start(f32[16,512]{1,0:T(8,128)S(1)} %get-tuple-element.68.end), channel_id=1, source_target_pairs={{96,0},{100,4},{104,8},{108,12},{112,16},{116,20},{120,24},{124,28... | collective-permute-start | bytes 98312 | tf_op jit(solution)/shard_map/ppermute | solution.py:299
  45.5 1.2 %local.7 = (f32[512,128]{1,0:T(8,128)S(1)}, f32[512,128]{1,0:T(8,128)S(1)}) custom-call(bf16[3,512,512]{2,1,0:T(8,128)(2,1)S(1)} %far.1.proj, bf16[3,16,512]{2,1,0:T(8,128)(2,1)S(1)} %collective-permute-done.6.halo, f32[3,3,512]{2,1,0:T(4,128)S(1)} %copy-done.5, f32[16,512]{1,0:T(8,128)S(1)} %copy-done.3, f32[16,512]{1,0:T(8,128)S(1)} %copy-done.4, ...), custom_call_target="tpu_custom_call" | custom-call | flops 33554432 | bytes 4194304 | tf_op jit(solution)/shard_map/local/pallas_call | solution.py:320
  46.6 1.2 %local.6 = (f32[512,128]{1,0:T(8,128)S(1)}, f32[512,128]{1,0:T(8,128)S(1)}) custom-call(bf16[3,512,512]{2,1,0:T(8,128)(2,1)S(1)} %far.1.proj, bf16[3,16,512]{2,1,0:T(8,128)(2,1)S(1)} %collective-permute-done.6.halo, f32[3,3,512]{2,1,0:T(4,128)S(1)} %copy-done.5, f32[16,512]{1,0:T(8,128)S(1)} %copy-done.3, f32[16,512]{1,0:T(8,128)S(1)} %copy-done.4, ...), custom_call_target="tpu_custom_call" | custom-call | flops 33554432 | bytes 4194304 | tf_op jit(solution)/shard_map/local/pallas_call | solution.py:320
  47.8 0.0 copy-start.2
  47.8 0.0 collective-permute-done.11.refs_0_
  47.8 1.8 %collective-permute-done.12.refs_1_ = f32[16,512]{1,0:T(8,128)S(1)} collective-permute-done((f32[16,512]{1,0:T(8,128)S(1)}, f32[16,512]{1,0:T(8,128)S(1)}, u32[]{:S(2)}, u32[]{:S(2)}) %collective-permute-start.12) | collective-permute-done | bytes 32800 | tf_op jit(solution)/shard_map/ppermute | solution.py:299
  49.7 0.0 collective-permute-done.13.refs_2_
  49.7 1.4 %gate.1 = (bf16[256,512]{1,0:T(8,128)(2,1)S(1)}, bf16[256,512]{1,0:T(8,128)(2,1)S(1)}) custom-call(f32[512,128]{1,0:T(8,128)S(1)} %get-tuple-element.66.refs_0_, f32[512,128]{1,0:T(8,128)S(1)} %get-tuple-element.67.refs_1_, f32[512,128]{1,0:T(8,128)S(1)} %get-tuple-element.70.refs_2_, f32[512,128]{1,0:T(8,128)S(1)} %get-tuple-element.71.refs_3_, ...), custom_call_target="tpu_custom_call" | custom-call | flops 4194304 | bytes 4194304 | tf_op jit(solution)/shard_map/gate/pallas_call | solution.py:320
  51.1 1.6 %collective-permute-start.14 = (bf16[256,512]{1,0:T(8,128)(2,1)S(1)}, bf16[256,512]{1,0:T(8,128)(2,1)S(1)}, u32[]{:S(2)}, u32[]{:S(2)}) collective-permute-start(bf16[256,512]{1,0:T(8,128)(2,1)S(1)} %get-tuple-element.81.refs_0_), channel_id=1, source_target_pairs={{0,3},{1,2},{2,1},{3,0},{4,7},{5,6},{6,5},{7,4},{8,11},{9,10},{10,... | collective-permute-start | bytes 786440 | tf_op jit(solution)/shard_map/ppermute | solution.py:34
  52.6 0.0 collective-permute-start.16
  52.7 0.0 copy-done.2
  52.7 0.3 mix.4.refs_2_
  53.0 0.3 mix.5.refs_2_
  53.3 1.8 %collective-permute-start.19 = (bf16[256,512]{1,0:T(8,128)(2,1)S(1)}, bf16[256,512]{1,0:T(8,128)(2,1)S(1)}, u32[]{:S(2)}, u32[]{:S(2)}) collective-permute-start(bf16[256,512]{1,0:T(8,128)(2,1)S(1)} %get-tuple-element.83.refs_0_), channel_id=1, source_target_pairs={{0,3},{1,2},{2,1},{3,0},{4,7},{5,6},{6,5},{7,4},{8,11},{9,10},{10,... | collective-permute-start | bytes 786440 | tf_op jit(solution)/shard_map/ppermute | solution.py:34
  55.1 1.4 %collective-permute-start.18 = (bf16[256,512]{1,0:T(8,128)(2,1)S(1)}, bf16[256,512]{1,0:T(8,128)(2,1)S(1)}, u32[]{:S(2)}, u32[]{:S(2)}) collective-permute-start(bf16[256,512]{1,0:T(8,128)(2,1)S(1)} %get-tuple-element.81.refs_0_), channel_id=1, source_target_pairs={{0,1},{1,0},{2,3},{3,2},{4,5},{5,4},{6,7},{7,6},{8,9},{9,8},{10,11... | collective-permute-start | bytes 786440 | tf_op jit(solution)/shard_map/ppermute | solution.py:34
  56.5 5.1 %collective-permute-done.14.refs_0_ = bf16[256,512]{1,0:T(8,128)(2,1)S(1)} collective-permute-done((bf16[256,512]{1,0:T(8,128)(2,1)S(1)}, bf16[256,512]{1,0:T(8,128)(2,1)S(1)}, u32[]{:S(2)}, u32[]{:S(2)}) %collective-permute-start.14) | collective-permute-done | bytes 262176 | tf_op jit(solution)/shard_map/ppermute | solution.py:34
  61.6 0.0 collective-permute-start.15
  61.6 0.3 collective-permute-done.16.refs_1_
  61.9 1.8 %collective-permute-start.17 = (bf16[256,512]{1,0:T(8,128)(2,1)S(1)}, bf16[256,512]{1,0:T(8,128)(2,1)S(1)}, u32[]{:S(2)}, u32[]{:S(2)}) collective-permute-start(bf16[256,512]{1,0:T(8,128)(2,1)S(1)} %collective-permute-done.16.refs_1_), channel_id=1, source_target_pairs={{0,3},{1,2},{2,1},{3,0},{4,7},{5,6},{6,5},{7,4},{8,11},{9,10},{10,... | collective-permute-start | bytes 786440 | tf_op jit(solution)/shard_map/ppermute | solution.py:34
  63.6 2.4 %collective-permute-done.19.refs_0_ = bf16[256,512]{1,0:T(8,128)(2,1)S(1)} collective-permute-done((bf16[256,512]{1,0:T(8,128)(2,1)S(1)}, bf16[256,512]{1,0:T(8,128)(2,1)S(1)}, u32[]{:S(2)}, u32[]{:S(2)}) %collective-permute-start.19) | collective-permute-done | bytes 262176 | tf_op jit(solution)/shard_map/ppermute | solution.py:34
  66.0 0.4 mix.7.high_part
  66.5 0.0 collective-permute-done.18.refs_1_
  66.5 0.4 mix.6.low_part
  66.9 1.9 %collective-permute-done.15.low = bf16[256,512]{1,0:T(8,128)(2,1)S(1)} collective-permute-done((bf16[256,512]{1,0:T(8,128)(2,1)S(1)}, bf16[256,512]{1,0:T(8,128)(2,1)S(1)}, u32[]{:S(2)}, u32[]{:S(2)}) %collective-permute-start.15) | collective-permute-done | bytes 262176 | tf_op jit(solution)/shard_map/ppermute | solution.py:34
  68.8 0.6 collective-permute-done.17.high
  69.5 1.2 %last.1 = bf16[512,512]{1,0:T(8,128)(2,1)} custom-call(bf16[2048,512]{1,0:T(8,128)(2,1)S(1)} %copy-done.2, bf16[256,512]{1,0:T(8,128)(2,1)S(1)} %collective-permute-done.15.low, bf16[256,512]{1,0:T(8,128)(2,1)S(1)} %collective-permute-done.17.high, f32[256,512]{1,0:T(8,128)S(1)} %mix.6.low_part, f32[256,512]{1,0:T(8,128)S(1)} %mix.7.high_part), custom_call_target="tpu_custom_call" | custom-call | flops 268435456 | bytes 2097152 | tf_op jit(solution)/shard_map/last/pallas_call | solution.py:320
  (12 shorter events, 0.1 us)
Async XLA Ops:
  1.1 9.9 %collective-permute-start = (bf16[256,512]{1,0:T(8,128)(2,1)S(1)}, bf16[256,512]{1,0:T(8,128)(2,1)S(1)}, u32[]{:S(2)}, u32[]{:S(2)}) collective-permute-start(bf16[256,512]{1,0:T(8,128)(2,1)S(1)} %get-tuple-element.47.block), channel_id=1, source_target_pairs={{0,3},{1,2},{2,1},{3,0},{4,7},{5,6},{6,5},{7,4},{8,11},{9,10},{10,... | collective-permute-start | bytes 786440 | tf_op jit(solution)/shard_map/ppermute | solution.py:34
  4.2 9.2 %collective-permute-start.3 = (bf16[256,512]{1,0:T(8,128)(2,1)S(1)}, bf16[256,512]{1,0:T(8,128)(2,1)S(1)}, u32[]{:S(2)}, u32[]{:S(2)}) collective-permute-start(bf16[256,512]{1,0:T(8,128)(2,1)S(1)} %get-tuple-element.46.block), channel_id=1, source_target_pairs={{0,1},{1,0},{2,3},{3,2},{4,5},{5,4},{6,7},{7,6},{8,9},{9,8},{10,11... | collective-permute-start | bytes 786440 | tf_op jit(solution)/shard_map/ppermute | solution.py:34
  4.4 2.8 %copy-start = (bf16[2048,3,512]{2,0,1:T(8,128)(2,1)S(1)}, bf16[2048,3,512]{2,0,1:T(8,128)(2,1)}, u32[]{:S(2)}) copy-start(bf16[2048,3,512]{2,0,1:T(8,128)(2,1)} %param.8) | copy-start | bytes 18874372
  7.2 7.5 %copy-start.3 = (f32[16,512]{1,0:T(8,128)S(1)}, f32[16,512]{1,0:T(8,128)}, u32[]{:S(2)}) copy-start(f32[16,512]{1,0:T(8,128)} %decay.17) | copy-start | bytes 98308
  7.2 7.5 %copy-start.4 = (f32[16,512]{1,0:T(8,128)S(1)}, f32[16,512]{1,0:T(8,128)}, u32[]{:S(2)}) copy-start(f32[16,512]{1,0:T(8,128)} %residue.9) | copy-start | bytes 98308
  7.2 7.6 %copy-start.1 = (bf16[2048,3,512]{2,0,1:T(8,128)(2,1)S(1)}, bf16[2048,3,512]{2,0,1:T(8,128)(2,1)}, u32[]{:S(2)}) copy-start(bf16[2048,3,512]{2,0,1:T(8,128)(2,1)} %param.8) | copy-start | bytes 18874372
  7.7 10.5 %collective-permute-start.2 = (bf16[256,512]{1,0:T(8,128)(2,1)S(1)}, bf16[256,512]{1,0:T(8,128)(2,1)S(1)}, u32[]{:S(2)}, u32[]{:S(2)}) collective-permute-start(bf16[256,512]{1,0:T(8,128)(2,1)S(1)} %get-tuple-element.46.block), channel_id=1, source_target_pairs={{0,3},{1,2},{2,1},{3,0},{4,7},{5,6},{6,5},{7,4},{8,11},{9,10},{10,... | collective-permute-start | bytes 786440 | tf_op jit(solution)/shard_map/ppermute | solution.py:34
  8.9 10.2 %collective-permute-start.1 = (bf16[256,512]{1,0:T(8,128)(2,1)S(1)}, bf16[256,512]{1,0:T(8,128)(2,1)S(1)}, u32[]{:S(2)}, u32[]{:S(2)}) collective-permute-start(bf16[256,512]{1,0:T(8,128)(2,1)S(1)} %get-tuple-element.47.block), channel_id=1, source_target_pairs={{0,1},{1,0},{2,3},{3,2},{4,5},{5,4},{6,7},{7,6},{8,9},{9,8},{10,11... | collective-permute-start | bytes 786440 | tf_op jit(solution)/shard_map/ppermute | solution.py:34
  11.0 12.3 %collective-permute-start.4 = (bf16[256,512]{1,0:T(8,128)(2,1)S(1)}, bf16[256,512]{1,0:T(8,128)(2,1)S(1)}, u32[]{:S(2)}, u32[]{:S(2)}) collective-permute-start(bf16[256,512]{1,0:T(8,128)(2,1)S(1)} %collective-permute-done.low_left), channel_id=1, source_target_pairs={{0,1},{1,0},{2,3},{3,2},{4,5},{5,4},{6,7},{7,6},{8,9},{9,8},{10,11... | collective-permute-start | bytes 786440 | tf_op jit(solution)/shard_map/ppermute | solution.py:34
  13.5 9.8 %collective-permute-start.5 = (bf16[256,512]{1,0:T(8,128)(2,1)S(1)}, bf16[256,512]{1,0:T(8,128)(2,1)S(1)}, u32[]{:S(2)}, u32[]{:S(2)}) collective-permute-start(bf16[256,512]{1,0:T(8,128)(2,1)S(1)} %collective-permute-done.3.high_right), channel_id=1, source_target_pairs={{0,3},{1,2},{2,1},{3,0},{4,7},{5,6},{6,5},{7,4},{8,11},{9,10},{10,... | collective-permute-start | bytes 786440 | tf_op jit(solution)/shard_map/ppermute | solution.py:34
  23.2 1.1 %copy-start.5 = (f32[3,3,512]{2,1,0:T(4,128)S(1)}, f32[3,3,512]{2,1,0:T(4,128)}, u32[]{:S(2)}) copy-start(f32[3,3,512]{2,1,0:T(4,128)} %taps.11) | copy-start | bytes 55300
  24.3 6.9 %collective-permute-start.6 = (bf16[3,16,512]{2,1,0:T(8,128)(2,1)S(1)}, bf16[3,16,512]{2,1,0:T(8,128)(2,1)S(1)}, u32[]{:S(2)}, u32[]{:S(2)}) collective-permute-start(bf16[3,16,512]{2,1,0:T(8,128)(2,1)S(1)} %slice.12), channel_id=1, source_target_pairs={{0,4},{4,8},{8,12},{12,16},{16,20},{20,24},{24,28},{28,32},{32,36}... | collective-permute-start | bytes 147464 | tf_op jit(solution)/shard_map/ppermute | solution.py:379
  26.7 9.1 %copy-start.6 = (f32[512]{0:T(512)S(1)}, f32[512]{0:T(512)}, u32[]{:S(2)}) copy-start(f32[512]{0:T(512)} %param.12) | copy-start | bytes 6148
  31.2 1.3 %collective-permute-start.7 = (f32[16,512]{1,0:T(8,128)S(1)}, f32[16,512]{1,0:T(8,128)S(1)}, u32[]{:S(2)}, u32[]{:S(2)}) collective-permute-start(f32[16,512]{1,0:T(8,128)S(1)} %get-tuple-element.54.end), channel_id=1, source_target_pairs={{4,0},{0,4},{12,8},{8,12},{20,16},{16,20},{28,24},{24,28},{36,32},... | collective-permute-start | bytes 98312 | tf_op jit(solution)/shard_map/ppermute | solution.py:299
  32.5 5.7 %collective-permute-start.10 = (f32[16,512]{1,0:T(8,128)S(1)}, f32[16,512]{1,0:T(8,128)S(1)}, u32[]{:S(2)}, u32[]{:S(2)}) collective-permute-start(f32[16,512]{1,0:T(8,128)S(1)} %get-tuple-element.55.end), channel_id=1, source_target_pairs={{24,0},{28,4},{0,8},{4,12},{8,16},{12,20},{16,24},{20,28},{56,32},... | collective-permute-start | bytes 98312 | tf_op jit(solution)/shard_map/ppermute | solution.py:299
  32.6 5.6 %collective-permute-start.8 = (f32[16,512]{1,0:T(8,128)S(1)}, f32[16,512]{1,0:T(8,128)S(1)}, u32[]{:S(2)}, u32[]{:S(2)}) collective-permute-start(f32[16,512]{1,0:T(8,128)S(1)} %get-tuple-element.55.end), channel_id=1, source_target_pairs={{8,0},{12,4},{16,8},{20,12},{24,16},{28,20},{0,24},{4,28},{40,32},... | collective-permute-start | bytes 98312 | tf_op jit(solution)/shard_map/ppermute | solution.py:299
  35.8 5.4 %collective-permute-start.9 = (f32[16,512]{1,0:T(8,128)S(1)}, f32[16,512]{1,0:T(8,128)S(1)}, u32[]{:S(2)}, u32[]{:S(2)}) collective-permute-start(f32[16,512]{1,0:T(8,128)S(1)} %get-tuple-element.55.end), channel_id=1, source_target_pairs={{16,0},{20,4},{24,8},{28,12},{0,16},{4,20},{8,24},{12,28},{48,32},... | collective-permute-start | bytes 98312 | tf_op jit(solution)/shard_map/ppermute | solution.py:299
  41.3 6.5 %collective-permute-start.11 = (f32[16,512]{1,0:T(8,128)S(1)}, f32[16,512]{1,0:T(8,128)S(1)}, u32[]{:S(2)}, u32[]{:S(2)}) collective-permute-start(f32[16,512]{1,0:T(8,128)S(1)} %get-tuple-element.68.end), channel_id=1, source_target_pairs={{32,0},{36,4},{40,8},{44,12},{48,16},{52,20},{56,24},{60,28},{64,3... | collective-permute-start | bytes 98312 | tf_op jit(solution)/shard_map/ppermute | solution.py:299
  44.2 5.5 %collective-permute-start.12 = (f32[16,512]{1,0:T(8,128)S(1)}, f32[16,512]{1,0:T(8,128)S(1)}, u32[]{:S(2)}, u32[]{:S(2)}) collective-permute-start(f32[16,512]{1,0:T(8,128)S(1)} %get-tuple-element.68.end), channel_id=1, source_target_pairs={{64,0},{68,4},{72,8},{76,12},{80,16},{84,20},{88,24},{92,28},{96,3... | collective-permute-start | bytes 98312 | tf_op jit(solution)/shard_map/ppermute | solution.py:299
  44.2 5.5 %collective-permute-start.13 = (f32[16,512]{1,0:T(8,128)S(1)}, f32[16,512]{1,0:T(8,128)S(1)}, u32[]{:S(2)}, u32[]{:S(2)}) collective-permute-start(f32[16,512]{1,0:T(8,128)S(1)} %get-tuple-element.68.end), channel_id=1, source_target_pairs={{96,0},{100,4},{104,8},{108,12},{112,16},{116,20},{120,24},{124,28... | collective-permute-start | bytes 98312 | tf_op jit(solution)/shard_map/ppermute | solution.py:299
  47.8 4.8 %copy-start.2 = (bf16[2048,512]{1,0:T(8,128)(2,1)S(1)}, bf16[2048,512]{1,0:T(8,128)(2,1)}, u32[]{:S(2)}) copy-start(bf16[2048,512]{1,0:T(8,128)(2,1)} %w_ref.9) | copy-start | bytes 6291460
  51.1 10.5 %collective-permute-start.14 = (bf16[256,512]{1,0:T(8,128)(2,1)S(1)}, bf16[256,512]{1,0:T(8,128)(2,1)S(1)}, u32[]{:S(2)}, u32[]{:S(2)}) collective-permute-start(bf16[256,512]{1,0:T(8,128)(2,1)S(1)} %get-tuple-element.81.refs_0_), channel_id=1, source_target_pairs={{0,3},{1,2},{2,1},{3,0},{4,7},{5,6},{6,5},{7,4},{8,11},{9,10},{10,... | collective-permute-start | bytes 786440 | tf_op jit(solution)/shard_map/ppermute | solution.py:34
  52.6 9.2 %collective-permute-start.16 = (bf16[256,512]{1,0:T(8,128)(2,1)S(1)}, bf16[256,512]{1,0:T(8,128)(2,1)S(1)}, u32[]{:S(2)}, u32[]{:S(2)}) collective-permute-start(bf16[256,512]{1,0:T(8,128)(2,1)S(1)} %get-tuple-element.83.refs_0_), channel_id=1, source_target_pairs={{0,1},{1,0},{2,3},{3,2},{4,5},{5,4},{6,7},{7,6},{8,9},{9,8},{10,11... | collective-permute-start | bytes 786440 | tf_op jit(solution)/shard_map/ppermute | solution.py:34
  53.3 12.8 %collective-permute-start.19 = (bf16[256,512]{1,0:T(8,128)(2,1)S(1)}, bf16[256,512]{1,0:T(8,128)(2,1)S(1)}, u32[]{:S(2)}, u32[]{:S(2)}) collective-permute-start(bf16[256,512]{1,0:T(8,128)(2,1)S(1)} %get-tuple-element.83.refs_0_), channel_id=1, source_target_pairs={{0,3},{1,2},{2,1},{3,0},{4,7},{5,6},{6,5},{7,4},{8,11},{9,10},{10,... | collective-permute-start | bytes 786440 | tf_op jit(solution)/shard_map/ppermute | solution.py:34
  55.1 11.4 %collective-permute-start.18 = (bf16[256,512]{1,0:T(8,128)(2,1)S(1)}, bf16[256,512]{1,0:T(8,128)(2,1)S(1)}, u32[]{:S(2)}, u32[]{:S(2)}) collective-permute-start(bf16[256,512]{1,0:T(8,128)(2,1)S(1)} %get-tuple-element.81.refs_0_), channel_id=1, source_target_pairs={{0,1},{1,0},{2,3},{3,2},{4,5},{5,4},{6,7},{7,6},{8,9},{9,8},{10,11... | collective-permute-start | bytes 786440 | tf_op jit(solution)/shard_map/ppermute | solution.py:34
  61.6 7.2 %collective-permute-start.15 = (bf16[256,512]{1,0:T(8,128)(2,1)S(1)}, bf16[256,512]{1,0:T(8,128)(2,1)S(1)}, u32[]{:S(2)}, u32[]{:S(2)}) collective-permute-start(bf16[256,512]{1,0:T(8,128)(2,1)S(1)} %collective-permute-done.14.refs_0_), channel_id=1, source_target_pairs={{0,1},{1,0},{2,3},{3,2},{4,5},{5,4},{6,7},{7,6},{8,9},{9,8},{10,11... | collective-permute-start | bytes 786440 | tf_op jit(solution)/shard_map/ppermute | solution.py:34
  61.9 7.6 %collective-permute-start.17 = (bf16[256,512]{1,0:T(8,128)(2,1)S(1)}, bf16[256,512]{1,0:T(8,128)(2,1)S(1)}, u32[]{:S(2)}, u32[]{:S(2)}) collective-permute-start(bf16[256,512]{1,0:T(8,128)(2,1)S(1)} %collective-permute-done.16.refs_1_), channel_id=1, source_target_pairs={{0,3},{1,2},{2,1},{3,0},{4,7},{5,6},{6,5},{7,4},{8,11},{9,10},{10,... | collective-permute-start | bytes 786440 | tf_op jit(solution)/shard_map/ppermute | solution.py:34
